TPU v7x, 512 devices: a whole 4x8x8 slice. The times are simulated.
512 devices in a mesh: rep: 32 (over y, x_hi, core), shard: 16 (over z, x_lo).
Axes of the slice: x: 4 (x_hi: 2, x_lo: 2; x = x_hi * 2 + x_lo), y: 8, z: 8, core: 2. Of those that a mesh axis runs over, the one named last changes fastest.
Arguments:
- tokens: bfloat16 [65536, 8192], P(('rep', 'shard')), may hold values from -24 to 24
- key_grad: bfloat16 [65536, 512], P(('rep', 'shard')), may hold values from -150 to 150
- weight_codes: bfloat16 [8192, 512], P('shard'), may hold values from -0.0625 to 0.0625
- block_scales: float32 [64], P('shard'), may hold values from 0.5 to 2
Outputs:
- input_grad: bfloat16 [65536, 8192], P(('rep', 'shard'))
- weight_grad: float32 [8192, 512], P('shard')
- peak_values: float32 [2], replicated
All inputs are finite; a program needn't handle non-finite values.
Results may differ from a plain program's by a relative error of at most 0.008.
Values may be sent and summed in bfloat16 or wider, within the bound.
No kernel may reach another device: no remote copies, remote signals or barrier semaphores. Data moves between devices by JAX's collectives and lax.ppermute only.
A program may use at most 64 MiB of HBM per device.

v0:
```python
import math

import jax
import jax.numpy as jnp
from jax import lax
from jax.sharding import PartitionSpec as P

QBLOCK = 128


def local(tokens, key_grad, weight_codes, block_scales):
    scale_rows = jnp.repeat(block_scales, QBLOCK)
    weight = (weight_codes.astype(jnp.float32) * scale_rows[:, None]).astype(jnp.bfloat16)
    token_count = lax.axis_size("rep") * lax.axis_size("shard") * tokens.shape[0]
    factor = 1.0 / math.sqrt(token_count)
    group_grad = lax.all_gather(key_grad, "shard", axis=0, tiled=True)
    columns = lax.all_to_all(tokens, "shard", split_axis=1, concat_axis=0, tiled=True)
    grad_share = lax.dot_general(
        columns, group_grad, (((0,), (0,)), ((), ())), preferred_element_type=jnp.float32
    )
    input_full = lax.dot_general(
        key_grad,
        lax.all_gather(weight, "shard", axis=0, tiled=True),
        (((1,), (1,)), ((), ())),
        preferred_element_type=jnp.float32,
    )
    input_grad = input_full.astype(jnp.bfloat16)
    input_peak = jnp.max(jnp.abs(input_grad.astype(jnp.float32)))
    weight_grad = lax.psum(grad_share, "rep") * factor
    input_peak = lax.pmax(input_peak, ("rep", "shard"))
    weight_peak = lax.pmax(jnp.max(jnp.abs(weight_grad)), "shard")
    peak_values = jnp.stack([input_peak, weight_peak])
    return (input_grad, weight_grad, peak_values)


def solution(mesh):
    return jax.shard_map(
        local,
        mesh=mesh,
        in_specs=(
            P(("rep", "shard"), None),
            P(("rep", "shard"), None),
            P("shard", None),
            P("shard"),
        ),
        out_specs=(P(("rep", "shard"), None), P("shard", None), P()),
        check_vma=False,
    )
```

profile of v0, /device:TPU:1, one launch (start us, length us, event | category | flops | bytes accessed | tf_op | source)
XLA Modules:
  0.0 706.4 jit_solution(15907259450375785658)
XLA Ops:
  7.2 0.0 copy-start
  7.2 4.1 copy.9
  11.3 11.9 %all-to-all-start = ((bf16[128,16,512]{0,2,1:T(8,128)(2,1)}), bf16[128,16,512]{0,2,1:T(8,128)(2,1)S(1)}, u32[]{:S(2)}, u32[]{:S(2)}) async-start(bf16[128,16,512]{0,2,1:T(8,128)(2,1)} %bitcast.14), calls=%async_computation | async-start | bytes 4194304 | tf_op jit(solution)/shard_map/all_to_all | solution.py:17
  23.2 0.0 all-gather.5.cloned.1.call-start
  23.2 0.7 all-gather.5.cloned.1.call-update
  23.9 0.0 all-reduce.2.cloned.1.call-start
  23.9 50.0 %all-to-all-done = bf16[128,16,512]{0,2,1:T(8,128)(2,1)S(1)} async-done(((bf16[128,16,512]{0,2,1:T(8,128)(2,1)}), bf16[128,16,512]{0,2,1:T(8,128)(2,1)S(1)}, u32[]{:S(2)}, u32[]{:S(2)}) %all-to-all-start) | async-done | bytes 2097184 | tf_op jit(solution)/shard_map/all_to_all | solution.py:17
  74.0 2.6 copy.10
  76.6 38.8 %all-gather.5.cloned.1.call-done = bf16[2048,512]{1,0:T(8,128)(2,1)} async-done(((bf16[128,512]{1,0:T(8,128)(2,1)}), bf16[2048,512]{1,0:T(8,128)(2,1)}) %all-gather.5.cloned.1.call-update) | async-done | bytes 2097168 | tf_op jit(solution)/shard_map/all_gather | solution.py:16
  115.3 4.5 fusion.1
  119.9 0.0 all-reduce.2.cloned.1.call-update
  119.9 0.0 copy-start.2
  119.9 0.0 all-gather.3.cloned.1.call-start
  120.0 0.1 broadcast_bitcast_fusion
  120.0 1.0 multiply_convert_fusion
  121.0 0.0 all-gather.3.cloned.1.call-update
  121.0 281.1 %all-reduce.2.cloned.1.call-done = f32[512,512]{1,0:T(8,128)} async-done(((f32[512,512]{1,0:T(8,128)}), f32[512,512]{1,0:T(8,128)}) %all-reduce.2.cloned.1.call-update) | async-done | bytes 1048592 | tf_op jit(solution)/shard_map/psum | solution.py:29
  402.2 2.9 abs_reduce_fusion.1
  405.1 31.2 %pmax.15 = f32[1]{0:T(128)} all-reduce(f32[1]{0:T(128)} %bitcast.6), channel_id=1, replica_groups=mesh['rep'=32,'shard'=16] {'shard'}, use_global_device_ids=true, to_apply=%region_4.0 | all-reduce | flops 1 | bytes 8 | tf_op jit(solution)/shard_map/pmax | solution.py:31
  436.3 154.2 %all-gather.3.cloned.1.call-done = bf16[8192,512]{1,0:T(8,128)(2,1)} async-done(((bf16[512,512]{1,0:T(8,128)(2,1)}), bf16[8192,512]{1,0:T(8,128)(2,1)}) %all-gather.3.cloned.1.call-update) | async-done | bytes 8388624 | tf_op jit(solution)/shard_map/all_gather | solution.py:23
  590.5 6.3 abs_reduce_fusion
  596.9 2.9 copy.11
  599.7 98.3 %pmax.14 = f32[1]{0:T(128)} all-reduce(f32[1]{0:T(128)} %bitcast.5), channel_id=1, replica_groups=mesh['rep'=32,'shard'=16] {'rep','shard'}, use_global_device_ids=true, to_apply=%region_2.0 | all-reduce | flops 1 | bytes 8 | tf_op jit(solution)/shard_map/pmax | solution.py:30
  698.0 1.8 pad_maximum_fusion
  (4 shorter events, 0.0 us)
Async XLA Ops:
  7.2 112.8 %copy-start = (f32[4]{0:T(128)S(1)}, f32[4]{0:T(128)}, u32[]{:S(2)}) copy-start(f32[4]{0:T(128)} %param.7) | copy-start | bytes 52
  11.3 62.7 %all-to-all-start = ((bf16[128,16,512]{0,2,1:T(8,128)(2,1)}), bf16[128,16,512]{0,2,1:T(8,128)(2,1)S(1)}, u32[]{:S(2)}, u32[]{:S(2)}) async-start(bf16[128,16,512]{0,2,1:T(8,128)(2,1)} %bitcast.14), calls=%async_computation | async-start | bytes 4194304 | tf_op jit(solution)/shard_map/all_to_all | solution.py:17
  23.2 92.2 %all-gather.5.cloned.1.call-start = ((), (), s32[]{:S(2)}) async-start(), calls=%async_computation.2 | async-start | bytes 2228224 | tf_op jit(solution)/shard_map/all_gather | solution.py:16
  23.9 378.3 %all-reduce.2.cloned.1.call-start = ((), (), s32[]{:S(2)}) async-start(), calls=%async_computation.3 | async-start | bytes 2097152 | tf_op jit(solution)/shard_map/psum | solution.py:29
  115.3 4.7 copy-start.1
  119.9 470.6 %copy-start.2 = (bf16[128,512]{1,0:T(8,128)(2,1)S(1)}, bf16[128,512]{1,0:T(8,128)(2,1)}, u32[]{:S(2)}) copy-start(bf16[128,512]{1,0:T(8,128)(2,1)} %param.5) | copy-start | bytes 393220
  119.9 470.6 %all-gather.3.cloned.1.call-start = ((), (), s32[]{:S(2)}) async-start(), calls=%async_computation.1 | async-start | bytes 8912896 | tf_op jit(solution)/shard_map/all_gather | solution.py:23
Sparse Core Ops, SparseCore 0:
  26.1 89.2 all-gather.4
  120.0 282.1 all-reduce.1
  405.0 185.4 all-gather.2
where the time goes:
time: 707 us; the launch traced here: 706 us
  waiting for transfers between devices  525 us (74%)
  blocking collectives  130 us (18%)
  between operations  13.8 us (2%)
  starting transfers between devices  12 us (2%)
  matrix products  10.8 us (2%)
  local copies, waits for them, and re-layouts  9.62 us (1%)
    psum x1, waiting for transfers between devices, local(): weight_grad = lax.psum(grad_share, 'rep') * factor  281 us
    all_gather x1, waiting for transfers between devices, local(): lax.all_gather(weight, 'shard', axis=0, tiled=True)  154 us
    pmax x1, blocking collectives, local(): input_peak = lax.pmax(input_peak, ('rep', 'shard'))  98.3 us
    all_to_all x1, waiting for transfers between devices, local(): lax.all_to_all(tokens, 'shard', split_axis=1, concat_axis=0, tiled=True)  50 us
    all_gather x1, waiting for transfers between devices, local(): group_grad = lax.all_gather(key_grad, 'shard', axis=0, tiled=True)  38.8 us
    pmax x1, blocking collectives, local(): weight_peak = lax.pmax(jnp.max(jnp.abs(weight_grad)), 'shard')  31.2 us
  transfers between devices with their start and end apart: 4, of which 4 were waited for; matrix products, arithmetic and copies ran while one was open for 1% of the time, Pallas kernels for 0%

commit v1 on v0

v1 whole, which is shorter than its diff:
```python
import math

import jax
import jax.numpy as jnp
from jax import lax
from jax.sharding import Mesh
from jax.sharding import PartitionSpec as P

QBLOCK = 128
AXES = ("yh", "yl", "xh", "core", "zh", "zl", "xl")
SIZES = (4, 2, 2, 2, 4, 2, 2)
CUBE = ("yl", "core", "zl", "xl")
SPREAD = ("yh", "xh", "zh")
PLANE = ("yh", "yl", "xh")
BF16 = jnp.bfloat16
F32 = jnp.float32


def shard_swap():
    pairs = []
    for yl in range(2):
        for core in range(2):
            for zh in range(4):
                source = (yl * 2 + core) * 4 + zh
                target = zh * 4 + (yl * 2 + core)
                pairs.append((source, target))
    return pairs


def peak_rows(first, second):
    row = jnp.concatenate([jnp.full((256,), first, BF16), jnp.full((256,), second, BF16)])
    return jnp.broadcast_to(row[None], (16, 512))


def local(tokens, key_grad, weight_codes, block_scales):
    count, width = tokens.shape
    kw = key_grad.shape[1]
    factor = 1.0 / math.sqrt(512 * count)
    scale_rows = jnp.repeat(block_scales, QBLOCK)
    weight = (weight_codes.astype(F32) * scale_rows[:, None]).astype(BF16)
    weight = lax.ppermute(weight, ("yl", "core", "zh"), shard_swap())

    parts = tokens.reshape(count, 4, 4, 4, 128).transpose(3, 2, 0, 1, 4).reshape(16, count, 512)
    keys = jnp.broadcast_to(key_grad.reshape(1, 2, 1, count // 2, kw), (2, 2, 4, count // 2, kw))
    packed = jnp.concatenate([parts, keys.reshape(16, count // 2, kw)], axis=1)
    got = lax.all_to_all(packed, CUBE, 0, 0, tiled=True)
    cols = got[:, :count]
    halves = lax.all_gather(got[:, count:], "core", axis=1, tiled=True)

    share = lax.dot_general(cols, halves, (((0, 1), (0, 1)), ((), ())), preferred_element_type=F32)
    share = share.astype(BF16).reshape(4, 8, 16, kw).transpose(1, 0, 2, 3).reshape(32, 16, kw)
    terms = lax.all_to_all(share, SPREAD, 0, 0, tiled=True)
    piece = (jnp.sum(terms.astype(F32), axis=0) * factor).astype(BF16)
    weight_peak = jnp.max(jnp.abs(piece))

    back = lax.dot_general(halves, weight, (((2,), (1,)), ((), ())), preferred_element_type=F32)
    back = back.astype(BF16)
    input_peak = jnp.max(jnp.abs(back))
    rows = jnp.broadcast_to(peak_rows(input_peak, weight_peak)[None], (16, 16, 512))
    back = lax.all_to_all(jnp.concatenate([back, rows], axis=1), CUBE, 0, 0, tiled=True)
    input_grad = back[:, :count].transpose(1, 0, 2).reshape(count, width)
    peaks = jnp.max(back[:, count:].reshape(16, 16, 2, 256), axis=(0, 1, 3))

    sent = jnp.concatenate([piece, peak_rows(peaks[0], peaks[1])], axis=0)
    sent = jnp.broadcast_to(sent[None], (16,) + sent.shape)
    plane = lax.all_to_all(sent, PLANE, 0, 0, tiled=True)
    peaks = jnp.max(plane[:, 16:].reshape(16, 16, 2, 256), axis=(0, 1, 3)).astype(F32)
    both = lax.all_gather(plane[:, :16], "core", axis=0, tiled=False)
    both = both.reshape(2, 4, 2, 2, 16, kw).transpose(2, 0, 1, 3, 4, 5)
    weight_grad = both.reshape(512, kw).astype(F32)
    tile = jnp.broadcast_to(peaks[None, :, None], (4, 2, 128))
    peaks = jnp.max(lax.all_to_all(tile, "zh", 0, 0, tiled=True), axis=(0, 2))
    return (input_grad, weight_grad, peaks)


def solution(mesh):
    fine = Mesh(mesh.devices.reshape(SIZES), AXES)
    shard = ("zh", "zl", "xl")
    return jax.shard_map(
        local,
        mesh=fine,
        in_specs=(P(AXES, None), P(AXES, None), P(shard, None), P(shard)),
        out_specs=(P(AXES, None), P(shard, None), P()),
        check_vma=False,
    )
```

time: 707 us -> 235 us (0.33)
  waiting for transfers between devices: 525 us -> 72.8 us
  blocking collectives: 130 us -> 84.1 us
  starting transfers between devices: 12 us -> 31.1 us
  local copies, waits for them, and re-layouts: 9.62 us -> 23.6 us
    psum x1 -> x0, waiting for transfers between devices: 281 us -> none  [local(): weight_grad = lax.psum(grad_share, 'rep') * factor]
    all_gather x2 -> x1, waiting for transfers between devices: 193 us -> 20.3 us  [local(): halves = lax.all_gather(got[:, count:], 'core', axis=1, tiled=True)]
    pmax x2 -> x0, blocking collectives: 130 us -> none  [the longest x1 98.3 us: local(): input_peak = lax.pmax(input_peak, ('rep', 'shard'))]
    all_to_all x0 -> x2, blocking collectives: none -> 79.7 us  [the longest x1 47.1 us: local(): got = lax.all_to_all(packed, CUBE, 0, 0, tiled=True)]
    ppermute x0 -> x1, waiting for transfers between devices: none -> 37.4 us  [local(): weight = lax.ppermute(weight, ('yl', 'core', 'zh'), shard_swap())]
    all_to_all x1 -> x3, waiting for transfers between devices: 50 us -> 15.1 us  [the longest x1 9.75 us: local(): plane = lax.all_to_all(sent, PLANE, 0, 0, tiled=True)]
    all_to_all x1 -> x3, starting transfers between devices: 11.9 us -> 26.4 us  [the longest x1 13.8 us: local(): terms = lax.all_to_all(share, SPREAD, 0, 0, tiled=True)]
    reshape x0 -> x4, local copies, waits for them, and re-layouts: none -> 9.12 us  [the longest x3 8.29 us: local(): tokens.reshape(count, 4, 4, 4, 128).transpose(3, 2, 0, 1, 4)]
  transfers between devices with their start and end apart: 4 -> 5, of which waited for: 4 -> 4; matrix products, arithmetic and copies ran while one was open for 1% -> 5% of each run, Pallas kernels for 0% -> 0%
where the time goes in v1:
time: 235 us
  blocking collectives  84.1 us (36%)
  waiting for transfers between devices  72.8 us (31%)
  starting transfers between devices  31.1 us (13%)
  local copies, waits for them, and re-layouts  23.6 us (10%)
  between operations  14.2 us (6%)
  matrix products  6.49 us (3%)
  other arithmetic  2.49 us (1%)
    all_to_all x1, blocking collectives, local(): got = lax.all_to_all(packed, CUBE, 0, 0, tiled=True)  47.1 us
    ppermute x1, waiting for transfers between devices, local(): weight = lax.ppermute(weight, ('yl', 'core', 'zh'), shard_swap())  37.4 us
    all_to_all x1, blocking collectives, local(): lax.all_to_all(jnp.concatenate([back, rows], axis=1), CUBE, 0, 0, tiled=T...  32.6 us
    all_gather x1, waiting for transfers between devices, local(): halves = lax.all_gather(got[:, count:], 'core', axis=1, tiled=True)  20.3 us
    all_to_all x1, starting transfers between devices, local(): terms = lax.all_to_all(share, SPREAD, 0, 0, tiled=True)  13.8 us
    all_to_all x1, waiting for transfers between devices, local(): plane = lax.all_to_all(sent, PLANE, 0, 0, tiled=True)  9.75 us
    all_to_all x1, starting transfers between devices, local(): plane = lax.all_to_all(sent, PLANE, 0, 0, tiled=True)  9.11 us
    reshape x3, local copies, waits for them, and re-layouts, local(): tokens.reshape(count, 4, 4, 4, 128).transpose(3, 2, 0, 1, 4)  8.29 us
  transfers between devices with their start and end apart: 5, of which 4 were waited for; matrix products, arithmetic and copies ran while one was open for 5% of the time, Pallas kernels for 0%

profile of v1, /device:TPU:1, one launch (start us, length us, event | category | flops | bytes accessed | tf_op | source)
XLA Modules:
  0.0 234.8 jit_solution(13269411856776771826)
XLA Ops:
  7.2 3.2 %reshape.42 = bf16[128,4,4,4,128]{4,3,2,1,0:T(4,128)(2,1)S(1)} reshape(bf16[128,8192]{1,0:T(8,128)(2,1)} %param.4) | data formatting | bytes 4194304 | tf_op jit(solution)/shard_map/reshape | solution.py:43
  10.5 2.3 copy.42
  12.7 2.8 %reshape.43 = bf16[16,128,512]{2,1,0:T(8,128)(2,1)S(1)} reshape(bf16[4,4,128,4,128]{4,3,2,1,0:T(4,128)(2,1)} %bitcast.32) | data formatting | bytes 4194304 | tf_op jit(solution)/shard_map/reshape | solution.py:43
  16.0 47.1 %all_to_all.25 = bf16[16,192,512]{2,1,0:T(8,128)(2,1)S(1)} all-to-all(bf16[16,192,512]{2,1,0:T(8,128)(2,1)S(1)} %pad_maximum_fusion), channel_id=1, replica_groups=mesh['yh'=4,'yl'=2,'xh'=2,'core'=2,'zh'=4,'zl'=2,'xl'=2] {'yl','core','z..., dimensions={0} | all-to-all | bytes 6291456 | tf_op jit(solution)/shard_map/all_to_all | solution.py:46
  63.1 1.1 slice.32
  64.2 20.3 %all-gather.3.cloned.1.call-done = bf16[16,128,512]{2,1,0:T(8,128)(2,1)} async-done(((bf16[16,64,512]{2,1,0:T(8,128)(2,1)}), bf16[16,128,512]{2,1,0:T(8,128)(2,1)}) %all-gather.3.cloned.1.call-update) | async-done | bytes 2097168 | tf_op jit(solution)/shard_map/all_gather | solution.py:48
  84.5 2.9 %fusion.5 = bf16[512,512]{1,0:T(8,128)(2,1)S(1)} fusion(bf16[16,128,512]{2,1,0:T(8,128)(2,1)} %all-gather.3.cloned.1.call-done, bf16[16,192,512]{2,1,0:T(8,128)(2,1)S(1)} %all_to_all.25), kind=kOutput, calls=%fused_computation.9 | convolution fusion | flops 1074003968 | bytes 4718592 | tf_op jit(solution)/shard_map/dot_general | solution.py:50
  87.4 0.8 copy.34
  88.2 13.8 %all-to-all-start.1 = ((bf16[32,16,512]{2,1,0:T(8,128)(2,1)}), bf16[32,16,512]{2,1,0:T(8,128)(2,1)S(1)}, u32[]{:S(2)}, u32[]{:S(2)}) async-start(bf16[32,16,512]{2,1,0:T(8,128)(2,1)} %bitcast.8), calls=%async_computation.1 | async-start | bytes 1048576 | tf_op jit(solution)/shard_map/all_to_all | solution.py:52
  102.2 4.7 %collective-permute-start = (bf16[512,512]{1,0:T(8,128)(2,1)S(1)}, bf16[512,512]{1,0:T(8,128)(2,1)S(1)}, u32[]{:S(2)}, u32[]{:S(2)}) collective-permute-start(bf16[512,512]{1,0:T(8,128)(2,1)S(1)} %multiply_convert_fusion), channel_id=1, source_target_pairs={{0,0},{4,16},{8,64},{12,80},{16,4},{20,20},{24,68},{28,84},{64,8},... | collective-permute-start | bytes 1572872 | tf_op jit(solution)/shard_map/ppermute | solution.py:41
  106.9 37.4 %collective-permute-done = bf16[512,512]{1,0:T(8,128)(2,1)S(1)} collective-permute-done((bf16[512,512]{1,0:T(8,128)(2,1)S(1)}, bf16[512,512]{1,0:T(8,128)(2,1)S(1)}, u32[]{:S(2)}, u32[]{:S(2)}) %collective-permute-start) | collective-permute-done | bytes 524320 | tf_op jit(solution)/shard_map/ppermute | solution.py:41
  144.3 3.6 %abs_reduce_fusion = (bf16[]{:T(256)}, bf16[16,128,512]{2,1,0:T(8,128)(2,1)S(1)}) fusion(bf16[16,128,512]{2,1,0:T(8,128)(2,1)} %all-gather.3.cloned.1.call-done, bf16[512,512]{1,0:T(8,128)(2,1)S(1)} %collective-permute-done), kind=kOutput, calls=%fused_computation.6 | convolution fusion | flops 1076887552 | bytes 4718594 | tf_op jit(solution)/shard_map/dot_general | solution.py:56
  150.2 32.6 %all_to_all.26 = bf16[16,144,512]{2,1,0:T(8,128)(2,1)S(1)} all-to-all(bf16[16,144,512]{2,1,0:T(8,128)(2,1)S(1)} %pad_maximum_fusion.1), channel_id=1, replica_groups=mesh['yh'=4,'yl'=2,'xh'=2,'core'=2,'zh'=4,'zl'=2,'xl'=2] {'yl','core','z..., dimensions={0} | all-to-all | bytes 4718592 | tf_op jit(solution)/shard_map/all_to_all | solution.py:60
  184.9 0.8 broadcast_in_dim.43
  185.8 9.1 %all-to-all-start.3 = ((bf16[16,32,512]{2,1,0:T(8,128)(2,1)}), bf16[16,32,512]{2,1,0:T(8,128)(2,1)S(1)}, u32[]{:S(2)}, u32[]{:S(2)}) async-start(bf16[16,32,512]{2,1,0:T(8,128)(2,1)} %broadcast_in_dim.43), calls=%async_computation.3 | async-start | bytes 1048576 | tf_op jit(solution)/shard_map/all_to_all | solution.py:66
  194.9 1.5 slice_bitcast_fusion
  196.4 3.0 %copy.35 = bf16[128,16,512]{0,2,1:T(8,128)(2,1)S(1)} copy(bf16[128,16,512]{2,0,1:T(8,128)(2,1)} %slice_bitcast_fusion) | data formatting | bytes 4194304 | tf_op jit(solution)/shard_map/transpose | solution.py:61
  199.4 2.9 %copy.38 = bf16[128,8192]{1,0:T(8,128)(2,1)} copy(bf16[128,8192]{0,1:T(8,128)(2,1)S(1)} %bitcast.33) | data formatting | bytes 4194304
  202.3 9.7 %all-to-all-done.3 = bf16[16,32,512]{2,1,0:T(8,128)(2,1)S(1)} async-done(((bf16[16,32,512]{2,1,0:T(8,128)(2,1)}), bf16[16,32,512]{2,1,0:T(8,128)(2,1)S(1)}, u32[]{:S(2)}, u32[]{:S(2)}) %all-to-all-start.3) | async-done | bytes 524320 | tf_op jit(solution)/shard_map/all_to_all | solution.py:66
  212.1 4.4 %all-gather = bf16[32,16,512]{2,1,0:T(8,128)(2,1)S(1)} all-gather(bf16[16,16,512]{2,1,0:T(8,128)(2,1)S(1)} %get-tuple-element.21), channel_id=2, replica_groups=mesh['yh'=4,'yl'=2,'xh'=2,'core'=2,'zh'=4,'zl'=2,'xl'=2] {'core'}, dimensions={0}, use_global_device_ids=true | all-gather | bytes 786432 | tf_op jit(solution)/shard_map/all_gather | solution.py:68
  216.6 0.7 broadcast_in_dim.44
  217.3 3.4 %all-to-all-start.4 = ((f32[4,2,128]{2,1,0:T(2,128)}), f32[4,2,128]{2,1,0:T(2,128)S(1)}, u32[]{:S(2)}, u32[]{:S(2)}) async-start(f32[4,2,128]{2,1,0:T(2,128)} %broadcast_in_dim.44), calls=%async_computation.4 | async-start | bytes 8192 | tf_op jit(solution)/shard_map/all_to_all | solution.py:72
  220.9 1.1 copy.36
  222.0 5.3 %all-to-all-done.4 = f32[4,2,128]{2,1,0:T(2,128)S(1)} async-done(((f32[4,2,128]{2,1,0:T(2,128)}), f32[4,2,128]{2,1,0:T(2,128)S(1)}, u32[]{:S(2)}, u32[]{:S(2)}) %all-to-all-start.4) | async-done | bytes 4128 | tf_op jit(solution)/shard_map/all_to_all | solution.py:72
  (32 shorter events, 6.0 us)
Async XLA Ops:
  7.2 57.0 %copy-start = (f32[4]{0:T(128)S(1)}, f32[4]{0:T(128)}, u32[]{:S(2)}) copy-start(f32[4]{0:T(128)} %param.7) | copy-start | bytes 52
  7.2 77.3 %all-gather.3.cloned.1.call-start = ((), (), s32[]{:S(2)}) async-start(), calls=%async_computation.5 | async-start | bytes 3145728 | tf_op jit(solution)/shard_map/all_gather | solution.py:48
  12.7 2.8 %copy-start.2 = (bf16[128,512]{1,0:T(8,128)(2,1)S(1)}, bf16[128,512]{1,0:T(8,128)(2,1)}, u32[]{:S(2)}) copy-start(bf16[128,512]{1,0:T(8,128)(2,1)} %param.5) | copy-start | bytes 393220
  87.4 14.7 %copy-start.1 = (bf16[512,512]{1,0:T(8,128)(2,1)S(1)}, bf16[512,512]{1,0:T(8,128)(2,1)}, u32[]{:S(2)}) copy-start(bf16[512,512]{1,0:T(8,128)(2,1)} %param.6) | copy-start | bytes 1572868
  88.2 59.7 %all-to-all-start.1 = ((bf16[32,16,512]{2,1,0:T(8,128)(2,1)}), bf16[32,16,512]{2,1,0:T(8,128)(2,1)S(1)}, u32[]{:S(2)}, u32[]{:S(2)}) async-start(bf16[32,16,512]{2,1,0:T(8,128)(2,1)} %bitcast.8), calls=%async_computation.1 | async-start | bytes 1048576 | tf_op jit(solution)/shard_map/all_to_all | solution.py:52
  102.2 42.1 %collective-permute-start = (bf16[512,512]{1,0:T(8,128)(2,1)S(1)}, bf16[512,512]{1,0:T(8,128)(2,1)S(1)}, u32[]{:S(2)}, u32[]{:S(2)}) collective-permute-start(bf16[512,512]{1,0:T(8,128)(2,1)S(1)} %multiply_convert_fusion), channel_id=1, source_target_pairs={{0,0},{4,16},{8,64},{12,80},{16,4},{20,20},{24,68},{28,84},{64,8},... | collective-permute-start | bytes 1572872 | tf_op jit(solution)/shard_map/ppermute | solution.py:41
  185.8 26.3 %all-to-all-start.3 = ((bf16[16,32,512]{2,1,0:T(8,128)(2,1)}), bf16[16,32,512]{2,1,0:T(8,128)(2,1)S(1)}, u32[]{:S(2)}, u32[]{:S(2)}) async-start(bf16[16,32,512]{2,1,0:T(8,128)(2,1)} %broadcast_in_dim.43), calls=%async_computation.3 | async-start | bytes 1048576 | tf_op jit(solution)/shard_map/all_to_all | solution.py:66
  217.3 10.0 %all-to-all-start.4 = ((f32[4,2,128]{2,1,0:T(2,128)}), f32[4,2,128]{2,1,0:T(2,128)S(1)}, u32[]{:S(2)}, u32[]{:S(2)}) async-start(f32[4,2,128]{2,1,0:T(2,128)} %broadcast_in_dim.44), calls=%async_computation.4 | async-start | bytes 8192 | tf_op jit(solution)/shard_map/all_to_all | solution.py:72
Sparse Core Ops, SparseCore 0:
  64.3 20.1 all-gather.2

commit v2 on v1

v2 whole, which is shorter than its diff:
```python
import math

import jax
import jax.numpy as jnp
from jax import lax
from jax.experimental import pallas as pl
from jax.experimental.pallas import tpu as pltpu
from jax.sharding import Mesh
from jax.sharding import PartitionSpec as P

QBLOCK = 128
AXES = ("yh", "yl", "xh", "core", "zh", "zl", "xl")
SIZES = (4, 2, 2, 2, 4, 2, 2)
CUBE = ("yl", "core", "zl", "xl")
SPREAD = ("yh", "xh", "zh")
PLANE = ("yh", "yl", "xh")
BF16 = jnp.bfloat16
F32 = jnp.float32
COUNT = 128
HALF = COUNT // 2
KW = 512
PACK = COUNT + HALF
RETURN = COUNT + 16
PARAMS = pltpu.CompilerParams(vmem_limit_bytes=24 * 2**20)


def cost(flops, moved):
    return pl.CostEstimate(flops=flops, bytes_accessed=moved, transcendentals=0)


def shard_swap():
    pairs = []
    for yl in range(2):
        for core in range(2):
            for zh in range(4):
                source = (yl * 2 + core) * 4 + zh
                target = zh * 4 + (yl * 2 + core)
                pairs.append((source, target))
    return pairs


def pack_kernel(tokens, keys, out):
    for part in range(16):
        q, e = part // 4, part % 4
        first = (q % 2) * HALF
        second = HALF - first
        lanes = pl.ds(e * 512 + q * 128, 128)
        out[part, 0:HALF, :] = tokens[first : first + HALF, lanes]
        out[part, HALF:COUNT, :] = tokens[second : second + HALF, lanes]
        out[part, COUNT:PACK, :] = keys[first : first + HALF, :]


def pack(tokens, key_grad):
    return pl.pallas_call(
        pack_kernel,
        grid=(4,),
        in_specs=[
            pl.BlockSpec((COUNT, 2048), lambda i: (0, i)),
            pl.BlockSpec((COUNT, 128), lambda i: (0, i)),
        ],
        out_specs=pl.BlockSpec((16, PACK, 128), lambda i: (0, 0, i)),
        out_shape=jax.ShapeDtypeStruct((16, PACK, KW), BF16),
        compiler_params=PARAMS,
        cost_estimate=cost(0, 5 * 2**20),
        name="pack",
    )(tokens, key_grad)


def share_kernel(got, other, out, acc):
    step = pl.program_id(0)

    @pl.when(step == 0)
    def _():
        acc[...] = jnp.zeros_like(acc)

    total = acc[...]
    for rows, keys in ((got[:, 0:HALF, :], got[:, COUNT:PACK, :]), (got[:, HALF:COUNT, :], other[...])):
        total += lax.dot_general(
            rows.reshape(-1, KW),
            keys.reshape(-1, KW),
            (((0,), (0,)), ((), ())),
            preferred_element_type=F32,
        )
    acc[...] = total

    @pl.when(step == pl.num_programs(0) - 1)
    def _():
        for zh in range(4):
            for w in range(8):
                row = (zh * 8 + w) * 16
                out[w * 4 + zh] = acc[row : row + 16, :].astype(BF16)


def share_of(got, other):
    return pl.pallas_call(
        share_kernel,
        grid=(4,),
        in_specs=[
            pl.BlockSpec((4, PACK, KW), lambda i: (i, 0, 0)),
            pl.BlockSpec((4, HALF, KW), lambda i: (i, 0, 0)),
        ],
        out_specs=pl.BlockSpec((32, 16, KW), lambda i: (0, 0, 0)),
        out_shape=jax.ShapeDtypeStruct((32, 16, KW), BF16),
        scratch_shapes=[pltpu.VMEM((KW, KW), F32)],
        compiler_params=PARAMS,
        cost_estimate=cost(2**30, 5 * 2**20),
        name="share",
    )(got, other)


def product_kernel(mine, other, weight, out, peak):
    step = pl.program_id(0)

    @pl.when(step == 0)
    def _():
        peak[...] = jnp.zeros_like(peak)

    high = peak[...]
    for half, keys in enumerate((mine, other)):
        product = lax.dot_general(
            keys[...].reshape(-1, KW), weight[...], (((1,), (1,)), ((), ())), preferred_element_type=F32
        )
        rounded = product.astype(BF16)
        out[:, half * HALF : (half + 1) * HALF, :] = rounded.reshape(4, HALF, KW)
        size = jnp.abs(rounded.astype(F32)).reshape(-1, 8, KW)
        high = jnp.maximum(high, jnp.max(size, axis=0))
    peak[...] = high
    out[:, COUNT:RETURN, :] = jnp.zeros((4, RETURN - COUNT, KW), BF16)


def product_of(got, other, weight):
    return pl.pallas_call(
        product_kernel,
        grid=(4,),
        in_specs=[
            pl.BlockSpec((4, HALF, KW), lambda i: (i, 2, 0)),
            pl.BlockSpec((4, HALF, KW), lambda i: (i, 0, 0)),
            pl.BlockSpec((KW, KW), lambda i: (0, 0)),
        ],
        out_specs=[
            pl.BlockSpec((4, RETURN, KW), lambda i: (i, 0, 0)),
            pl.BlockSpec((8, KW), lambda i: (0, 0)),
        ],
        out_shape=[
            jax.ShapeDtypeStruct((16, RETURN, KW), BF16),
            jax.ShapeDtypeStruct((8, KW), F32),
        ],
        compiler_params=PARAMS,
        cost_estimate=cost(2**30, 5 * 2**20),
        name="product",
    )(got, other, weight)


def reduce_kernel(factor, terms, high, back_in, piece, back, rows, sem):
    total = terms[0].astype(F32)
    for k in range(1, 32):
        total += terms[k].astype(F32)
    rounded = (total * factor).astype(BF16)
    piece[...] = rounded
    first = jnp.max(high[...])
    second = jnp.max(jnp.abs(rounded.astype(F32)))
    lane = lax.broadcasted_iota(jnp.int32, (16, KW), 1)
    line = jnp.where(lane < 256, first, second).astype(BF16)
    for k in range(16):
        rows[k] = line
    copy = pltpu.make_async_copy(rows, back.at[:, COUNT:RETURN, :], sem)
    copy.start()
    copy.wait()


def reduce_terms(factor, terms, high, back):
    vmem = pl.BlockSpec(memory_space=pltpu.VMEM)
    return pl.pallas_call(
        lambda *refs: reduce_kernel(factor, *refs),
        in_specs=[vmem, vmem, pl.BlockSpec(memory_space=pl.ANY)],
        out_specs=[vmem, pl.BlockSpec(memory_space=pl.ANY)],
        out_shape=[
            jax.ShapeDtypeStruct((16, KW), BF16),
            jax.ShapeDtypeStruct(back.shape, BF16),
        ],
        input_output_aliases={2: 1},
        scratch_shapes=[pltpu.VMEM((16, 16, KW), BF16), pltpu.SemaphoreType.DMA],
        compiler_params=PARAMS,
        cost_estimate=cost(2**18, 2**20),
        name="reduce_terms",
    )(terms, high, back)


def spread_kernel(rows, piece, out):
    high = jnp.max(rows[...].astype(F32), axis=0)
    lane = lax.broadcasted_iota(jnp.int32, (16, KW), 1)
    first = jnp.max(jnp.where(lane < 256, high, 0.0))
    second = jnp.max(jnp.where(lane < 256, 0.0, high))
    line = jnp.where(lane < 256, first, second).astype(BF16)
    for k in range(16):
        out[k, 0:16, :] = piece[...]
        out[k, 16:32, :] = line


def spread(back, piece):
    return pl.pallas_call(
        spread_kernel,
        grid=(1,),
        in_specs=[
            pl.BlockSpec((16, 16, KW), lambda i: (0, COUNT // 16, 0)),
            pl.BlockSpec((16, KW), lambda i: (0, 0)),
        ],
        out_specs=pl.BlockSpec((16, 32, KW), lambda i: (0, 0, 0)),
        out_shape=jax.ShapeDtypeStruct((16, 32, KW), BF16),
        compiler_params=PARAMS,
        cost_estimate=cost(2**17, 2**20),
        name="spread",
    )(back, piece)


def unpack_kernel(back, out):
    second = pl.program_id(0) % 2

    def put(first):
        for e in range(4):
            lanes = pl.ds(e * 512, 512)
            out[first : first + HALF, lanes] = back[e, 0:HALF, :]
            out[HALF - first : COUNT - first, lanes] = back[e, HALF:COUNT, :]

    @pl.when(second == 0)
    def _():
        put(0)

    @pl.when(second == 1)
    def _():
        put(HALF)


def unpack(back):
    return pl.pallas_call(
        unpack_kernel,
        grid=(4,),
        in_specs=[pl.BlockSpec((4, RETURN, KW), lambda i: (i, 0, 0))],
        out_specs=pl.BlockSpec((COUNT, 2048), lambda i: (0, i)),
        out_shape=jax.ShapeDtypeStruct((COUNT, 8192), BF16),
        compiler_params=PARAMS,
        cost_estimate=cost(0, 5 * 2**20),
        name="unpack",
    )(back)


def merge_kernel(mine, other, out):
    core = lax.axis_index("core")
    for yl in range(2):
        for source, at in ((mine, core), (other, 1 - core)):
            for yh in range(4):
                for xh in range(2):
                    row = pl.multiple_of(yl * 256 + at * 128 + (yh * 2 + xh) * 16, 16)
                    out[pl.ds(row, 16), :] = source[(yh * 2 + yl) * 2 + xh, 0:16, :].astype(F32)


def merge(plane, other):
    vmem = pl.BlockSpec(memory_space=pltpu.VMEM)
    return pl.pallas_call(
        merge_kernel,
        in_specs=[vmem, vmem],
        out_specs=vmem,
        out_shape=jax.ShapeDtypeStruct((512, KW), F32),
        compiler_params=PARAMS,
        cost_estimate=cost(0, 2 * 2**20),
        name="merge",
    )(plane, other)


def local(tokens, key_grad, weight_codes, block_scales):
    factor = 1.0 / math.sqrt(512 * COUNT)
    scale_rows = jnp.repeat(block_scales, QBLOCK)
    weight = (weight_codes.astype(F32) * scale_rows[:, None]).astype(BF16)
    weight = lax.ppermute(weight, ("yl", "core", "zh"), shard_swap())

    got = lax.all_to_all(pack(tokens, key_grad), CUBE, 0, 0, tiled=True)
    got, weight = lax.optimization_barrier((got, weight))
    other = lax.ppermute(got[:, COUNT:], "core", [(0, 1), (1, 0)])

    terms = lax.all_to_all(share_of(got, other), SPREAD, 0, 0, tiled=True)

    back, high = product_of(got, other, weight)
    piece, back = reduce_terms(factor, terms, high, back)
    back = lax.all_to_all(back, CUBE, 0, 0, tiled=True)
    input_grad = unpack(back)

    plane = lax.all_to_all(spread(back, piece), PLANE, 0, 0, tiled=True)
    peaks = jnp.max(plane[:, 16:].reshape(16, 16, 2, 256), axis=(0, 1, 3)).astype(F32)
    other = lax.ppermute(plane[:, :16], "core", [(0, 1), (1, 0)])
    weight_grad = merge(plane, other)
    tile = jnp.broadcast_to(peaks[None, :, None], (4, 2, 128))
    peaks = jnp.max(lax.all_to_all(tile, "zh", 0, 0, tiled=True), axis=(0, 2))
    return (input_grad, weight_grad, peaks)


def solution(mesh):
    fine = Mesh(mesh.devices.reshape(SIZES), AXES)
    shard = ("zh", "zl", "xl")
    return jax.shard_map(
        local,
        mesh=fine,
        in_specs=(P(AXES, None), P(AXES, None), P(shard, None), P(shard)),
        out_specs=(P(AXES, None), P(shard, None), P()),
        check_vma=False,
    )
```

time: 235 us -> 200 us (0.85)
  blocking collectives: 84.1 us -> 61.8 us
  between operations: 14.2 us -> 0.79 us
  local copies, waits for them, and re-layouts: 23.6 us -> 12.9 us
  Pallas kernels: 0 us -> 9.68 us
  matrix products: 6.49 us -> 0 us
  waiting for transfers between devices: 72.8 us -> 77.4 us
  starting transfers between devices: 31.1 us -> 34.7 us
    all_to_all x2, waiting for transfers between devices: 9.75 us -> 34.5 us  [the longest x1 22.5 us: local(): got = lax.all_to_all(pack(tokens, key_grad), CUBE, 0, 0, tiled=True)]
    all_gather x1 -> x0, waiting for transfers between devices: 20.3 us -> none  [local(): halves = lax.all_gather(got[:, count:], 'core', axis=1, tiled=True)]
    all_to_all x2, blocking collectives: 79.7 us -> 61.8 us  [the longest x1 39.8 us: local(): back = lax.all_to_all(back, CUBE, 0, 0, tiled=True)]
    pallas_call x0 -> x7, Pallas kernels: none -> 9.68 us  [the longest x1 2.06 us: product_of(): pl.pallas_call(product_kernel, grid=(4,), in_specs=[pl.BlockSpec((4, HALF...]
    unnamed x7 -> x22, local copies, waits for them, and re-layouts: 2.91 us -> 12 us
    reshape x4 -> x0, local copies, waits for them, and re-layouts: 9.12 us -> none  [the longest x3 8.29 us: local(): tokens.reshape(count, 4, 4, 4, 128).transpose(3, 2, 0, 1, 4)]
    dot_general x2 -> x0, matrix products: 6.49 us -> none  [the longest x1 3.62 us: local(): lax.dot_general(halves, weight, (((2,), (1,)), ((), ())), preferred_eleme...]
    ppermute x0 -> x2, starting transfers between devices: none -> 6.37 us  [the longest x1 4.45 us: local(): other = lax.ppermute(plane[:, :16], 'core', [(0, 1), (1, 0)])]
  transfers between devices with their start and end apart: 5 -> 6, of which waited for: 4 -> 5; matrix products, arithmetic and copies ran while one was open for 5% -> 1% of each run, Pallas kernels for 0% -> 2%
where the time goes in v2:
time: 200 us; the launch traced here: 199 us
  waiting for transfers between devices  77.4 us (39%)
  blocking collectives  61.8 us (31%)
  starting transfers between devices  34.7 us (17%)
  local copies, waits for them, and re-layouts  12.9 us (6%)
  Pallas kernels  9.68 us (5%)
  other arithmetic  2.02 us (1%)
    all_to_all x1, blocking collectives, local(): back = lax.all_to_all(back, CUBE, 0, 0, tiled=True)  39.8 us
    ppermute x1, waiting for transfers between devices, local(): weight = lax.ppermute(weight, ('yl', 'core', 'zh'), shard_swap())  35.6 us
    all_to_all x1, waiting for transfers between devices, local(): got = lax.all_to_all(pack(tokens, key_grad), CUBE, 0, 0, tiled=True)  22.5 us
    all_to_all x1, blocking collectives, local(): plane = lax.all_to_all(spread(back, piece), PLANE, 0, 0, tiled=True)  22 us
    all_to_all x1, starting transfers between devices, local(): terms = lax.all_to_all(share_of(got, other), SPREAD, 0, 0, tiled=True)  12.2 us
    unnamed x22, local copies, waits for them, and re-layouts  12 us
    all_to_all x1, waiting for transfers between devices, local(): terms = lax.all_to_all(share_of(got, other), SPREAD, 0, 0, tiled=True)  11.9 us
    all_to_all x1, starting transfers between devices, local(): got = lax.all_to_all(pack(tokens, key_grad), CUBE, 0, 0, tiled=True)  10.4 us
  transfers between devices with their start and end apart: 6, of which 5 were waited for; matrix products, arithmetic and copies ran while one was open for 1% of the time, Pallas kernels for 2%

profile of v2, /device:TPU:1, one launch (start us, length us, event | category | flops | bytes accessed | tf_op | source)
XLA Modules:
  0.0 199.2 jit_solution(16935813983521398721)
XLA Ops:
  0.7 1.6 copy-done.7
  3.1 1.3 pack.1
  4.4 1.6 copy-done.1
  6.0 10.4 %all-to-all-start = ((bf16[16,192,512]{2,1,0:T(8,128)(2,1)}), bf16[16,192,512]{2,1,0:T(8,128)(2,1)S(1)}, u32[]{:S(2)}, u32[]{:S(2)}) async-start(bf16[16,192,512]{2,1,0:T(8,128)(2,1)} %copy-done.1), calls=%async_computation | async-start | bytes 6291456 | tf_op jit(solution)/shard_map/all_to_all | solution.py:276
  16.5 1.2 multiply_convert_fusion
  17.8 2.5 %collective-permute-start = (bf16[512,512]{1,0:T(8,128)(2,1)S(1)}, bf16[512,512]{1,0:T(8,128)(2,1)S(1)}, u32[]{:S(2)}, u32[]{:S(2)}) collective-permute-start(bf16[512,512]{1,0:T(8,128)(2,1)S(1)} %multiply_convert_fusion), channel_id=1, source_target_pairs={{0,0},{4,16},{8,64},{12,80},{16,4},{20,20},{24,68},{28,84},{64,8},... | collective-permute-start | bytes 1572872 | tf_op jit(solution)/shard_map/ppermute | solution.py:274
  20.2 35.6 %collective-permute-done.weight = bf16[512,512]{1,0:T(8,128)(2,1)S(1)} collective-permute-done((bf16[512,512]{1,0:T(8,128)(2,1)S(1)}, bf16[512,512]{1,0:T(8,128)(2,1)S(1)}, u32[]{:S(2)}, u32[]{:S(2)}) %collective-permute-start) | collective-permute-done | bytes 524320 | tf_op jit(solution)/shard_map/ppermute | solution.py:274
  56.7 22.5 %all-to-all-done.got.mine = bf16[16,192,512]{2,1,0:T(8,128)(2,1)S(1)} async-done(((bf16[16,192,512]{2,1,0:T(8,128)(2,1)}), bf16[16,192,512]{2,1,0:T(8,128)(2,1)S(1)}, u32[]{:S(2)}, u32[]{:S(2)}) %all-to-all-start) | async-done | bytes 3145760 | tf_op jit(solution)/shard_map/all_to_all | solution.py:276
  79.3 1.9 collective-permute-start.1
  81.2 2.6 %collective-permute-done.1.other = bf16[16,64,512]{2,1,0:T(8,128)(2,1)S(1)} collective-permute-done((bf16[16,64,512]{2,1,0:T(8,128)(2,1)S(1)}, bf16[16,64,512]{2,1,0:T(8,128)(2,1)S(1)}, u32[]{:S(2)}, u32[]{:S(2)}) %collective-permute-start.1) | collective-permute-done | bytes 1048608 | tf_op jit(solution)/shard_map/ppermute | solution.py:278
  83.9 2.0 %share.1 = bf16[32,16,512]{2,1,0:T(8,128)(2,1)S(1)} custom-call(bf16[16,192,512]{2,1,0:T(8,128)(2,1)S(1)} %all-to-all-done.got.mine, bf16[16,64,512]{2,1,0:T(8,128)(2,1)S(1)} %collective-permute-done.1.other), custom_call_target="tpu_custom_call" | custom-call | flops 1073741824 | bytes 5242880 | tf_op jit(solution)/shard_map/share/pallas_call | solution.py:95
  87.6 12.2 %all-to-all-start.1 = ((bf16[32,16,512]{2,1,0:T(8,128)(2,1)}), bf16[32,16,512]{2,1,0:T(8,128)(2,1)}, u32[]{:S(2)}, u32[]{:S(2)}) async-start(bf16[32,16,512]{2,1,0:T(8,128)(2,1)} %copy-done.6), calls=%async_computation.1 | async-start | bytes 1048576 | tf_op jit(solution)/shard_map/all_to_all | solution.py:280
  99.8 1.2 copy-done.5
  102.1 2.1 %product.1 = (bf16[16,144,512]{2,1,0:T(8,128)(2,1)S(1)}, f32[8,512]{1,0:T(8,128)S(1)}) custom-call(bf16[16,192,512]{2,1,0:T(8,128)(2,1)S(1)} %all-to-all-done.got.mine, bf16[16,64,512]{2,1,0:T(8,128)(2,1)S(1)} %copy-done.5, bf16[512,512]{1,0:T(8,128)(2,1)S(1)} %copy-done.9), custom_call_target="tpu_custom_call" | custom-call | flops 1073741824 | bytes 5242880 | tf_op jit(solution)/shard_map/product/pallas_call | solution.py:132
  104.2 1.4 copy-done.2
  105.6 11.9 %all-to-all-done.1.refs_0_ = bf16[32,16,512]{2,1,0:T(8,128)(2,1)} async-done(((bf16[32,16,512]{2,1,0:T(8,128)(2,1)}), bf16[32,16,512]{2,1,0:T(8,128)(2,1)}, u32[]{:S(2)}, u32[]{:S(2)}) %all-to-all-start.1) | async-done | bytes 524320 | tf_op jit(solution)/shard_map/all_to_all | solution.py:280
  117.5 1.7 copy-done.3
  119.2 1.3 reduce_terms.1
  120.5 39.8 %all_to_all.25.back.rows = bf16[16,144,512]{2,1,0:T(8,128)(2,1)S(1)} all-to-all(bf16[16,144,512]{2,1,0:T(8,128)(2,1)S(1)} %get-tuple-element.13), channel_id=1, replica_groups=mesh['yh'=4,'yl'=2,'xh'=2,'core'=2,'zh'=4,'zl'=2,'xl'=2] {'yl','core','z..., dimensions={0} | all-to-all | bytes 4718592 | tf_op jit(solution)/shard_map/all_to_all | solution.py:284
  160.5 22.0 %all_to_all.26.mine = bf16[16,32,512]{2,1,0:T(8,128)(2,1)S(1)} all-to-all(bf16[16,32,512]{2,1,0:T(8,128)(2,1)S(1)} %spread.1), channel_id=1, replica_groups=mesh['yh'=4,'yl'=2,'xh'=2,'core'=2,'zh'=4,'zl'=2,'xl'=2] {'yh','yl','xh'}, dimensions={0} | all-to-all | bytes 1048576 | tf_op jit(solution)/shard_map/all_to_all | solution.py:287
  182.5 4.5 %collective-permute-start.2 = (bf16[16,16,512]{2,1,0:T(8,128)(2,1)S(1)}, bf16[16,16,512]{2,1,0:T(8,128)(2,1)S(1)}, u32[]{:S(2)}, u32[]{:S(2)}) collective-permute-start(bf16[16,16,512]{2,1,0:T(8,128)(2,1)S(1)} %get-tuple-element.16), channel_id=1, source_target_pairs={{0,16},{16,0},{1,17},{17,1},{2,18},{18,2},{3,19},{19,3},{4,20},{20... | collective-permute-start | bytes 786440 | tf_op jit(solution)/shard_map/ppermute | solution.py:289
  187.8 3.2 %all-to-all-start.4 = ((f32[4,2,128]{2,1,0:T(2,128)}), f32[4,2,128]{2,1,0:T(2,128)S(1)}, u32[]{:S(2)}, u32[]{:S(2)}) async-start(f32[4,2,128]{2,1,0:T(2,128)} %broadcast_in_dim.10), calls=%async_computation.4 | async-start | bytes 8192 | tf_op jit(solution)/shard_map/all_to_all | solution.py:292
  191.0 1.9 unpack.1
  192.9 4.7 %all-to-all-done.4 = f32[4,2,128]{2,1,0:T(2,128)S(1)} async-done(((f32[4,2,128]{2,1,0:T(2,128)}), f32[4,2,128]{2,1,0:T(2,128)S(1)}, u32[]{:S(2)}, u32[]{:S(2)}) %all-to-all-start.4) | async-done | bytes 4128 | tf_op jit(solution)/shard_map/all_to_all | solution.py:292
  (27 shorter events, 7.4 us)
Async XLA Ops:
  0.6 15.8 %copy-start = (f32[4]{0:T(128)S(1)}, f32[4]{0:T(128)}, u32[]{:S(2)}) copy-start(f32[4]{0:T(128)} %param.7) | copy-start | bytes 52
  0.6 1.6 copy-start.7
  2.2 0.9 copy-start.10
  4.4 1.6 copy-start.1
  6.0 73.2 %all-to-all-start = ((bf16[16,192,512]{2,1,0:T(8,128)(2,1)}), bf16[16,192,512]{2,1,0:T(8,128)(2,1)S(1)}, u32[]{:S(2)}, u32[]{:S(2)}) async-start(bf16[16,192,512]{2,1,0:T(8,128)(2,1)} %copy-done.1), calls=%async_computation | async-start | bytes 6291456 | tf_op jit(solution)/shard_map/all_to_all | solution.py:276
  17.8 38.1 %collective-permute-start = (bf16[512,512]{1,0:T(8,128)(2,1)S(1)}, bf16[512,512]{1,0:T(8,128)(2,1)S(1)}, u32[]{:S(2)}, u32[]{:S(2)}) collective-permute-start(bf16[512,512]{1,0:T(8,128)(2,1)S(1)} %multiply_convert_fusion), channel_id=1, source_target_pairs={{0,0},{4,16},{8,64},{12,80},{16,4},{20,20},{24,68},{28,84},{64,8},... | collective-permute-start | bytes 1572872 | tf_op jit(solution)/shard_map/ppermute | solution.py:274
  55.9 0.8 copy-start.8
  79.3 4.6 %collective-permute-start.1 = (bf16[16,64,512]{2,1,0:T(8,128)(2,1)S(1)}, bf16[16,64,512]{2,1,0:T(8,128)(2,1)S(1)}, u32[]{:S(2)}, u32[]{:S(2)}) collective-permute-start(bf16[16,64,512]{2,1,0:T(8,128)(2,1)S(1)} %slice.9), channel_id=1, source_target_pairs={{0,16},{16,0},{1,17},{17,1},{2,18},{18,2},{3,19},{19,3},{4,20},{20... | collective-permute-start | bytes 3145736 | tf_op jit(solution)/shard_map/ppermute | solution.py:278
  85.9 1.0 copy-start.4
  86.9 0.8 copy-start.6
  87.6 29.9 %all-to-all-start.1 = ((bf16[32,16,512]{2,1,0:T(8,128)(2,1)}), bf16[32,16,512]{2,1,0:T(8,128)(2,1)}, u32[]{:S(2)}, u32[]{:S(2)}) async-start(bf16[32,16,512]{2,1,0:T(8,128)(2,1)} %copy-done.6), calls=%async_computation.1 | async-start | bytes 1048576 | tf_op jit(solution)/shard_map/all_to_all | solution.py:280
  99.8 1.2 copy-start.5
  101.0 1.0 copy-start.9
  104.2 1.4 copy-start.2
  117.5 1.7 copy-start.3
  182.5 15.7 %collective-permute-start.2 = (bf16[16,16,512]{2,1,0:T(8,128)(2,1)S(1)}, bf16[16,16,512]{2,1,0:T(8,128)(2,1)S(1)}, u32[]{:S(2)}, u32[]{:S(2)}) collective-permute-start(bf16[16,16,512]{2,1,0:T(8,128)(2,1)S(1)} %get-tuple-element.16), channel_id=1, source_target_pairs={{0,16},{16,0},{1,17},{17,1},{2,18},{18,2},{3,19},{19,3},{4,20},{20... | collective-permute-start | bytes 786440 | tf_op jit(solution)/shard_map/ppermute | solution.py:289
  187.8 9.8 %all-to-all-start.4 = ((f32[4,2,128]{2,1,0:T(2,128)}), f32[4,2,128]{2,1,0:T(2,128)S(1)}, u32[]{:S(2)}, u32[]{:S(2)}) async-start(f32[4,2,128]{2,1,0:T(2,128)} %broadcast_in_dim.10), calls=%async_computation.4 | async-start | bytes 8192 | tf_op jit(solution)/shard_map/all_to_all | solution.py:292

commit v3 on v0

v3 whole, which is shorter than its diff:
```python
import math

import jax
import jax.numpy as jnp
from jax import lax
from jax.experimental import pallas as pl
from jax.experimental.pallas import tpu as pltpu
from jax.sharding import Mesh
from jax.sharding import PartitionSpec as P

QBLOCK = 128
AXES = ("yh", "yl", "xh", "core", "z", "xl")
SIZES = (4, 2, 2, 2, 8, 2)
GROUP = ("yl", "xh", "core", "xl")
SPREAD = ("yh", "z")
PLANE = ("yh", "yl", "xh")
SHIFT = (0, 4, 1, 7, 2, 6, 3, 5)
BF16 = jnp.bfloat16
F32 = jnp.float32
COUNT = 128
HALF = COUNT // 2
KW = 512
PACK = COUNT + HALF
RETURN = COUNT + 16
WIDE = KW + 128
PARAMS = pltpu.CompilerParams(vmem_limit_bytes=24 * 2**20)
VMEM = pl.BlockSpec(memory_space=pltpu.VMEM)
ANY = pl.BlockSpec(memory_space=pl.ANY)


def call(kernel, name, out_shape, in_specs, out_specs, flops, moved, **more):
    return pl.pallas_call(
        kernel,
        in_specs=in_specs,
        out_specs=out_specs,
        out_shape=out_shape,
        compiler_params=PARAMS,
        cost_estimate=pl.CostEstimate(flops=flops, bytes_accessed=moved, transcendentals=0),
        name=name,
        **more,
    )


def array(shape, dtype=BF16):
    return jax.ShapeDtypeStruct(shape, dtype)


def pack_kernel(tokens, keys, codes, scales, out, weight, columns, own, held, sems):
    loads = [
        pltpu.make_async_copy(tokens.at[:, pl.ds(m * 2048, 2048)], columns.at[m], sems.at[m]) for m in range(4)
    ]
    loads.append(pltpu.make_async_copy(keys, own, sems.at[4]))
    loads.append(pltpu.make_async_copy(codes, held, sems.at[5]))
    for load in loads:
        load.start()
    low = lax.broadcasted_iota(jnp.int32, (HALF, 128), 1) < 64
    for m in range(4):
        loads[m].wait()
        for t in range(4):
            for e in range(2):
                for half in range(2):
                    rows = pl.ds(half * HALF, HALF)
                    even = columns[m, rows, pl.ds(e * 512 + t * 128, 128)]
                    odd = columns[m, rows, pl.ds(1024 + e * 512 + t * 128, 128)]
                    for core in range(2):
                        first, second = (even, odd) if core == 0 else (odd, even)
                        at = HALF * (half ^ core)
                        out[t * 4 + core * 2 + e, at : at + HALF, m * 128 : (m + 1) * 128] = jnp.where(
                            low, first, second
                        )
    loads[4].wait()
    for part in range(16):
        core = part // 2 % 2
        out[part, COUNT:PACK, :] = own[core * HALF : (core + 1) * HALF, :]
    loads[5].wait()
    for block in range(4):
        rows = pl.ds(block * QBLOCK, QBLOCK)
        weight[rows, :] = (held[rows, :].astype(F32) * scales[block]).astype(BF16)


def pack(tokens, key_grad, codes, scales):
    return call(
        pack_kernel,
        "pack",
        [array((16, PACK, KW)), array((512, KW))],
        [ANY, ANY, ANY, pl.BlockSpec(memory_space=pltpu.SMEM)],
        [VMEM, VMEM],
        0,
        6 * 2**20,
        scratch_shapes=[
            pltpu.VMEM((4, COUNT, 2048), BF16),
            pltpu.VMEM((COUNT, KW), BF16),
            pltpu.VMEM((512, KW), BF16),
            pltpu.SemaphoreType.DMA((6,)),
        ],
    )(tokens, key_grad, codes, scales)


def gradients(rows, keys):
    return lax.dot_general(
        rows.reshape(-1, KW), keys.reshape(-1, KW), (((0,), (0,)), ((), ())), preferred_element_type=F32
    )


def products(keys, weight):
    out = lax.dot_general(
        keys.reshape(-1, KW), weight, (((1,), (1,)), ((), ())), preferred_element_type=F32
    ).astype(BF16)
    return out, jnp.max(jnp.abs(out.astype(F32)).reshape(-1, 8, KW), axis=0)


def own_kernel(got, weight, total, product, high):
    total[...] = gradients(got[:, 0:HALF, :], got[:, COUNT:PACK, :])
    out, size = products(got[:, COUNT:PACK, :], weight[...])
    product[...] = out.reshape(16, HALF, KW)
    high[...] = size


def own_half(got, weight):
    return call(
        own_kernel,
        "own_half",
        [array((KW, KW), F32), array((16, HALF, KW)), array((8, KW), F32)],
        [VMEM] * 2,
        [VMEM] * 3,
        2**30,
        5 * 2**20,
    )(got, weight)


def other_kernel(got, other, weight, total, product, high_in, share, back, high):
    core = lax.axis_index("core")
    out, size = products(other[...], weight[...])
    back[:, 0:HALF, :] = product[...]
    back[:, HALF:COUNT, :] = out.reshape(16, HALF, KW)
    back[:, COUNT:RETURN, :] = jnp.zeros((16, RETURN - COUNT, KW), BF16)
    high[...] = jnp.maximum(high_in[...], size)
    summed = (total[...] + gradients(got[:, HALF:COUNT, :], other[...])).astype(BF16)
    for m in range(4):
        for s in range(2):
            z = 2 * m + jnp.where(core == 0, s, 1 - s)
            for yh in range(4):
                row = m * 128 + s * 64 + yh * 16
                share[yh * 8 + z] = summed[row : row + 16, :]


def other_half(got, other, weight, total, product, high):
    return call(
        other_kernel,
        "other_half",
        [array((32, 16, KW)), array((16, RETURN, KW)), array((8, KW), F32)],
        [VMEM] * 6,
        [VMEM] * 3,
        2**30,
        7 * 2**20,
    )(got, other, weight, total, product, high)


def reduce_kernel(factor, terms, high, back_in, piece, back, rows, sem):
    total = terms[0].astype(F32)
    for k in range(1, 32):
        total += terms[k].astype(F32)
    rounded = (total * factor).astype(BF16)
    piece[...] = rounded
    first = jnp.max(high[...])
    second = jnp.max(jnp.abs(rounded.astype(F32)))
    lane = lax.broadcasted_iota(jnp.int32, (16, KW), 1)
    line = jnp.where(lane < 256, first, second).astype(BF16)
    for k in range(16):
        rows[k] = line
    copy = pltpu.make_async_copy(rows, back.at[:, COUNT:RETURN, :], sem)
    copy.start()
    copy.wait()


def reduce_terms(factor, terms, high, back):
    return call(
        lambda *refs: reduce_kernel(factor, *refs),
        "reduce_terms",
        [array((16, KW)), array(back.shape)],
        [VMEM, VMEM, ANY],
        [VMEM, ANY],
        2**18,
        2**20,
        input_output_aliases={2: 1},
        scratch_shapes=[pltpu.VMEM((16, 16, KW), BF16), pltpu.SemaphoreType.DMA],
    )(terms, high, back)


def spread_kernel(rows, piece, out):
    high = jnp.max(rows[...].astype(F32), axis=0)
    lane = lax.broadcasted_iota(jnp.int32, (16, KW), 1)
    first = jnp.max(jnp.where(lane < 256, high, 0.0))
    second = jnp.max(jnp.where(lane < 256, 0.0, high))
    lane = lax.broadcasted_iota(jnp.int32, (16, 128), 1)
    line = jnp.where(lane < 64, first, second).astype(BF16)
    for k in range(16):
        out[k, :, 0:KW] = piece[...]
        out[k, :, KW:WIDE] = line


def spread(back, piece):
    return call(
        spread_kernel,
        "spread",
        array((16, 16, WIDE)),
        [
            pl.BlockSpec((16, 16, KW), lambda i: (0, COUNT // 16, 0)),
            pl.BlockSpec((16, KW), lambda i: (0, 0)),
        ],
        pl.BlockSpec((16, 16, WIDE), lambda i: (0, 0, 0)),
        2**17,
        2**20,
        grid=(1,),
    )(back, piece)


def unpack_kernel(place, back, out):
    second = pl.program_id(0) % 2

    def put(first):
        for e in range(2):
            lanes = pl.ds(e * 512, 512)
            out[first : first + HALF, lanes] = back[e, 0:HALF, :]
            out[HALF - first : COUNT - first, lanes] = back[e, HALF:COUNT, :]

    @pl.when(second == 0)
    def _():
        put(0)

    @pl.when(second == 1)
    def _():
        put(HALF)


def unpack(place, back):
    return pl.pallas_call(
        unpack_kernel,
        grid_spec=pltpu.PrefetchScalarGridSpec(
            num_scalar_prefetch=1,
            grid=(8,),
            in_specs=[pl.BlockSpec((2, RETURN, KW), lambda i, place: (i, 0, 0))],
            out_specs=pl.BlockSpec((COUNT, 1024), lambda i, place: (0, place[i])),
        ),
        out_shape=array((COUNT, 8192)),
        compiler_params=PARAMS,
        cost_estimate=pl.CostEstimate(flops=0, bytes_accessed=5 * 2**20, transcendentals=0),
        name="unpack",
    )(place, back)


def tile_kernel(plane, out):
    high = jnp.max(plane[:, :, KW:WIDE].astype(F32), axis=0)
    high = jnp.max(high.reshape(2, 8, 128), axis=0)
    for k in range(8):
        out[k] = high


def tile_of(plane):
    return call(tile_kernel, "tile", array((8, 8, 128), F32), [VMEM], VMEM, 2**15, 2**17)(plane)


def merge_kernel(mine, other, out):
    turn = lax.rem(lax.axis_index("core") + lax.axis_index("z"), 2)
    for source, s in ((mine, turn), (other, 1 - turn)):
        for yh in range(4):
            for t in range(4):
                row = pl.multiple_of(t * 128 + s * 64 + yh * 16, 16)
                out[pl.ds(row, 16), :] = source[yh * 4 + t, :, 0:KW].astype(F32)


def merge(plane, other):
    return call(merge_kernel, "merge", array((512, KW), F32), [VMEM] * 2, VMEM, 0, 2 * 2**20)(plane, other)


def swap(x):
    return lax.ppermute(x, "core", [(0, 1), (1, 0)])


def shift_weight(weight):
    pairs = [(q * 8 + (z + SHIFT[q]) % 8, q * 8 + z) for q in range(8) for z in range(8)]
    return lax.ppermute(weight, ("yl", "xh", "core", "z"), pairs)


def local(tokens, key_grad, weight_codes, block_scales):
    factor = 1.0 / math.sqrt(512 * COUNT)
    place = lax.rem(jnp.array(SHIFT, jnp.int32) + lax.axis_index("z"), 8)

    packed, weight = pack(tokens, key_grad, weight_codes, block_scales)
    weight = shift_weight(weight)
    got = lax.all_to_all(packed, GROUP, 0, 0, tiled=True)
    other = swap(got[:, COUNT:])
    total, product, high = own_half(got, weight)
    share, back, high = other_half(got, other, weight, total, product, high)

    terms = lax.all_to_all(share, SPREAD, 0, 0, tiled=True)
    piece, back = reduce_terms(factor, terms, high, back)

    back = lax.all_to_all(back, GROUP, 0, 0, tiled=True)
    input_grad = unpack(place, back)

    plane = lax.all_to_all(spread(back, piece), PLANE, 0, 0, tiled=True)
    weight_grad = merge(plane, swap(plane))
    tile = lax.all_to_all(tile_of(plane), "z", 0, 0, tiled=True)
    tile, weight_grad, input_grad = lax.optimization_barrier((tile, weight_grad, input_grad))
    peaks = jnp.max(tile.reshape(64, 2, 64), axis=(0, 2))
    return (input_grad, weight_grad, peaks)


def solution(mesh):
    fine = Mesh(mesh.devices.reshape(SIZES), AXES)
    return jax.shard_map(
        local,
        mesh=fine,
        in_specs=(P(AXES, None), P(AXES, None), P(("z", "xl"), None), P(("z", "xl"))),
        out_specs=(P(AXES, None), P(("z", "xl"), None), P()),
        check_vma=False,
    )
```

time: 707 us -> 184 us (0.26)
  waiting for transfers between devices: 525 us -> 15.7 us
  between operations: 13.8 us -> 0.75 us
  matrix products: 10.8 us -> 0 us
  Pallas kernels: 0 us -> 9.78 us
    psum x1 -> x0, waiting for transfers between devices: 281 us -> none  [local(): weight_grad = lax.psum(grad_share, 'rep') * factor]
    all_gather x2 -> x0, waiting for transfers between devices: 193 us -> none  [the longest x1 154 us: local(): lax.all_gather(weight, 'shard', axis=0, tiled=True)]
    all_to_all x0 -> x4, blocking collectives: none -> 134 us  [the longest x1 47.1 us: local(): got = lax.all_to_all(packed, GROUP, 0, 0, tiled=True)]
    pmax x2 -> x0, blocking collectives: 130 us -> none  [the longest x1 98.3 us: local(): input_peak = lax.pmax(input_peak, ('rep', 'shard'))]
    all_to_all x1, waiting for transfers between devices: 50 us -> 2.15 us  [local(): tile = lax.all_to_all(tile_of(plane), 'z', 0, 0, tiled=True)]
    ppermute x0 -> x3, starting transfers between devices: none -> 15 us  [the longest x1 7.85 us: shift_weight(): return lax.ppermute(weight, ('yl', 'xh', 'core', 'z'), pairs)]
    ppermute x0 -> x3, waiting for transfers between devices: none -> 13.5 us  [the longest x1 13.5 us: shift_weight(): return lax.ppermute(weight, ('yl', 'xh', 'core', 'z'), pairs)]
    dot_general x2 -> x0, matrix products: 10.8 us -> none  [the longest x1 6.33 us: local(): lax.dot_general(key_grad, lax.all_gather(weight, 'shard', axis=0, tiled=T...]
  transfers between devices with their start and end apart: 4 -> 4, of which waited for: 4 -> 2; matrix products, arithmetic and copies ran while one was open for 1% -> 0% of each run, Pallas kernels for 0% -> 4%
where the time goes in v3:
time: 184 us; the launch traced here: 183 us
  blocking collectives  134 us (73%)
  starting transfers between devices  18.3 us (10%)
  waiting for transfers between devices  15.7 us (9%)
  Pallas kernels  9.78 us (5%)
  local copies, waits for them, and re-layouts  4.36 us (2%)
    all_to_all x1, blocking collectives, local(): got = lax.all_to_all(packed, GROUP, 0, 0, tiled=True)  47.1 us
    all_to_all x1, blocking collectives, local(): back = lax.all_to_all(back, GROUP, 0, 0, tiled=True)  37.4 us
    all_to_all x1, blocking collectives, local(): terms = lax.all_to_all(share, SPREAD, 0, 0, tiled=True)  29 us
    all_to_all x1, blocking collectives, local(): plane = lax.all_to_all(spread(back, piece), PLANE, 0, 0, tiled=True)  20.1 us
    ppermute x1, waiting for transfers between devices, shift_weight(): return lax.ppermute(weight, ('yl', 'xh', 'core', 'z'), pairs)  13.5 us
    ppermute x1, starting transfers between devices, shift_weight(): return lax.ppermute(weight, ('yl', 'xh', 'core', 'z'), pairs)  7.85 us
    ppermute x2, starting transfers between devices, swap(): return lax.ppermute(x, 'core', [(0, 1), (1, 0)])  7.11 us
    unnamed x10, local copies, waits for them, and re-layouts  4.19 us
  transfers between devices with their start and end apart: 4, of which 2 were waited for; matrix products, arithmetic and copies ran while one was open for 0% of the time, Pallas kernels for 4%

profile of v3, /device:TPU:1, one launch (start us, length us, event | category | flops | bytes accessed | tf_op | source)
XLA Modules:
  0.0 183.1 jit_solution(10864777984246777433)
XLA Ops:
  0.6 1.6 copy-done
  2.2 1.0 copy-done.1
  3.3 0.9 copy-done.2
  4.2 0.7 copy-done.3
  4.8 1.5 pack.1
  6.3 47.1 %all_to_all.25.got = bf16[16,192,512]{2,1,0:T(8,128)(2,1)S(1)} all-to-all(bf16[16,192,512]{2,1,0:T(8,128)(2,1)S(1)} %get-tuple-element.16), channel_id=1, replica_groups=mesh['yh'=4,'yl'=2,'xh'=2,'core'=2,'z'=8,'xl'=2] {'yl','xh','core','xl'}, dimensions={0} | all-to-all | bytes 6291456 | tf_op jit(solution)/shard_map/all_to_all | solution.py:291
  53.4 0.1 slice.4
  53.5 3.3 %collective-permute-start = (bf16[16,64,512]{2,1,0:T(8,128)(2,1)S(1)}, bf16[16,64,512]{2,1,0:T(8,128)(2,1)S(1)}, u32[]{:S(2)}, u32[]{:S(2)}) collective-permute-start(bf16[16,64,512]{2,1,0:T(8,128)(2,1)S(1)} %slice.4), channel_id=1, source_target_pairs={{0,16},{16,0},{1,17},{17,1},{2,18},{18,2},{3,19},{19,3},{4,20},{20... | collective-permute-start | bytes 3145736 | tf_op jit(solution)/shard_map/ppermute | solution.py:277
  56.8 7.8 %collective-permute-start.1 = (bf16[512,512]{1,0:T(8,128)(2,1)S(1)}, bf16[512,512]{1,0:T(8,128)(2,1)S(1)}, u32[]{:S(2)}, u32[]{:S(2)}) collective-permute-start(bf16[512,512]{1,0:T(8,128)(2,1)S(1)} %get-tuple-element.17), channel_id=1, source_target_pairs={{0,0},{2,2},{4,4},{6,6},{8,8},{10,10},{12,12},{14,14},{24,16},{26,... | collective-permute-start | bytes 1572872 | tf_op jit(solution)/shard_map/ppermute | solution.py:282
  64.7 13.5 %collective-permute-done.1.weight = bf16[512,512]{1,0:T(8,128)(2,1)S(1)} collective-permute-done((bf16[512,512]{1,0:T(8,128)(2,1)S(1)}, bf16[512,512]{1,0:T(8,128)(2,1)S(1)}, u32[]{:S(2)}, u32[]{:S(2)}) %collective-permute-start.1) | collective-permute-done | bytes 524320 | tf_op jit(solution)/shard_map/ppermute | solution.py:282
  78.2 1.3 own_half.1
  79.5 1.4 other_half.1
  80.9 29.0 %all_to_all.26.refs_0_ = bf16[32,16,512]{2,1,0:T(8,128)(2,1)S(1)} all-to-all(bf16[32,16,512]{2,1,0:T(8,128)(2,1)S(1)} %get-tuple-element.21), channel_id=1, replica_groups=mesh['yh'=4,'yl'=2,'xh'=2,'core'=2,'z'=8,'xl'=2] {'yh','z'}, dimensions={0} | all-to-all | bytes 1048576 | tf_op jit(solution)/shard_map/all_to_all | solution.py:296
  109.9 0.2 reduce_terms.1
  110.1 37.4 %all_to_all.27.rows.back = bf16[16,144,512]{2,1,0:T(8,128)(2,1)S(1)} all-to-all(bf16[16,144,512]{2,1,0:T(8,128)(2,1)S(1)} %get-tuple-element.24), channel_id=1, replica_groups=mesh['yh'=4,'yl'=2,'xh'=2,'core'=2,'z'=8,'xl'=2] {'yl','xh','core','xl'}, dimensions={0} | all-to-all | bytes 4718592 | tf_op jit(solution)/shard_map/all_to_all | solution.py:299
  147.5 0.2 spread.1
  147.7 20.1 %all_to_all.28.plane.mine = bf16[16,16,640]{2,1,0:T(8,128)(2,1)S(1)} all-to-all(bf16[16,16,640]{2,1,0:T(8,128)(2,1)S(1)} %spread.1), channel_id=1, replica_groups=mesh['yh'=4,'yl'=2,'xh'=2,'core'=2,'z'=8,'xl'=2] {'yh','yl','xh'}, dimensions={0} | all-to-all | bytes 655360 | tf_op jit(solution)/shard_map/all_to_all | solution.py:302
  167.8 3.8 %collective-permute-start.2 = (bf16[16,16,640]{2,1,0:T(8,128)(2,1)S(1)}, bf16[16,16,640]{2,1,0:T(8,128)(2,1)S(1)}, u32[]{:S(2)}, u32[]{:S(2)}) collective-permute-start(bf16[16,16,640]{2,1,0:T(8,128)(2,1)S(1)} %all_to_all.28.plane.mine), channel_id=1, source_target_pairs={{0,16},{16,0},{1,17},{17,1},{2,18},{18,2},{3,19},{19,3},{4,20},{20... | collective-permute-start | bytes 983048 | tf_op jit(solution)/shard_map/ppermute | solution.py:277
  171.6 0.6 tile.1
  172.2 3.3 %all-to-all-start.4 = ((f32[8,8,128]{2,1,0:T(8,128)}), f32[8,8,128]{2,1,0:T(8,128)S(1)}, u32[]{:S(2)}, u32[]{:S(2)}) async-start(f32[8,8,128]{2,1,0:T(8,128)} %tile.1), calls=%async_computation.4 | async-start | bytes 65536 | tf_op jit(solution)/shard_map/all_to_all | solution.py:304
  175.6 3.6 %unpack.1 = bf16[128,8192]{1,0:T(8,128)(2,1)} custom-call(s32[8]{0:T(128)S(1)} %compare_select_fusion.place, bf16[16,144,512]{2,1,0:T(8,128)(2,1)S(1)} %all_to_all.27.rows.back), custom_call_target="tpu_custom_call" | custom-call | bytes 5242880 | tf_op jit(solution)/shard_map/unpack/pallas_call | solution.py:237
  179.1 1.0 merge.1
  180.2 2.2 %all-to-all-done.4 = f32[8,8,128]{2,1,0:T(8,128)S(1)} async-done(((f32[8,8,128]{2,1,0:T(8,128)}), f32[8,8,128]{2,1,0:T(8,128)S(1)}, u32[]{:S(2)}, u32[]{:S(2)}) %all-to-all-start.4) | async-done | bytes 32800 | tf_op jit(solution)/shard_map/all_to_all | solution.py:304
  182.4 0.6 reduce_max.18
  (11 shorter events, 0.1 us)
Async XLA Ops:
  0.6 1.6 copy-start
  2.2 1.0 copy-start.1
  3.3 0.9 copy-start.2
  4.2 0.7 copy-start.3
  53.5 26.0 %collective-permute-start = (bf16[16,64,512]{2,1,0:T(8,128)(2,1)S(1)}, bf16[16,64,512]{2,1,0:T(8,128)(2,1)S(1)}, u32[]{:S(2)}, u32[]{:S(2)}) collective-permute-start(bf16[16,64,512]{2,1,0:T(8,128)(2,1)S(1)} %slice.4), channel_id=1, source_target_pairs={{0,16},{16,0},{1,17},{17,1},{2,18},{18,2},{3,19},{19,3},{4,20},{20... | collective-permute-start | bytes 3145736 | tf_op jit(solution)/shard_map/ppermute | solution.py:277
  56.8 21.4 %collective-permute-start.1 = (bf16[512,512]{1,0:T(8,128)(2,1)S(1)}, bf16[512,512]{1,0:T(8,128)(2,1)S(1)}, u32[]{:S(2)}, u32[]{:S(2)}) collective-permute-start(bf16[512,512]{1,0:T(8,128)(2,1)S(1)} %get-tuple-element.17), channel_id=1, source_target_pairs={{0,0},{2,2},{4,4},{6,6},{8,8},{10,10},{12,12},{14,14},{24,16},{26,... | collective-permute-start | bytes 1572872 | tf_op jit(solution)/shard_map/ppermute | solution.py:282
  147.5 28.1 %copy-start.4 = (s32[8]{0:T(128)S(1)}, s32[8]{0:T(128)}, u32[]{:S(2)}) copy-start(s32[8]{0:T(128)} %constant.15.clone) | copy-start | bytes 100
  167.8 11.3 %collective-permute-start.2 = (bf16[16,16,640]{2,1,0:T(8,128)(2,1)S(1)}, bf16[16,16,640]{2,1,0:T(8,128)(2,1)S(1)}, u32[]{:S(2)}, u32[]{:S(2)}) collective-permute-start(bf16[16,16,640]{2,1,0:T(8,128)(2,1)S(1)} %all_to_all.28.plane.mine), channel_id=1, source_target_pairs={{0,16},{16,0},{1,17},{17,1},{2,18},{18,2},{3,19},{19,3},{4,20},{20... | collective-permute-start | bytes 983048 | tf_op jit(solution)/shard_map/ppermute | solution.py:277
  172.2 10.1 %all-to-all-start.4 = ((f32[8,8,128]{2,1,0:T(8,128)}), f32[8,8,128]{2,1,0:T(8,128)S(1)}, u32[]{:S(2)}, u32[]{:S(2)}) async-start(f32[8,8,128]{2,1,0:T(8,128)} %tile.1), calls=%async_computation.4 | async-start | bytes 65536 | tf_op jit(solution)/shard_map/all_to_all | solution.py:304

commit v4 on v3

v4 whole, which is shorter than its diff:
```python
import math

import jax
import jax.numpy as jnp
from jax import lax
from jax.experimental import pallas as pl
from jax.experimental.pallas import tpu as pltpu
from jax.sharding import Mesh
from jax.sharding import PartitionSpec as P

QBLOCK = 128
AXES = ("yh", "yl", "xh", "core", "z", "xl")
SIZES = (4, 2, 2, 2, 8, 2)
GROUP = ("yl", "xh", "core", "xl")
SPREAD = ("yh", "z")
PLANE = ("yh", "yl", "xh")
SHIFT = (0, 4, 1, 7, 2, 6, 3, 5)
BF16 = jnp.bfloat16
F32 = jnp.float32
COUNT = 128
HALF = COUNT // 2
KW = 512
PACK = COUNT + HALF
WIDE = KW + 128
PARAMS = pltpu.CompilerParams(vmem_limit_bytes=24 * 2**20)
VMEM = pl.BlockSpec(memory_space=pltpu.VMEM)
ANY = pl.BlockSpec(memory_space=pl.ANY)


def call(kernel, name, out_shape, in_specs, out_specs, flops, moved, **more):
    return pl.pallas_call(
        kernel,
        in_specs=in_specs,
        out_specs=out_specs,
        out_shape=out_shape,
        compiler_params=PARAMS,
        cost_estimate=pl.CostEstimate(flops=flops, bytes_accessed=moved, transcendentals=0),
        name=name,
        **more,
    )


def array(shape, dtype=BF16):
    return jax.ShapeDtypeStruct(shape, dtype)


def pack_kernel(tokens, keys, codes, scales, out, weight, columns, own, held, ready, scaled, sems):
    loads = [
        pltpu.make_async_copy(tokens.at[:, pl.ds(z * 1024, 1024)], columns.at[z], sems.at[z]) for z in range(8)
    ]
    loads.append(pltpu.make_async_copy(keys, own, sems.at[8]))
    loads.append(pltpu.make_async_copy(codes, held, sems.at[9]))
    for load in loads[8:] + loads[:8]:
        load.start()
    stores = []
    loads[9].wait()
    for block in range(4):
        rows = pl.ds(block * QBLOCK, QBLOCK)
        scaled[rows, :] = (held[rows, :].astype(F32) * scales[block]).astype(BF16)
    stores.append(pltpu.make_async_copy(scaled, weight, sems.at[10]))
    stores[-1].start()
    loads[8].wait()
    for part in range(16):
        core = part // 2 % 2
        ready[part, COUNT:PACK, :] = own[core * HALF : (core + 1) * HALF, :]
    low = lax.broadcasted_iota(jnp.int32, (HALF, 128), 1) < 64
    for m in range(4):
        loads[2 * m].wait()
        loads[2 * m + 1].wait()
        lanes = pl.ds(m * 128, 128)
        for t in range(4):
            for e in range(2):
                for half in range(2):
                    rows = pl.ds(half * HALF, HALF)
                    column = pl.ds(e * 512 + t * 128, 128)
                    even = columns[2 * m, rows, column]
                    odd = columns[2 * m + 1, rows, column]
                    for core in range(2):
                        first, second = (even, odd) if core == 0 else (odd, even)
                        at = HALF * (half ^ core)
                        ready[t * 4 + core * 2 + e, at : at + HALF, lanes] = jnp.where(low, first, second)
        stores.append(pltpu.make_async_copy(ready.at[:, :, lanes], out.at[:, :, lanes], sems.at[11 + m]))
        stores[-1].start()
    for store in stores:
        store.wait()


def hbm(x):
    return pltpu.with_memory_space_constraint(x, pltpu.HBM)


def pack(tokens, key_grad, codes, scales):
    return call(
        pack_kernel,
        "pack",
        [pltpu.HBM((16, PACK, KW), BF16), pltpu.HBM((512, KW), BF16)],
        [ANY, ANY, ANY, pl.BlockSpec(memory_space=pltpu.SMEM)],
        [ANY, ANY],
        0,
        9 * 2**20,
        scratch_shapes=[
            pltpu.VMEM((8, COUNT, 1024), BF16),
            pltpu.VMEM((COUNT, KW), BF16),
            pltpu.VMEM((512, KW), BF16),
            pltpu.VMEM((16, PACK, KW), BF16),
            pltpu.VMEM((512, KW), BF16),
            pltpu.SemaphoreType.DMA((15,)),
        ],
    )(hbm(tokens), hbm(key_grad), hbm(codes), scales)


def gradients(rows, keys):
    return lax.dot_general(
        rows.reshape(-1, KW), keys.reshape(-1, KW), (((0,), (0,)), ((), ())), preferred_element_type=F32
    )


def products(keys, weight):
    out = lax.dot_general(
        keys.reshape(-1, KW), weight, (((1,), (1,)), ((), ())), preferred_element_type=F32
    ).astype(BF16)
    return out, jnp.max(jnp.abs(out.astype(F32)).reshape(-1, 8, KW), axis=0)


def own_kernel(got, weight, total, product, high):
    total[...] = gradients(got[:, 0:HALF, :], got[:, COUNT:PACK, :])
    out, size = products(got[:, COUNT:PACK, :], weight[...])
    product[...] = out.reshape(16, HALF, KW)
    high[...] = size


def own_half(got, weight):
    return call(
        own_kernel,
        "own_half",
        [array((KW, KW), F32), array((16, HALF, KW)), array((8, KW), F32)],
        [VMEM] * 2,
        [VMEM] * 3,
        2**30,
        5 * 2**20,
    )(got, weight)


def other_kernel(got, other, weight, total, product, high_in, share, back, high):
    core = lax.axis_index("core")
    out, size = products(other[...], weight[...])
    back[:, 0:HALF, :] = product[...]
    back[:, HALF:COUNT, :] = out.reshape(16, HALF, KW)
    high[...] = jnp.maximum(high_in[...], size)
    summed = (total[...] + gradients(got[:, HALF:COUNT, :], other[...])).astype(BF16)
    for m in range(4):
        for s in range(2):
            z = 2 * m + jnp.where(core == 0, s, 1 - s)
            for yh in range(4):
                row = m * 128 + s * 64 + yh * 16
                share[yh * 8 + z] = summed[row : row + 16, :]


def other_half(got, other, weight, total, product, high):
    return call(
        other_kernel,
        "other_half",
        [array((32, 16, KW)), array((16, COUNT, KW)), array((8, KW), F32)],
        [VMEM] * 6,
        [VMEM] * 3,
        2**30,
        7 * 2**20,
    )(got, other, weight, total, product, high)


def reduce_kernel(factor, terms, high, piece, peaks):
    total = terms[0].astype(F32)
    for k in range(1, 32):
        total += terms[k].astype(F32)
    rounded = (total * factor).astype(BF16)
    piece[...] = rounded
    first = jnp.max(high[...])
    second = jnp.max(jnp.abs(rounded.astype(F32)))
    lane = lax.broadcasted_iota(jnp.int32, (8, 128), 1)
    peaks[...] = jnp.where(lane < 64, first, second)


def reduce_terms(factor, terms, high):
    return call(
        lambda *refs: reduce_kernel(factor, *refs),
        "reduce_terms",
        [array((16, KW)), array((8, 128), F32)],
        [VMEM] * 2,
        [VMEM] * 2,
        2**18,
        2**20,
    )(terms, high)


def spread_kernel(piece, peaks, out):
    line = jnp.concatenate([peaks[...], peaks[...]], axis=0).astype(BF16)
    for k in range(16):
        out[k, :, 0:KW] = piece[...]
        out[k, :, KW:WIDE] = line


def spread(piece, peaks):
    return call(spread_kernel, "spread", array((16, 16, WIDE)), [VMEM] * 2, VMEM, 0, 2**19)(piece, peaks)


def unpack_kernel(place, back, out):
    second = pl.program_id(0) % 2

    def put(first):
        for e in range(2):
            lanes = pl.ds(e * 512, 512)
            out[first : first + HALF, lanes] = back[e, 0:HALF, :]
            out[HALF - first : COUNT - first, lanes] = back[e, HALF:COUNT, :]

    @pl.when(second == 0)
    def _():
        put(0)

    @pl.when(second == 1)
    def _():
        put(HALF)


def unpack(place, back):
    return pl.pallas_call(
        unpack_kernel,
        grid_spec=pltpu.PrefetchScalarGridSpec(
            num_scalar_prefetch=1,
            grid=(8,),
            in_specs=[pl.BlockSpec((2, COUNT, KW), lambda i, place: (i, 0, 0))],
            out_specs=pl.BlockSpec((COUNT, 1024), lambda i, place: (0, place[i])),
        ),
        out_shape=array((COUNT, 8192)),
        compiler_params=PARAMS,
        cost_estimate=pl.CostEstimate(flops=0, bytes_accessed=5 * 2**20, transcendentals=0),
        name="unpack",
    )(place, back)


def merge_kernel(mine, other, out, peaks):
    turn = lax.rem(lax.axis_index("core") + lax.axis_index("z"), 2)
    for source, s in ((mine, turn), (other, 1 - turn)):
        for yh in range(4):
            for t in range(4):
                row = pl.multiple_of(t * 128 + s * 64 + yh * 16, 16)
                out[pl.ds(row, 16), :] = source[yh * 4 + t, :, 0:KW].astype(F32)
    high = jnp.maximum(mine[:, :, KW:WIDE], other[:, :, KW:WIDE]).astype(F32)
    high = jnp.max(high.reshape(32, 8, 128), axis=0)
    low = lax.broadcasted_iota(jnp.int32, (8, 128), 1) < 64
    peaks[0] = jnp.max(jnp.where(low, high, 0.0))
    peaks[1] = jnp.max(jnp.where(low, 0.0, high))


def merge(plane, other):
    return call(
        merge_kernel,
        "merge",
        [array((512, KW), F32), array((2,), F32)],
        [VMEM] * 2,
        [VMEM, pl.BlockSpec(memory_space=pltpu.SMEM)],
        0,
        2 * 2**20,
    )(plane, other)


def over_shards(peaks):
    for step in (1, 2, 4):
        peaks = jnp.maximum(peaks, lax.ppermute(peaks, "z", [(z, (z + step) % 8) for z in range(8)]))
    return jnp.maximum(peaks, lax.ppermute(peaks, "xl", [(0, 1), (1, 0)]))


def swap(x):
    return lax.ppermute(x, "core", [(0, 1), (1, 0)])


def shift_weight(weight):
    pairs = [(q * 8 + (z + SHIFT[q]) % 8, q * 8 + z) for q in range(8) for z in range(8)]
    return lax.ppermute(weight, ("yl", "xh", "core", "z"), pairs)


def local(tokens, key_grad, weight_codes, block_scales):
    factor = 1.0 / math.sqrt(512 * COUNT)
    place = lax.rem(jnp.array(SHIFT, jnp.int32) + lax.axis_index("z"), 8)

    packed, weight = pack(tokens, key_grad, weight_codes, block_scales)
    weight = shift_weight(weight)
    got = lax.all_to_all(packed, GROUP, 0, 0, tiled=True)
    got, weight = lax.optimization_barrier((got, weight))
    other = swap(got[:, COUNT:])
    total, product, high = own_half(got, weight)
    share, back, high = other_half(got, other, weight, total, product, high)

    terms = lax.all_to_all(share, SPREAD, 0, 0, tiled=True)
    piece, peaks = reduce_terms(factor, terms, high)

    back, piece = lax.optimization_barrier((back, piece))
    back = lax.all_to_all(back, GROUP, 0, 0, tiled=True)
    peaks = over_shards(peaks)
    back, piece, peaks = lax.optimization_barrier((back, piece, peaks))
    input_grad = unpack(place, back)

    plane = lax.all_to_all(spread(piece, peaks), PLANE, 0, 0, tiled=True)
    weight_grad, peaks = merge(plane, swap(plane))
    return (input_grad, weight_grad, peaks)


def solution(mesh):
    fine = Mesh(mesh.devices.reshape(SIZES), AXES)
    return jax.shard_map(
        local,
        mesh=fine,
        in_specs=(P(AXES, None), P(AXES, None), P(("z", "xl"), None), P(("z", "xl"))),
        out_specs=(P(AXES, None), P(("z", "xl"), None), P()),
        check_vma=False,
    )
```

time: 184 us -> 154 us (0.84)
  blocking collectives: 134 us -> 45.6 us
  starting transfers between devices: 18.3 us -> 51.4 us
  waiting for transfers between devices: 15.7 us -> 40.2 us
    all_to_all x3 -> x1, blocking collectives: 105 us -> 19 us  [local(): plane = lax.all_to_all(spread(piece, peaks), PLANE, 0, 0, tiled=True)]
    all_to_all x1 -> x2, waiting for transfers between devices: 2.15 us -> 22.3 us  [the longest x1 21.9 us: local(): got = lax.all_to_all(packed, GROUP, 0, 0, tiled=True)]
    all_to_all x1 -> x2, starting transfers between devices: 3.34 us -> 18.8 us  [the longest x1 10.4 us: local(): got = lax.all_to_all(packed, GROUP, 0, 0, tiled=True)]
    ppermute x0 -> x4, starting transfers between devices: none -> 14.5 us  [the longest x3 11.3 us: over_shards(): lax.ppermute(peaks, 'z', [(z, (z + step) % 8) for z in range(8)])]
    ppermute x0 -> x4, waiting for transfers between devices: none -> 10.8 us  [the longest x3 9.29 us: over_shards(): lax.ppermute(peaks, 'z', [(z, (z + step) % 8) for z in range(8)])]
    ppermute x1, waiting for transfers between devices: 13.5 us -> 7.17 us  [shift_weight(): return lax.ppermute(weight, ('yl', 'xh', 'core', 'z'), pairs)]
    ppermute x2, starting transfers between devices: 7.11 us -> 11.1 us  [swap(): return lax.ppermute(x, 'core', [(0, 1), (1, 0)])]
    all_to_all x1, blocking collectives: 29 us -> 26.6 us  [local(): terms = lax.all_to_all(share, SPREAD, 0, 0, tiled=True)]
  transfers between devices with their start and end apart: 4 -> 9, of which waited for: 2 -> 7; matrix products, arithmetic and copies ran while one was open for 0% -> 0% of each run, Pallas kernels for 4% -> 3%
where the time goes in v4:
time: 154 us; the launch traced here: 153 us
  starting transfers between devices  51.4 us (33%)
  blocking collectives  45.6 us (30%)
  waiting for transfers between devices  40.2 us (26%)
  Pallas kernels  11.3 us (7%)
  local copies, waits for them, and re-layouts  3.88 us (3%)
    all_to_all x1, blocking collectives, local(): terms = lax.all_to_all(share, SPREAD, 0, 0, tiled=True)  26.6 us
    all_to_all x1, waiting for transfers between devices, local(): got = lax.all_to_all(packed, GROUP, 0, 0, tiled=True)  21.9 us
    all_to_all x1, blocking collectives, local(): plane = lax.all_to_all(spread(piece, peaks), PLANE, 0, 0, tiled=True)  19 us
    ppermute x3, starting transfers between devices, over_shards(): lax.ppermute(peaks, 'z', [(z, (z + step) % 8) for z in range(8)])  11.3 us
    ppermute x2, starting transfers between devices, swap(): return lax.ppermute(x, 'core', [(0, 1), (1, 0)])  11.1 us
    all_to_all x1, starting transfers between devices, local(): got = lax.all_to_all(packed, GROUP, 0, 0, tiled=True)  10.4 us
    ppermute x3, waiting for transfers between devices, over_shards(): lax.ppermute(peaks, 'z', [(z, (z + step) % 8) for z in range(8)])  9.29 us
    all_to_all x1, starting transfers between devices, local(): back = lax.all_to_all(back, GROUP, 0, 0, tiled=True)  8.33 us
  transfers between devices with their start and end apart: 9, of which 7 were waited for; matrix products, arithmetic and copies ran while one was open for 0% of the time, Pallas kernels for 3%

profile of v4, /device:TPU:1, one launch (start us, length us, event | category | flops | bytes accessed | tf_op | source)
XLA Modules:
  0.0 153.2 jit_solution(7603110670685857982)
XLA Ops:
  1.3 3.8 %pack.1 = (bf16[16,192,512]{2,1,0:T(8,128)(2,1)}, bf16[512,512]{1,0:T(8,128)(2,1)}) custom-call(bf16[128,8192]{1,0:T(8,128)(2,1)} %tokens.1, bf16[128,512]{1,0:T(8,128)(2,1)} %keys.1, bf16[512,512]{1,0:T(8,128)(2,1)} %codes.1, f32[4]{0:T(128)S(1)} %copy-done.3), custom_call_target="tpu_custom_call" | custom-call | bytes 9437184 | tf_op jit(solution)/shard_map/pack/pallas_call | solution.py:93
  5.1 10.4 %all-to-all-start = ((bf16[16,192,512]{2,1,0:T(8,128)(2,1)}), bf16[16,192,512]{2,1,0:T(8,128)(2,1)S(1)}, u32[]{:S(2)}, u32[]{:S(2)}) async-start(bf16[16,192,512]{2,1,0:T(8,128)(2,1)} %get-tuple-element.22), calls=%async_computation | async-start | bytes 6291456 | tf_op jit(solution)/shard_map/all_to_all | solution.py:287
  15.5 7.0 %collective-permute-start = (bf16[512,512]{1,0:T(8,128)(2,1)}, bf16[512,512]{1,0:T(8,128)(2,1)S(1)}, u32[]{:S(2)}, u32[]{:S(2)}) collective-permute-start(bf16[512,512]{1,0:T(8,128)(2,1)} %get-tuple-element.23), channel_id=1, source_target_pairs={{0,0},{2,2},{4,4},{6,6},{8,8},{10,10},{12,12},{14,14},{24,16},{26,... | collective-permute-start | bytes 1572872 | tf_op jit(solution)/shard_map/ppermute | solution.py:278
  22.5 7.2 %collective-permute-done.weight = bf16[512,512]{1,0:T(8,128)(2,1)S(1)} collective-permute-done((bf16[512,512]{1,0:T(8,128)(2,1)}, bf16[512,512]{1,0:T(8,128)(2,1)S(1)}, u32[]{:S(2)}, u32[]{:S(2)}) %collective-permute-start) | collective-permute-done | bytes 524320 | tf_op jit(solution)/shard_map/ppermute | solution.py:278
  30.5 21.9 %all-to-all-done.got = bf16[16,192,512]{2,1,0:T(8,128)(2,1)S(1)} async-done(((bf16[16,192,512]{2,1,0:T(8,128)(2,1)}), bf16[16,192,512]{2,1,0:T(8,128)(2,1)S(1)}, u32[]{:S(2)}, u32[]{:S(2)}) %all-to-all-start) | async-done | bytes 3145760 | tf_op jit(solution)/shard_map/all_to_all | solution.py:287
  52.5 4.0 %collective-permute-start.1 = (bf16[16,64,512]{2,1,0:T(8,128)(2,1)S(1)}, bf16[16,64,512]{2,1,0:T(8,128)(2,1)S(1)}, u32[]{:S(2)}, u32[]{:S(2)}) collective-permute-start(bf16[16,64,512]{2,1,0:T(8,128)(2,1)S(1)} %slice.3), channel_id=1, source_target_pairs={{0,16},{16,0},{1,17},{17,1},{2,18},{18,2},{3,19},{19,3},{4,20},{20... | collective-permute-start | bytes 3145736 | tf_op jit(solution)/shard_map/ppermute | solution.py:273
  56.5 1.0 copy-done.2
  57.6 1.3 own_half.1
  58.9 1.4 other_half.1
  60.2 1.3 copy-done
  61.6 26.6 %all_to_all.20.refs_0_ = bf16[32,16,512]{2,1,0:T(8,128)(2,1)S(1)} all-to-all(bf16[32,16,512]{2,1,0:T(8,128)(2,1)S(1)} %get-tuple-element.30), channel_id=1, replica_groups=mesh['yh'=4,'yl'=2,'xh'=2,'core'=2,'z'=8,'xl'=2] {'yh','z'}, dimensions={0} | all-to-all | bytes 1048576 | tf_op jit(solution)/shard_map/all_to_all | solution.py:293
  88.4 8.3 %all-to-all-start.2 = ((bf16[16,128,512]{2,1,0:T(8,128)(2,1)}), bf16[16,128,512]{2,1,0:T(8,128)(2,1)S(1)}, u32[]{:S(2)}, u32[]{:S(2)}) async-start(bf16[16,128,512]{2,1,0:T(8,128)(2,1)} %copy-done), calls=%async_computation.2 | async-start | bytes 4194304 | tf_op jit(solution)/shard_map/all_to_all | solution.py:297
  96.7 3.9 %collective-permute-start.2 = (f32[8,128]{1,0:T(8,128)S(1)}, f32[8,128]{1,0:T(8,128)S(1)}, u32[]{:S(2)}, u32[]{:S(2)}) collective-permute-start(f32[8,128]{1,0:T(8,128)S(1)} %get-tuple-element.35), channel_id=1, source_target_pairs={{0,2},{2,4},{4,6},{6,8},{8,10},{10,12},{12,14},{14,0},{1,3},{3,5},... | collective-permute-start | bytes 12296 | tf_op jit(solution)/shard_map/ppermute | solution.py:268
  100.6 2.0 %collective-permute-done.2 = f32[8,128]{1,0:T(8,128)S(1)} collective-permute-done((f32[8,128]{1,0:T(8,128)S(1)}, f32[8,128]{1,0:T(8,128)S(1)}, u32[]{:S(2)}, u32[]{:S(2)}) %collective-permute-start.2) | collective-permute-done | bytes 4128 | tf_op jit(solution)/shard_map/ppermute | solution.py:268
  102.6 2.9 %collective-permute-start.3 = (f32[8,128]{1,0:T(8,128)S(1)}, f32[8,128]{1,0:T(8,128)S(1)}, u32[]{:S(2)}, u32[]{:S(2)}) collective-permute-start(f32[8,128]{1,0:T(8,128)S(1)} %max.12), channel_id=1, source_target_pairs={{0,4},{2,6},{4,8},{6,10},{8,12},{10,14},{12,0},{14,2},{1,5},{3,7},... | collective-permute-start | bytes 12296 | tf_op jit(solution)/shard_map/ppermute | solution.py:268
  105.5 3.6 %collective-permute-done.3 = f32[8,128]{1,0:T(8,128)S(1)} collective-permute-done((f32[8,128]{1,0:T(8,128)S(1)}, f32[8,128]{1,0:T(8,128)S(1)}, u32[]{:S(2)}, u32[]{:S(2)}) %collective-permute-start.3) | collective-permute-done | bytes 4128 | tf_op jit(solution)/shard_map/ppermute | solution.py:268
  109.0 4.5 %collective-permute-start.4 = (f32[8,128]{1,0:T(8,128)S(1)}, f32[8,128]{1,0:T(8,128)S(1)}, u32[]{:S(2)}, u32[]{:S(2)}) collective-permute-start(f32[8,128]{1,0:T(8,128)S(1)} %max.13), channel_id=1, source_target_pairs={{0,8},{2,10},{4,12},{6,14},{8,0},{10,2},{12,4},{14,6},{1,9},{3,11}... | collective-permute-start | bytes 12296 | tf_op jit(solution)/shard_map/ppermute | solution.py:268
  113.5 3.8 %collective-permute-done.4 = f32[8,128]{1,0:T(8,128)S(1)} collective-permute-done((f32[8,128]{1,0:T(8,128)S(1)}, f32[8,128]{1,0:T(8,128)S(1)}, u32[]{:S(2)}, u32[]{:S(2)}) %collective-permute-start.4) | collective-permute-done | bytes 4128 | tf_op jit(solution)/shard_map/ppermute | solution.py:268
  117.3 3.2 %collective-permute-start.5 = (f32[8,128]{1,0:T(8,128)S(1)}, f32[8,128]{1,0:T(8,128)S(1)}, u32[]{:S(2)}, u32[]{:S(2)}) collective-permute-start(f32[8,128]{1,0:T(8,128)S(1)} %max.14), channel_id=1, source_target_pairs={{0,1},{1,0},{2,3},{3,2},{4,5},{5,4},{6,7},{7,6},{8,9},{9,8},{10,11... | collective-permute-start | bytes 12296 | tf_op jit(solution)/shard_map/ppermute | solution.py:269
  120.5 1.5 collective-permute-done.5
  122.4 19.0 %all_to_all.21.mine = bf16[16,16,640]{2,1,0:T(8,128)(2,1)S(1)} all-to-all(bf16[16,16,640]{2,1,0:T(8,128)(2,1)S(1)} %spread.1), channel_id=1, replica_groups=mesh['yh'=4,'yl'=2,'xh'=2,'core'=2,'z'=8,'xl'=2] {'yh','yl','xh'}, dimensions={0} | all-to-all | bytes 655360 | tf_op jit(solution)/shard_map/all_to_all | solution.py:302
  141.5 7.1 %collective-permute-start.6 = (bf16[16,16,640]{2,1,0:T(8,128)(2,1)S(1)}, bf16[16,16,640]{2,1,0:T(8,128)(2,1)S(1)}, u32[]{:S(2)}, u32[]{:S(2)}) collective-permute-start(bf16[16,16,640]{2,1,0:T(8,128)(2,1)S(1)} %all_to_all.21.mine), channel_id=1, source_target_pairs={{0,16},{16,0},{1,17},{17,1},{2,18},{18,2},{3,19},{19,3},{4,20},{20... | collective-permute-start | bytes 983048 | tf_op jit(solution)/shard_map/ppermute | solution.py:273
  148.6 3.6 %unpack.1 = bf16[128,8192]{1,0:T(8,128)(2,1)} custom-call(s32[8]{0:T(128)S(1)} %compare_select_fusion.place, bf16[16,128,512]{2,1,0:T(8,128)(2,1)S(1)} %all-to-all-done.2.back), custom_call_target="tpu_custom_call" | custom-call | bytes 5242880 | tf_op jit(solution)/shard_map/unpack/pallas_call | solution.py:225
  152.1 1.1 merge.1
  (19 shorter events, 2.2 us)
Async XLA Ops:
  0.6 0.7 copy-start.3
  5.1 47.3 %all-to-all-start = ((bf16[16,192,512]{2,1,0:T(8,128)(2,1)}), bf16[16,192,512]{2,1,0:T(8,128)(2,1)S(1)}, u32[]{:S(2)}, u32[]{:S(2)}) async-start(bf16[16,192,512]{2,1,0:T(8,128)(2,1)} %get-tuple-element.22), calls=%async_computation | async-start | bytes 6291456 | tf_op jit(solution)/shard_map/all_to_all | solution.py:287
  15.5 14.2 %collective-permute-start = (bf16[512,512]{1,0:T(8,128)(2,1)}, bf16[512,512]{1,0:T(8,128)(2,1)S(1)}, u32[]{:S(2)}, u32[]{:S(2)}) collective-permute-start(bf16[512,512]{1,0:T(8,128)(2,1)} %get-tuple-element.23), channel_id=1, source_target_pairs={{0,0},{2,2},{4,4},{6,6},{8,8},{10,10},{12,12},{14,14},{24,16},{26,... | collective-permute-start | bytes 1572872 | tf_op jit(solution)/shard_map/ppermute | solution.py:278
  29.7 0.8 copy-start.1
  52.5 6.4 %collective-permute-start.1 = (bf16[16,64,512]{2,1,0:T(8,128)(2,1)S(1)}, bf16[16,64,512]{2,1,0:T(8,128)(2,1)S(1)}, u32[]{:S(2)}, u32[]{:S(2)}) collective-permute-start(bf16[16,64,512]{2,1,0:T(8,128)(2,1)S(1)} %slice.3), channel_id=1, source_target_pairs={{0,16},{16,0},{1,17},{17,1},{2,18},{18,2},{3,19},{19,3},{4,20},{20... | collective-permute-start | bytes 3145736 | tf_op jit(solution)/shard_map/ppermute | solution.py:273
  56.5 1.0 copy-start.2
  60.2 1.3 copy-start
  88.4 60.2 %copy-start.4 = (s32[8]{0:T(128)S(1)}, s32[8]{0:T(128)}, u32[]{:S(2)}) copy-start(s32[8]{0:T(128)} %constant.13.clone) | copy-start | bytes 100
  88.4 34.0 %all-to-all-start.2 = ((bf16[16,128,512]{2,1,0:T(8,128)(2,1)}), bf16[16,128,512]{2,1,0:T(8,128)(2,1)S(1)}, u32[]{:S(2)}, u32[]{:S(2)}) async-start(bf16[16,128,512]{2,1,0:T(8,128)(2,1)} %copy-done), calls=%async_computation.2 | async-start | bytes 4194304 | tf_op jit(solution)/shard_map/all_to_all | solution.py:297
  96.7 5.9 %collective-permute-start.2 = (f32[8,128]{1,0:T(8,128)S(1)}, f32[8,128]{1,0:T(8,128)S(1)}, u32[]{:S(2)}, u32[]{:S(2)}) collective-permute-start(f32[8,128]{1,0:T(8,128)S(1)} %get-tuple-element.35), channel_id=1, source_target_pairs={{0,2},{2,4},{4,6},{6,8},{8,10},{10,12},{12,14},{14,0},{1,3},{3,5},... | collective-permute-start | bytes 12296 | tf_op jit(solution)/shard_map/ppermute | solution.py:268
  102.6 6.5 %collective-permute-start.3 = (f32[8,128]{1,0:T(8,128)S(1)}, f32[8,128]{1,0:T(8,128)S(1)}, u32[]{:S(2)}, u32[]{:S(2)}) collective-permute-start(f32[8,128]{1,0:T(8,128)S(1)} %max.12), channel_id=1, source_target_pairs={{0,4},{2,6},{4,8},{6,10},{8,12},{10,14},{12,0},{14,2},{1,5},{3,7},... | collective-permute-start | bytes 12296 | tf_op jit(solution)/shard_map/ppermute | solution.py:268
  109.0 8.2 %collective-permute-start.4 = (f32[8,128]{1,0:T(8,128)S(1)}, f32[8,128]{1,0:T(8,128)S(1)}, u32[]{:S(2)}, u32[]{:S(2)}) collective-permute-start(f32[8,128]{1,0:T(8,128)S(1)} %max.13), channel_id=1, source_target_pairs={{0,8},{2,10},{4,12},{6,14},{8,0},{10,2},{12,4},{14,6},{1,9},{3,11}... | collective-permute-start | bytes 12296 | tf_op jit(solution)/shard_map/ppermute | solution.py:268
  117.3 4.7 %collective-permute-start.5 = (f32[8,128]{1,0:T(8,128)S(1)}, f32[8,128]{1,0:T(8,128)S(1)}, u32[]{:S(2)}, u32[]{:S(2)}) collective-permute-start(f32[8,128]{1,0:T(8,128)S(1)} %max.14), channel_id=1, source_target_pairs={{0,1},{1,0},{2,3},{3,2},{4,5},{5,4},{6,7},{7,6},{8,9},{9,8},{10,11... | collective-permute-start | bytes 12296 | tf_op jit(solution)/shard_map/ppermute | solution.py:269
  141.5 10.6 %collective-permute-start.6 = (bf16[16,16,640]{2,1,0:T(8,128)(2,1)S(1)}, bf16[16,16,640]{2,1,0:T(8,128)(2,1)S(1)}, u32[]{:S(2)}, u32[]{:S(2)}) collective-permute-start(bf16[16,16,640]{2,1,0:T(8,128)(2,1)S(1)} %all_to_all.21.mine), channel_id=1, source_target_pairs={{0,16},{16,0},{1,17},{17,1},{2,18},{18,2},{3,19},{19,3},{4,20},{20... | collective-permute-start | bytes 983048 | tf_op jit(solution)/shard_map/ppermute | solution.py:273

commit v5 on v4

--- a/solution.py
+++ b/solution.py
@@ -44,19 +44,21 @@
     return jax.ShapeDtypeStruct(shape, dtype)
 
 
-def pack_kernel(tokens, keys, codes, scales, out, weight, columns, own, held, ready, scaled, sems):
+def pack_kernel(tokens, keys, codes, scales, out, weight, columns, own, held, ready, scaled, factors, sems):
     loads = [
         pltpu.make_async_copy(tokens.at[:, pl.ds(z * 1024, 1024)], columns.at[z], sems.at[z]) for z in range(8)
     ]
     loads.append(pltpu.make_async_copy(keys, own, sems.at[8]))
     loads.append(pltpu.make_async_copy(codes, held, sems.at[9]))
+    loads.append(pltpu.make_async_copy(scales, factors, sems.at[15]))
     for load in loads[8:] + loads[:8]:
         load.start()
     stores = []
     loads[9].wait()
+    loads[10].wait()
     for block in range(4):
         rows = pl.ds(block * QBLOCK, QBLOCK)
-        scaled[rows, :] = (held[rows, :].astype(F32) * scales[block]).astype(BF16)
+        scaled[rows, :] = (held[rows, :].astype(F32) * factors[block]).astype(BF16)
     stores.append(pltpu.make_async_copy(scaled, weight, sems.at[10]))
     stores[-1].start()
     loads[8].wait()
@@ -94,8 +96,8 @@
         pack_kernel,
         "pack",
         [pltpu.HBM((16, PACK, KW), BF16), pltpu.HBM((512, KW), BF16)],
-        [ANY, ANY, ANY, pl.BlockSpec(memory_space=pltpu.SMEM)],
-        [ANY, ANY],
+        [ANY] * 4,
+        [ANY] * 2,
         0,
         9 * 2**20,
         scratch_shapes=[
@@ -104,9 +106,10 @@
             pltpu.VMEM((512, KW), BF16),
             pltpu.VMEM((16, PACK, KW), BF16),
             pltpu.VMEM((512, KW), BF16),
-            pltpu.SemaphoreType.DMA((15,)),
+            pltpu.SMEM((4,), F32),
+            pltpu.SemaphoreType.DMA((16,)),
         ],
-    )(hbm(tokens), hbm(key_grad), hbm(codes), scales)
+    )(hbm(tokens), hbm(key_grad), hbm(codes), hbm(scales))
 
 
 def gradients(rows, keys):
@@ -141,11 +144,14 @@
     )(got, weight)
 
 
-def other_kernel(got, other, weight, total, product, high_in, share, back, high):
+def other_kernel(got, other, weight, total, product, high_in, share, back, high, rest, sems):
     core = lax.axis_index("core")
+    first = pltpu.make_async_copy(product, back.at[:, 0:HALF, :], sems.at[0])
+    first.start()
     out, size = products(other[...], weight[...])
-    back[:, 0:HALF, :] = product[...]
-    back[:, HALF:COUNT, :] = out.reshape(16, HALF, KW)
+    rest[...] = out.reshape(16, HALF, KW)
+    second = pltpu.make_async_copy(rest, back.at[:, HALF:COUNT, :], sems.at[1])
+    second.start()
     high[...] = jnp.maximum(high_in[...], size)
     summed = (total[...] + gradients(got[:, HALF:COUNT, :], other[...])).astype(BF16)
     for m in range(4):
@@ -154,17 +160,20 @@
             for yh in range(4):
                 row = m * 128 + s * 64 + yh * 16
                 share[yh * 8 + z] = summed[row : row + 16, :]
+    first.wait()
+    second.wait()
 
 
 def other_half(got, other, weight, total, product, high):
     return call(
         other_kernel,
         "other_half",
-        [array((32, 16, KW)), array((16, COUNT, KW)), array((8, KW), F32)],
+        [array((32, 16, KW)), pltpu.HBM((16, COUNT, KW), BF16), array((8, KW), F32)],
         [VMEM] * 6,
-        [VMEM] * 3,
+        [VMEM, ANY, VMEM],
         2**30,
         7 * 2**20,
+        scratch_shapes=[pltpu.VMEM((16, HALF, KW), BF16), pltpu.SemaphoreType.DMA((2,))],
     )(got, other, weight, total, product, high)
 
 
@@ -203,38 +212,38 @@
     return call(spread_kernel, "spread", array((16, 16, WIDE)), [VMEM] * 2, VMEM, 0, 2**19)(piece, peaks)
 
 
-def unpack_kernel(place, back, out):
-    second = pl.program_id(0) % 2
-
-    def put(first):
+def unpack_kernel(back, out, sems):
+    z = lax.axis_index("z")
+    copies = []
+    for q in range(8):
+        place = lax.rem(z + SHIFT[q], 8) * 1024
         for e in range(2):
-            lanes = pl.ds(e * 512, 512)
-            out[first : first + HALF, lanes] = back[e, 0:HALF, :]
-            out[HALF - first : COUNT - first, lanes] = back[e, HALF:COUNT, :]
-
-    @pl.when(second == 0)
-    def _():
-        put(0)
-
-    @pl.when(second == 1)
-    def _():
-        put(HALF)
-
-
-def unpack(place, back):
-    return pl.pallas_call(
+            lanes = pl.ds(pl.multiple_of(place + e * 512, 512), 512)
+            for half in range(2):
+                at = HALF * (half ^ (q % 2))
+                copies.append(
+                    pltpu.make_async_copy(
+                        back.at[q * 2 + e, pl.ds(half * HALF, HALF), :],
+                        out.at[pl.ds(at, HALF), lanes],
+                        sems.at[len(copies)],
+                    )
+                )
+                copies[-1].start()
+    for copy in copies:
+        copy.wait()
+
+
+def unpack(back):
+    return call(
         unpack_kernel,
-        grid_spec=pltpu.PrefetchScalarGridSpec(
-            num_scalar_prefetch=1,
-            grid=(8,),
-            in_specs=[pl.BlockSpec((2, COUNT, KW), lambda i, place: (i, 0, 0))],
-            out_specs=pl.BlockSpec((COUNT, 1024), lambda i, place: (0, place[i])),
-        ),
-        out_shape=array((COUNT, 8192)),
-        compiler_params=PARAMS,
-        cost_estimate=pl.CostEstimate(flops=0, bytes_accessed=5 * 2**20, transcendentals=0),
-        name="unpack",
-    )(place, back)
+        "unpack",
+        pltpu.HBM((COUNT, 8192), BF16),
+        [ANY],
+        ANY,
+        0,
+        4 * 2**20,
+        scratch_shapes=[pltpu.SemaphoreType.DMA((32,))],
+    )(back)
 
 
 def merge_kernel(mine, other, out, peaks):
@@ -245,13 +254,13 @@
                 row = pl.multiple_of(t * 128 + s * 64 + yh * 16, 16)
                 out[pl.ds(row, 16), :] = source[yh * 4 + t, :, 0:KW].astype(F32)
     high = jnp.maximum(mine[:, :, KW:WIDE], other[:, :, KW:WIDE]).astype(F32)
-    high = jnp.max(high.reshape(32, 8, 128), axis=0)
-    low = lax.broadcasted_iota(jnp.int32, (8, 128), 1) < 64
+    high = jnp.max(high, axis=0)
+    low = lax.broadcasted_iota(jnp.int32, (16, 128), 1) < 64
     peaks[0] = jnp.max(jnp.where(low, high, 0.0))
     peaks[1] = jnp.max(jnp.where(low, 0.0, high))
 
 
-def merge(plane, other):
+def merge(mine, other):
     return call(
         merge_kernel,
         "merge",
@@ -260,17 +269,27 @@
         [VMEM, pl.BlockSpec(memory_space=pltpu.SMEM)],
         0,
         2 * 2**20,
-    )(plane, other)
+    )(mine, other)
+
+
+def from_ahead(x, axis, size, step):
+    return lax.ppermute(x, axis, [((i + step) % size, i) for i in range(size)])
 
 
 def over_shards(peaks):
-    for step in (1, 2, 4):
-        peaks = jnp.maximum(peaks, lax.ppermute(peaks, "z", [(z, (z + step) % 8) for z in range(8)]))
-    return jnp.maximum(peaks, lax.ppermute(peaks, "xl", [(0, 1), (1, 0)]))
+    pairs = [(((z + 1) % 8) * 2 + 1 - xl, z * 2 + xl) for z in range(8) for xl in range(2)]
+    near = [
+        from_ahead(peaks, "z", 8, 1),
+        from_ahead(peaks, "xl", 2, 1),
+        lax.ppermute(peaks, ("z", "xl"), pairs),
+    ]
+    peaks = jnp.maximum(jnp.maximum(peaks, near[0]), jnp.maximum(near[1], near[2]))
+    far = [from_ahead(peaks, "z", 8, step) for step in (2, 4, 6)]
+    return jnp.maximum(jnp.maximum(peaks, far[0]), jnp.maximum(far[1], far[2]))
 
 
 def swap(x):
-    return lax.ppermute(x, "core", [(0, 1), (1, 0)])
+    return from_ahead(x, "core", 2, 1)
 
 
 def shift_weight(weight):
@@ -280,7 +299,6 @@
 
 def local(tokens, key_grad, weight_codes, block_scales):
     factor = 1.0 / math.sqrt(512 * COUNT)
-    place = lax.rem(jnp.array(SHIFT, jnp.int32) + lax.axis_index("z"), 8)
 
     packed, weight = pack(tokens, key_grad, weight_codes, block_scales)
     weight = shift_weight(weight)
@@ -297,7 +315,7 @@
     back = lax.all_to_all(back, GROUP, 0, 0, tiled=True)
     peaks = over_shards(peaks)
     back, piece, peaks = lax.optimization_barrier((back, piece, peaks))
-    input_grad = unpack(place, back)
+    input_grad = unpack(back)
 
     plane = lax.all_to_all(spread(piece, peaks), PLANE, 0, 0, tiled=True)
     weight_grad, peaks = merge(plane, swap(plane))

time: 154 us -> 162 us (1.052)
  waiting for transfers between devices: 40.2 us -> 46.5 us
  starting transfers between devices: 51.4 us -> 56 us
  local copies, waits for them, and re-layouts: 3.88 us -> 1.92 us
    ppermute x6 -> x8, waiting for transfers between devices: 10.8 us -> 17.4 us  [the longest x7 17.4 us: from_ahead(): return lax.ppermute(x, axis, [((i + step) % size, i) for i in range(size)])]
    ppermute x6 -> x8, starting transfers between devices: 25.6 us -> 30.2 us  [the longest x7 26 us: from_ahead(): return lax.ppermute(x, axis, [((i + step) % size, i) for i in range(size)])]
    unnamed x10 -> x4, local copies, waits for them, and re-layouts: 3.8 us -> 1.83 us
  transfers between devices with their start and end apart: 9 -> 11, of which waited for: 7 -> 5; matrix products, arithmetic and copies ran while one was open for 0% -> 0% of each run, Pallas kernels for 3% -> 2%
where the time goes in v5:
time: 162 us; the launch traced here: 161 us
  starting transfers between devices  56 us (35%)
  waiting for transfers between devices  46.5 us (29%)
  blocking collectives  46.5 us (29%)
  Pallas kernels  9.71 us (6%)
  local copies, waits for them, and re-layouts  1.92 us (1%)
    all_to_all x1, blocking collectives, local(): terms = lax.all_to_all(share, SPREAD, 0, 0, tiled=True)  26.6 us
    ppermute x7, starting transfers between devices, from_ahead(): return lax.ppermute(x, axis, [((i + step) % size, i) for i in range(size)])  26 us
    all_to_all x1, waiting for transfers between devices, local(): got = lax.all_to_all(packed, GROUP, 0, 0, tiled=True)  21.9 us
    all_to_all x1, blocking collectives, local(): plane = lax.all_to_all(spread(piece, peaks), PLANE, 0, 0, tiled=True)  19.9 us
    ppermute x7, waiting for transfers between devices, from_ahead(): return lax.ppermute(x, axis, [((i + step) % size, i) for i in range(size)])  17.4 us
    all_to_all x1, starting transfers between devices, local(): got = lax.all_to_all(packed, GROUP, 0, 0, tiled=True)  10.4 us
    all_to_all x1, starting transfers between devices, local(): back = lax.all_to_all(back, GROUP, 0, 0, tiled=True)  8.37 us
    ppermute x1, waiting for transfers between devices, shift_weight(): return lax.ppermute(weight, ('yl', 'xh', 'core', 'z'), pairs)  7.17 us
  transfers between devices with their start and end apart: 11, of which 5 were waited for; matrix products, arithmetic and copies ran while one was open for 0% of the time, Pallas kernels for 2%

profile of v5, /device:TPU:1, one launch (start us, length us, event | category | flops | bytes accessed | tf_op | source)
XLA Modules:
  0.0 161.4 jit_solution(11564758221073228753)
XLA Ops:
  0.6 3.2 %pack.1 = (bf16[16,192,512]{2,1,0:T(8,128)(2,1)}, bf16[512,512]{1,0:T(8,128)(2,1)}) custom-call(bf16[128,8192]{1,0:T(8,128)(2,1)} %tokens.1, bf16[128,512]{1,0:T(8,128)(2,1)} %keys.1, bf16[512,512]{1,0:T(8,128)(2,1)} %codes.1, f32[4]{0:T(128)} %scales.1), custom_call_target="tpu_custom_call" | custom-call | bytes 9437184 | tf_op jit(solution)/shard_map/pack/pallas_call | solution.py:95
  3.9 10.4 %all-to-all-start = ((bf16[16,192,512]{2,1,0:T(8,128)(2,1)}), bf16[16,192,512]{2,1,0:T(8,128)(2,1)S(1)}, u32[]{:S(2)}, u32[]{:S(2)}) async-start(bf16[16,192,512]{2,1,0:T(8,128)(2,1)} %get-tuple-element.22), calls=%async_computation | async-start | bytes 6291456 | tf_op jit(solution)/shard_map/all_to_all | solution.py:305
  14.3 7.0 %collective-permute-start = (bf16[512,512]{1,0:T(8,128)(2,1)}, bf16[512,512]{1,0:T(8,128)(2,1)S(1)}, u32[]{:S(2)}, u32[]{:S(2)}) collective-permute-start(bf16[512,512]{1,0:T(8,128)(2,1)} %get-tuple-element.23), channel_id=1, source_target_pairs={{0,0},{2,2},{4,4},{6,6},{8,8},{10,10},{12,12},{14,14},{24,16},{26,... | collective-permute-start | bytes 1572872 | tf_op jit(solution)/shard_map/ppermute | solution.py:297
  21.4 7.2 %collective-permute-done.weight = bf16[512,512]{1,0:T(8,128)(2,1)S(1)} collective-permute-done((bf16[512,512]{1,0:T(8,128)(2,1)}, bf16[512,512]{1,0:T(8,128)(2,1)S(1)}, u32[]{:S(2)}, u32[]{:S(2)}) %collective-permute-start) | collective-permute-done | bytes 524320 | tf_op jit(solution)/shard_map/ppermute | solution.py:297
  28.5 0.8 copy-done
  29.3 21.9 %all-to-all-done.got = bf16[16,192,512]{2,1,0:T(8,128)(2,1)S(1)} async-done(((bf16[16,192,512]{2,1,0:T(8,128)(2,1)}), bf16[16,192,512]{2,1,0:T(8,128)(2,1)S(1)}, u32[]{:S(2)}, u32[]{:S(2)}) %all-to-all-start) | async-done | bytes 3145760 | tf_op jit(solution)/shard_map/all_to_all | solution.py:305
  51.3 4.0 %collective-permute-start.1 = (bf16[16,64,512]{2,1,0:T(8,128)(2,1)S(1)}, bf16[16,64,512]{2,1,0:T(8,128)(2,1)S(1)}, u32[]{:S(2)}, u32[]{:S(2)}) collective-permute-start(bf16[16,64,512]{2,1,0:T(8,128)(2,1)S(1)} %slice.3), channel_id=1, source_target_pairs={{16,0},{0,16},{17,1},{1,17},{18,2},{2,18},{19,3},{3,19},{20,4},{4,... | collective-permute-start | bytes 3145736 | tf_op jit(solution)/shard_map/ppermute | solution.py:276
  55.4 1.0 copy-done.1
  56.4 1.3 own_half.1
  57.7 2.3 %other_half.1 = (bf16[32,16,512]{2,1,0:T(8,128)(2,1)S(1)}, bf16[16,128,512]{2,1,0:T(8,128)(2,1)}, f32[8,512]{1,0:T(8,128)S(1)}) custom-call(bf16[16,192,512]{2,1,0:T(8,128)(2,1)S(1)} %all-to-all-done.got, bf16[16,64,512]{2,1,0:T(8,128)(2,1)S(1)} %collective-permute-done.1.other, bf16[512,512]{1,0:T(8,128)(2,1)S(1)} %copy-done.1, ...), custom_call_target="tpu_custom_call" | custom-call | flops 1073741824 | bytes 7340032 | tf_op jit(solution)/shard_map/other_half/pallas_call | solution.py:168
  60.0 26.6 %all_to_all.20.refs_0_ = bf16[32,16,512]{2,1,0:T(8,128)(2,1)S(1)} all-to-all(bf16[32,16,512]{2,1,0:T(8,128)(2,1)S(1)} %get-tuple-element.30), channel_id=1, replica_groups=mesh['yh'=4,'yl'=2,'xh'=2,'core'=2,'z'=8,'xl'=2] {'yh','z'}, dimensions={0} | all-to-all | bytes 1048576 | tf_op jit(solution)/shard_map/all_to_all | solution.py:311
  86.8 8.4 %all-to-all-start.2 = ((bf16[16,128,512]{2,1,0:T(8,128)(2,1)}), bf16[16,128,512]{2,1,0:T(8,128)(2,1)S(1)}, u32[]{:S(2)}, u32[]{:S(2)}) async-start(bf16[16,128,512]{2,1,0:T(8,128)(2,1)} %get-tuple-element.33), calls=%async_computation.2 | async-start | bytes 4194304 | tf_op jit(solution)/shard_map/all_to_all | solution.py:315
  95.2 4.2 %collective-permute-start.4 = (f32[8,128]{1,0:T(8,128)S(1)}, f32[8,128]{1,0:T(8,128)S(1)}, u32[]{:S(2)}, u32[]{:S(2)}) collective-permute-start(f32[8,128]{1,0:T(8,128)S(1)} %get-tuple-element.35), channel_id=1, source_target_pairs={{3,0},{2,1},{5,2},{4,3},{7,4},{6,5},{9,6},{8,7},{11,8},{10,9},{13,... | collective-permute-start | bytes 12296 | tf_op jit(solution)/shard_map/ppermute | solution.py:284
  99.4 2.0 %collective-permute-start.3 = (f32[8,128]{1,0:T(8,128)S(1)}, f32[8,128]{1,0:T(8,128)S(1)}, u32[]{:S(2)}, u32[]{:S(2)}) collective-permute-start(f32[8,128]{1,0:T(8,128)S(1)} %get-tuple-element.35), channel_id=1, source_target_pairs={{1,0},{0,1},{3,2},{2,3},{5,4},{4,5},{7,6},{6,7},{9,8},{8,9},{11,10... | collective-permute-start | bytes 12296 | tf_op jit(solution)/shard_map/ppermute | solution.py:276
  101.4 2.5 %collective-permute-start.2 = (f32[8,128]{1,0:T(8,128)S(1)}, f32[8,128]{1,0:T(8,128)S(1)}, u32[]{:S(2)}, u32[]{:S(2)}) collective-permute-start(f32[8,128]{1,0:T(8,128)S(1)} %get-tuple-element.35), channel_id=1, source_target_pairs={{2,0},{4,2},{6,4},{8,6},{10,8},{12,10},{14,12},{0,14},{3,1},{5,3},... | collective-permute-start | bytes 12296 | tf_op jit(solution)/shard_map/ppermute | solution.py:276
  103.9 16.3 %collective-permute-done.3 = f32[8,128]{1,0:T(8,128)S(1)} collective-permute-done((f32[8,128]{1,0:T(8,128)S(1)}, f32[8,128]{1,0:T(8,128)S(1)}, u32[]{:S(2)}, u32[]{:S(2)}) %collective-permute-start.3) | collective-permute-done | bytes 4128 | tf_op jit(solution)/shard_map/ppermute | solution.py:276
  120.3 4.0 %collective-permute-start.7 = (f32[8,128]{1,0:T(8,128)S(1)}, f32[8,128]{1,0:T(8,128)S(1)}, u32[]{:S(2)}, u32[]{:S(2)}) collective-permute-start(f32[8,128]{1,0:T(8,128)S(1)} %maximum_maximum_fusion.1), channel_id=1, source_target_pairs={{12,0},{14,2},{0,4},{2,6},{4,8},{6,10},{8,12},{10,14},{13,1},{15,3... | collective-permute-start | bytes 12296 | tf_op jit(solution)/shard_map/ppermute | solution.py:276
  124.3 3.4 %collective-permute-start.6 = (f32[8,128]{1,0:T(8,128)S(1)}, f32[8,128]{1,0:T(8,128)S(1)}, u32[]{:S(2)}, u32[]{:S(2)}) collective-permute-start(f32[8,128]{1,0:T(8,128)S(1)} %maximum_maximum_fusion.1), channel_id=1, source_target_pairs={{8,0},{10,2},{12,4},{14,6},{0,8},{2,10},{4,12},{6,14},{9,1},{11,3}... | collective-permute-start | bytes 12296 | tf_op jit(solution)/shard_map/ppermute | solution.py:276
  127.7 4.5 %collective-permute-start.5 = (f32[8,128]{1,0:T(8,128)S(1)}, f32[8,128]{1,0:T(8,128)S(1)}, u32[]{:S(2)}, u32[]{:S(2)}) collective-permute-start(f32[8,128]{1,0:T(8,128)S(1)} %maximum_maximum_fusion.1), channel_id=1, source_target_pairs={{4,0},{6,2},{8,4},{10,6},{12,8},{14,10},{0,12},{2,14},{5,1},{7,3},... | collective-permute-start | bytes 12296 | tf_op jit(solution)/shard_map/ppermute | solution.py:276
  132.5 0.7 collective-permute-done.5
  133.2 19.9 %all_to_all.21.mine = bf16[16,16,640]{2,1,0:T(8,128)(2,1)S(1)} all-to-all(bf16[16,16,640]{2,1,0:T(8,128)(2,1)S(1)} %spread.1), channel_id=1, replica_groups=mesh['yh'=4,'yl'=2,'xh'=2,'core'=2,'z'=8,'xl'=2] {'yh','yl','xh'}, dimensions={0} | all-to-all | bytes 655360 | tf_op jit(solution)/shard_map/all_to_all | solution.py:320
  153.1 5.7 %collective-permute-start.8 = (bf16[16,16,640]{2,1,0:T(8,128)(2,1)S(1)}, bf16[16,16,640]{2,1,0:T(8,128)(2,1)S(1)}, u32[]{:S(2)}, u32[]{:S(2)}) collective-permute-start(bf16[16,16,640]{2,1,0:T(8,128)(2,1)S(1)} %all_to_all.21.mine), channel_id=1, source_target_pairs={{16,0},{0,16},{17,1},{1,17},{18,2},{2,18},{19,3},{3,19},{20,4},{4,... | collective-permute-start | bytes 983048 | tf_op jit(solution)/shard_map/ppermute | solution.py:276
  158.8 1.6 unpack.1
  160.4 1.1 merge.1
  (14 shorter events, 0.7 us)
Async XLA Ops:
  3.9 47.3 %all-to-all-start = ((bf16[16,192,512]{2,1,0:T(8,128)(2,1)}), bf16[16,192,512]{2,1,0:T(8,128)(2,1)S(1)}, u32[]{:S(2)}, u32[]{:S(2)}) async-start(bf16[16,192,512]{2,1,0:T(8,128)(2,1)} %get-tuple-element.22), calls=%async_computation | async-start | bytes 6291456 | tf_op jit(solution)/shard_map/all_to_all | solution.py:305
  14.3 14.2 %collective-permute-start = (bf16[512,512]{1,0:T(8,128)(2,1)}, bf16[512,512]{1,0:T(8,128)(2,1)S(1)}, u32[]{:S(2)}, u32[]{:S(2)}) collective-permute-start(bf16[512,512]{1,0:T(8,128)(2,1)} %get-tuple-element.23), channel_id=1, source_target_pairs={{0,0},{2,2},{4,4},{6,6},{8,8},{10,10},{12,12},{14,14},{24,16},{26,... | collective-permute-start | bytes 1572872 | tf_op jit(solution)/shard_map/ppermute | solution.py:297
  28.5 0.8 copy-start
  51.3 6.3 %collective-permute-start.1 = (bf16[16,64,512]{2,1,0:T(8,128)(2,1)S(1)}, bf16[16,64,512]{2,1,0:T(8,128)(2,1)S(1)}, u32[]{:S(2)}, u32[]{:S(2)}) collective-permute-start(bf16[16,64,512]{2,1,0:T(8,128)(2,1)S(1)} %slice.3), channel_id=1, source_target_pairs={{16,0},{0,16},{17,1},{1,17},{18,2},{2,18},{19,3},{3,19},{20,4},{4,... | collective-permute-start | bytes 3145736 | tf_op jit(solution)/shard_map/ppermute | solution.py:276
  55.3 1.0 copy-start.1
  86.8 46.4 %all-to-all-start.2 = ((bf16[16,128,512]{2,1,0:T(8,128)(2,1)}), bf16[16,128,512]{2,1,0:T(8,128)(2,1)S(1)}, u32[]{:S(2)}, u32[]{:S(2)}) async-start(bf16[16,128,512]{2,1,0:T(8,128)(2,1)} %get-tuple-element.33), calls=%async_computation.2 | async-start | bytes 4194304 | tf_op jit(solution)/shard_map/all_to_all | solution.py:315
  95.2 8.7 %collective-permute-start.4 = (f32[8,128]{1,0:T(8,128)S(1)}, f32[8,128]{1,0:T(8,128)S(1)}, u32[]{:S(2)}, u32[]{:S(2)}) collective-permute-start(f32[8,128]{1,0:T(8,128)S(1)} %get-tuple-element.35), channel_id=1, source_target_pairs={{3,0},{2,1},{5,2},{4,3},{7,4},{6,5},{9,6},{8,7},{11,8},{10,9},{13,... | collective-permute-start | bytes 12296 | tf_op jit(solution)/shard_map/ppermute | solution.py:284
  99.4 20.8 %collective-permute-start.3 = (f32[8,128]{1,0:T(8,128)S(1)}, f32[8,128]{1,0:T(8,128)S(1)}, u32[]{:S(2)}, u32[]{:S(2)}) collective-permute-start(f32[8,128]{1,0:T(8,128)S(1)} %get-tuple-element.35), channel_id=1, source_target_pairs={{1,0},{0,1},{3,2},{2,3},{5,4},{4,5},{7,6},{6,7},{9,8},{8,9},{11,10... | collective-permute-start | bytes 12296 | tf_op jit(solution)/shard_map/ppermute | solution.py:276
  101.4 18.8 %collective-permute-start.2 = (f32[8,128]{1,0:T(8,128)S(1)}, f32[8,128]{1,0:T(8,128)S(1)}, u32[]{:S(2)}, u32[]{:S(2)}) collective-permute-start(f32[8,128]{1,0:T(8,128)S(1)} %get-tuple-element.35), channel_id=1, source_target_pairs={{2,0},{4,2},{6,4},{8,6},{10,8},{12,10},{14,12},{0,14},{3,1},{5,3},... | collective-permute-start | bytes 12296 | tf_op jit(solution)/shard_map/ppermute | solution.py:276
  120.3 11.9 %collective-permute-start.7 = (f32[8,128]{1,0:T(8,128)S(1)}, f32[8,128]{1,0:T(8,128)S(1)}, u32[]{:S(2)}, u32[]{:S(2)}) collective-permute-start(f32[8,128]{1,0:T(8,128)S(1)} %maximum_maximum_fusion.1), channel_id=1, source_target_pairs={{12,0},{14,2},{0,4},{2,6},{4,8},{6,10},{8,12},{10,14},{13,1},{15,3... | collective-permute-start | bytes 12296 | tf_op jit(solution)/shard_map/ppermute | solution.py:276
  124.3 8.3 %collective-permute-start.6 = (f32[8,128]{1,0:T(8,128)S(1)}, f32[8,128]{1,0:T(8,128)S(1)}, u32[]{:S(2)}, u32[]{:S(2)}) collective-permute-start(f32[8,128]{1,0:T(8,128)S(1)} %maximum_maximum_fusion.1), channel_id=1, source_target_pairs={{8,0},{10,2},{12,4},{14,6},{0,8},{2,10},{4,12},{6,14},{9,1},{11,3}... | collective-permute-start | bytes 12296 | tf_op jit(solution)/shard_map/ppermute | solution.py:276
  127.7 5.5 %collective-permute-start.5 = (f32[8,128]{1,0:T(8,128)S(1)}, f32[8,128]{1,0:T(8,128)S(1)}, u32[]{:S(2)}, u32[]{:S(2)}) collective-permute-start(f32[8,128]{1,0:T(8,128)S(1)} %maximum_maximum_fusion.1), channel_id=1, source_target_pairs={{4,0},{6,2},{8,4},{10,6},{12,8},{14,10},{0,12},{2,14},{5,1},{7,3},... | collective-permute-start | bytes 12296 | tf_op jit(solution)/shard_map/ppermute | solution.py:276
  153.1 7.3 %collective-permute-start.8 = (bf16[16,16,640]{2,1,0:T(8,128)(2,1)S(1)}, bf16[16,16,640]{2,1,0:T(8,128)(2,1)S(1)}, u32[]{:S(2)}, u32[]{:S(2)}) collective-permute-start(bf16[16,16,640]{2,1,0:T(8,128)(2,1)S(1)} %all_to_all.21.mine), channel_id=1, source_target_pairs={{16,0},{0,16},{17,1},{1,17},{18,2},{2,18},{19,3},{3,19},{20,4},{4,... | collective-permute-start | bytes 983048 | tf_op jit(solution)/shard_map/ppermute | solution.py:276

commit v6 on v5

--- a/solution.py
+++ b/solution.py
@@ -125,56 +125,96 @@
     return out, jnp.max(jnp.abs(out.astype(F32)).reshape(-1, 8, KW), axis=0)
 
 
-def own_kernel(got, weight, total, product, high):
+def own_kernel(got, total, mine, sem):
+    copy = pltpu.make_async_copy(got.at[:, pl.ds(COUNT, HALF), :], mine, sem)
+    copy.start()
     total[...] = gradients(got[:, 0:HALF, :], got[:, COUNT:PACK, :])
-    out, size = products(got[:, COUNT:PACK, :], weight[...])
-    product[...] = out.reshape(16, HALF, KW)
-    high[...] = size
-
-
-def own_half(got, weight):
+    copy.wait()
+
+
+def own_half(got):
     return call(
         own_kernel,
         "own_half",
-        [array((KW, KW), F32), array((16, HALF, KW)), array((8, KW), F32)],
-        [VMEM] * 2,
-        [VMEM] * 3,
-        2**30,
-        5 * 2**20,
-    )(got, weight)
-
-
-def other_kernel(got, other, weight, total, product, high_in, share, back, high, rest, sems):
+        [array((KW, KW), F32), pltpu.HBM((16, HALF, KW), BF16)],
+        [VMEM],
+        [VMEM, ANY],
+        2**29,
+        4 * 2**20,
+        scratch_shapes=[pltpu.SemaphoreType.DMA],
+    )(got)
+
+
+def other_kernel(got, other, total, share, kept, chunks, sems):
     core = lax.axis_index("core")
-    first = pltpu.make_async_copy(product, back.at[:, 0:HALF, :], sems.at[0])
-    first.start()
-    out, size = products(other[...], weight[...])
-    rest[...] = out.reshape(16, HALF, KW)
-    second = pltpu.make_async_copy(rest, back.at[:, HALF:COUNT, :], sems.at[1])
-    second.start()
-    high[...] = jnp.maximum(high_in[...], size)
+    keep = pltpu.make_async_copy(other, kept, sems.at[0])
+    keep.start()
     summed = (total[...] + gradients(got[:, HALF:COUNT, :], other[...])).astype(BF16)
     for m in range(4):
         for s in range(2):
             z = 2 * m + jnp.where(core == 0, s, 1 - s)
             for yh in range(4):
                 row = m * 128 + s * 64 + yh * 16
-                share[yh * 8 + z] = summed[row : row + 16, :]
-    first.wait()
-    second.wait()
-
-
-def other_half(got, other, weight, total, product, high):
+                chunks[yh * 8 + z] = summed[row : row + 16, :]
+    store = pltpu.make_async_copy(chunks, share, sems.at[1])
+    store.start()
+    keep.wait()
+    store.wait()
+
+
+def other_half(got, other, total):
     return call(
         other_kernel,
         "other_half",
-        [array((32, 16, KW)), pltpu.HBM((16, COUNT, KW), BF16), array((8, KW), F32)],
-        [VMEM] * 6,
-        [VMEM, ANY, VMEM],
+        [pltpu.HBM((32, 16, KW), BF16), pltpu.HBM((16, HALF, KW), BF16)],
+        [VMEM] * 3,
+        [ANY] * 2,
+        2**29,
+        4 * 2**20,
+        scratch_shapes=[pltpu.VMEM((32, 16, KW), BF16), pltpu.SemaphoreType.DMA((2,))],
+    )(got, other, total)
+
+
+def product_kernel(mine, other, weight, back, high, keys, scaled, rest, sems):
+    loads = [
+        pltpu.make_async_copy(weight, scaled, sems.at[0]),
+        pltpu.make_async_copy(mine, keys.at[0], sems.at[1]),
+        pltpu.make_async_copy(other, keys.at[1], sems.at[2]),
+    ]
+    for load in loads:
+        load.start()
+    loads[0].wait()
+    stores = []
+    sizes = []
+    for half in range(2):
+        loads[1 + half].wait()
+        out, size = products(keys[half], scaled[...])
+        sizes.append(size)
+        rest[half] = out.reshape(16, HALF, KW)
+        rows = pl.ds(half * HALF, HALF)
+        stores.append(pltpu.make_async_copy(rest.at[half], back.at[:, rows, :], sems.at[3 + half]))
+        stores[-1].start()
+    high[...] = jnp.maximum(sizes[0], sizes[1])
+    for store in stores:
+        store.wait()
+
+
+def product(mine, other, weight):
+    return call(
+        product_kernel,
+        "product",
+        [pltpu.HBM((16, COUNT, KW), BF16), array((8, KW), F32)],
+        [ANY] * 3,
+        [ANY, VMEM],
         2**30,
-        7 * 2**20,
-        scratch_shapes=[pltpu.VMEM((16, HALF, KW), BF16), pltpu.SemaphoreType.DMA((2,))],
-    )(got, other, weight, total, product, high)
+        5 * 2**20,
+        scratch_shapes=[
+            pltpu.VMEM((2, 16, HALF, KW), BF16),
+            pltpu.VMEM((KW, KW), BF16),
+            pltpu.VMEM((2, 16, HALF, KW), BF16),
+            pltpu.SemaphoreType.DMA((5,)),
+        ],
+    )(hbm(mine), hbm(other), hbm(weight))
 
 
 def reduce_kernel(factor, terms, high, piece, peaks):
@@ -246,46 +286,49 @@
     )(back)
 
 
-def merge_kernel(mine, other, out, peaks):
+def peaks_kernel(mine, other, out):
+    high = jnp.maximum(mine[:, :, KW:WIDE], other[:, :, KW:WIDE]).astype(F32)
+    high = jnp.max(high, axis=0)
+    out[...] = jnp.maximum(high[0:8], high[8:16])
+
+
+def peaks_of(mine, other):
+    return call(peaks_kernel, "peaks_of", array((8, 128), F32), [VMEM] * 2, VMEM, 2**15, 2**17)(mine, other)
+
+
+def last_kernel(a, b, out):
+    high = jnp.maximum(a[...], b[...])
+    low = lax.broadcasted_iota(jnp.int32, (8, 128), 1) < 64
+    out[0] = jnp.max(jnp.where(low, high, 0.0))
+    out[1] = jnp.max(jnp.where(low, 0.0, high))
+
+
+def last(a, b):
+    smem = pl.BlockSpec(memory_space=pltpu.SMEM)
+    return call(last_kernel, "last", array((2,), F32), [VMEM] * 2, smem, 2**12, 2**13)(a, b)
+
+
+def merge_kernel(mine, other, out):
     turn = lax.rem(lax.axis_index("core") + lax.axis_index("z"), 2)
     for source, s in ((mine, turn), (other, 1 - turn)):
         for yh in range(4):
             for t in range(4):
                 row = pl.multiple_of(t * 128 + s * 64 + yh * 16, 16)
                 out[pl.ds(row, 16), :] = source[yh * 4 + t, :, 0:KW].astype(F32)
-    high = jnp.maximum(mine[:, :, KW:WIDE], other[:, :, KW:WIDE]).astype(F32)
-    high = jnp.max(high, axis=0)
-    low = lax.broadcasted_iota(jnp.int32, (16, 128), 1) < 64
-    peaks[0] = jnp.max(jnp.where(low, high, 0.0))
-    peaks[1] = jnp.max(jnp.where(low, 0.0, high))
 
 
 def merge(mine, other):
-    return call(
-        merge_kernel,
-        "merge",
-        [array((512, KW), F32), array((2,), F32)],
-        [VMEM] * 2,
-        [VMEM, pl.BlockSpec(memory_space=pltpu.SMEM)],
-        0,
-        2 * 2**20,
-    )(mine, other)
+    return call(merge_kernel, "merge", array((512, KW), F32), [VMEM] * 2, VMEM, 0, 2 * 2**20)(mine, other)
 
 
 def from_ahead(x, axis, size, step):
     return lax.ppermute(x, axis, [((i + step) % size, i) for i in range(size)])
 
 
-def over_shards(peaks):
-    pairs = [(((z + 1) % 8) * 2 + 1 - xl, z * 2 + xl) for z in range(8) for xl in range(2)]
-    near = [
-        from_ahead(peaks, "z", 8, 1),
-        from_ahead(peaks, "xl", 2, 1),
-        lax.ppermute(peaks, ("z", "xl"), pairs),
-    ]
-    peaks = jnp.maximum(jnp.maximum(peaks, near[0]), jnp.maximum(near[1], near[2]))
-    far = [from_ahead(peaks, "z", 8, step) for step in (2, 4, 6)]
-    return jnp.maximum(jnp.maximum(peaks, far[0]), jnp.maximum(far[1], far[2]))
+def with_neighbours(peaks, step):
+    ahead = from_ahead(peaks, "z", 8, step)
+    behind = from_ahead(peaks, "z", 8, 8 - step)
+    return jnp.maximum(peaks, jnp.maximum(ahead, behind))
 
 
 def swap(x):
@@ -304,22 +347,25 @@
     weight = shift_weight(weight)
     got = lax.all_to_all(packed, GROUP, 0, 0, tiled=True)
     got, weight = lax.optimization_barrier((got, weight))
-    other = swap(got[:, COUNT:])
-    total, product, high = own_half(got, weight)
-    share, back, high = other_half(got, other, weight, total, product, high)
+    total, mine = own_half(got)
+    share, other = other_half(got, swap(got[:, COUNT:]), total)
+    back, high = product(mine, other, weight)
 
     terms = lax.all_to_all(share, SPREAD, 0, 0, tiled=True)
     piece, peaks = reduce_terms(factor, terms, high)
 
-    back, piece = lax.optimization_barrier((back, piece))
+    plane = lax.all_to_all(spread(piece, peaks), PLANE, 0, 0, tiled=True)
+
+    back, plane = lax.optimization_barrier((back, plane))
     back = lax.all_to_all(back, GROUP, 0, 0, tiled=True)
-    peaks = over_shards(peaks)
-    back, piece, peaks = lax.optimization_barrier((back, piece, peaks))
+    other = swap(plane)
+    peaks = with_neighbours(peaks_of(plane, other), 1)
+    weight_grad = merge(plane, other)
+    weight_grad, peaks = lax.optimization_barrier((weight_grad, peaks))
+    peaks = with_neighbours(peaks, 3)
     input_grad = unpack(back)
-
-    plane = lax.all_to_all(spread(piece, peaks), PLANE, 0, 0, tiled=True)
-    weight_grad, peaks = merge(plane, swap(plane))
-    return (input_grad, weight_grad, peaks)
+    input_grad, across = lax.optimization_barrier((input_grad, from_ahead(peaks, "xl", 2, 1)))
+    return (input_grad, weight_grad, last(peaks, across))
 
 
 def solution(mesh):

time: 162 us -> 145 us (0.90); the launches traced: 161 us -> 143 us
  blocking collectives: 46.5 us -> 21.5 us
  starting transfers between devices: 56 us -> 59.6 us
  Pallas kernels: 9.71 us -> 13.2 us
  local copies, waits for them, and re-layouts: 1.92 us -> 0.09 us
    all_to_all x1 -> x0, blocking collectives: 26.6 us -> none  [local(): terms = lax.all_to_all(share, SPREAD, 0, 0, tiled=True)]
    ppermute x7, waiting for transfers between devices: 17.4 us -> 4.76 us  [from_ahead(): return lax.ppermute(x, axis, [((i + step) % size, i) for i in range(size)])]
    all_to_all x0 -> x1, waiting for transfers between devices: none -> 11.8 us  [local(): terms = lax.all_to_all(share, SPREAD, 0, 0, tiled=True)]
    all_to_all x0 -> x1, starting transfers between devices: none -> 11.2 us  [local(): terms = lax.all_to_all(share, SPREAD, 0, 0, tiled=True)]
    ppermute x1 -> x0, starting transfers between devices: 4.19 us -> none  [over_shards(): lax.ppermute(peaks, ('z', 'xl'), pairs)]
    pallas_call x3 -> x6, Pallas kernels: 4.65 us -> 8.21 us  [the longest x1 3.88 us: product(): call(product_kernel, 'product', [pltpu.HBM((16, COUNT, KW), BF16), array(...]
    ppermute x7, starting transfers between devices: 26 us -> 23.9 us  [from_ahead(): return lax.ppermute(x, axis, [((i + step) % size, i) for i in range(size)])]
    unnamed x4 -> x0, local copies, waits for them, and re-layouts: 1.83 us -> none
  transfers between devices with their start and end apart: 11 -> 11, of which waited for: 5 -> 8; matrix products, arithmetic and copies ran while one was open for 0% -> 0% of each run, Pallas kernels for 2% -> 5%
where the time goes in v6:
time: 145 us; the launch traced here: 143 us
  starting transfers between devices  59.6 us (41%)
  waiting for transfers between devices  47.6 us (33%)
  blocking collectives  21.5 us (15%)
  Pallas kernels  13.2 us (9%)
    ppermute x7, starting transfers between devices, from_ahead(): return lax.ppermute(x, axis, [((i + step) % size, i) for i in range(size)])  23.9 us
    all_to_all x1, waiting for transfers between devices, local(): got = lax.all_to_all(packed, GROUP, 0, 0, tiled=True)  22.6 us
    all_to_all x1, blocking collectives, local(): plane = lax.all_to_all(spread(piece, peaks), PLANE, 0, 0, tiled=True)  21.5 us
    all_to_all x1, waiting for transfers between devices, local(): terms = lax.all_to_all(share, SPREAD, 0, 0, tiled=True)  11.8 us
    all_to_all x1, starting transfers between devices, local(): terms = lax.all_to_all(share, SPREAD, 0, 0, tiled=True)  11.2 us
    all_to_all x1, starting transfers between devices, local(): got = lax.all_to_all(packed, GROUP, 0, 0, tiled=True)  10.4 us
    ppermute x1, waiting for transfers between devices, shift_weight(): return lax.ppermute(weight, ('yl', 'xh', 'core', 'z'), pairs)  7.27 us
    all_to_all x1, starting transfers between devices, local(): back = lax.all_to_all(back, GROUP, 0, 0, tiled=True)  7.1 us
  transfers between devices with their start and end apart: 11, of which 8 were waited for; matrix products, arithmetic and copies ran while one was open for 0% of the time, Pallas kernels for 5%

profile of v6, /device:TPU:1, one launch (start us, length us, event | category | flops | bytes accessed | tf_op | source)
XLA Modules:
  0.0 142.7 jit_solution(1291853604565317110)
XLA Ops:
  0.6 3.2 %pack.1 = (bf16[16,192,512]{2,1,0:T(8,128)(2,1)}, bf16[512,512]{1,0:T(8,128)(2,1)}) custom-call(bf16[128,8192]{1,0:T(8,128)(2,1)} %tokens.1, bf16[128,512]{1,0:T(8,128)(2,1)} %keys.1, bf16[512,512]{1,0:T(8,128)(2,1)} %codes.1, f32[4]{0:T(128)} %scales.1), custom_call_target="tpu_custom_call" | custom-call | bytes 9437184 | tf_op jit(solution)/shard_map/pack/pallas_call | solution.py:95
  3.9 10.4 %all-to-all-start = ((bf16[16,192,512]{2,1,0:T(8,128)(2,1)}), bf16[16,192,512]{2,1,0:T(8,128)(2,1)S(1)}, u32[]{:S(2)}, u32[]{:S(2)}) async-start(bf16[16,192,512]{2,1,0:T(8,128)(2,1)} %get-tuple-element.21), calls=%async_computation | async-start | bytes 6291456 | tf_op jit(solution)/shard_map/all_to_all | solution.py:348
  14.3 7.0 %collective-permute-start = (bf16[512,512]{1,0:T(8,128)(2,1)}, bf16[512,512]{1,0:T(8,128)(2,1)}, u32[]{:S(2)}, u32[]{:S(2)}) collective-permute-start(bf16[512,512]{1,0:T(8,128)(2,1)} %get-tuple-element.22), channel_id=1, source_target_pairs={{0,0},{2,2},{4,4},{6,6},{8,8},{10,10},{12,12},{14,14},{24,16},{26,... | collective-permute-start | bytes 1572872 | tf_op jit(solution)/shard_map/ppermute | solution.py:340
  21.3 7.3 %collective-permute-done.weight = bf16[512,512]{1,0:T(8,128)(2,1)} collective-permute-done((bf16[512,512]{1,0:T(8,128)(2,1)}, bf16[512,512]{1,0:T(8,128)(2,1)}, u32[]{:S(2)}, u32[]{:S(2)}) %collective-permute-start) | collective-permute-done | bytes 524320 | tf_op jit(solution)/shard_map/ppermute | solution.py:340
  28.6 22.6 %all-to-all-done.got = bf16[16,192,512]{2,1,0:T(8,128)(2,1)S(1)} async-done(((bf16[16,192,512]{2,1,0:T(8,128)(2,1)}), bf16[16,192,512]{2,1,0:T(8,128)(2,1)S(1)}, u32[]{:S(2)}, u32[]{:S(2)}) %all-to-all-start) | async-done | bytes 3145760 | tf_op jit(solution)/shard_map/all_to_all | solution.py:348
  51.3 4.0 %collective-permute-start.1 = (bf16[16,64,512]{2,1,0:T(8,128)(2,1)S(1)}, bf16[16,64,512]{2,1,0:T(8,128)(2,1)S(1)}, u32[]{:S(2)}, u32[]{:S(2)}) collective-permute-start(bf16[16,64,512]{2,1,0:T(8,128)(2,1)S(1)} %slice.3), channel_id=1, source_target_pairs={{16,0},{0,16},{17,1},{1,17},{18,2},{2,18},{19,3},{3,19},{20,4},{4,... | collective-permute-start | bytes 3145736 | tf_op jit(solution)/shard_map/ppermute | solution.py:325
  56.3 1.3 collective-permute-done.1.other
  57.6 1.6 %other_half.1 = (bf16[32,16,512]{2,1,0:T(8,128)(2,1)}, bf16[16,64,512]{2,1,0:T(8,128)(2,1)}) custom-call(bf16[16,192,512]{2,1,0:T(8,128)(2,1)S(1)} %all-to-all-done.got, bf16[16,64,512]{2,1,0:T(8,128)(2,1)S(1)} %collective-permute-done.1.other, f32[512,512]{1,0:T(8,128)S(1)} %get-tuple-element.25.total), custom_call_target="tpu_custom_call" | custom-call | flops 536870912 | bytes 4194304 | tf_op jit(solution)/shard_map/other_half/pallas_call | solution.py:166
  59.2 11.2 %all-to-all-start.1 = ((bf16[32,16,512]{2,1,0:T(8,128)(2,1)}), bf16[32,16,512]{2,1,0:T(8,128)(2,1)S(1)}, u32[]{:S(2)}, u32[]{:S(2)}) async-start(bf16[32,16,512]{2,1,0:T(8,128)(2,1)} %get-tuple-element.29), calls=%async_computation.1 | async-start | bytes 1048576 | tf_op jit(solution)/shard_map/all_to_all | solution.py:354
  70.4 3.9 %product.1 = (bf16[16,128,512]{2,1,0:T(8,128)(2,1)}, f32[8,512]{1,0:T(8,128)S(1)}) custom-call(bf16[16,64,512]{2,1,0:T(8,128)(2,1)} %get-tuple-element.24.mine, bf16[16,64,512]{2,1,0:T(8,128)(2,1)} %get-tuple-element.26.other, bf16[512,512]{1,0:T(8,128)(2,1)} %collective-permute-done.weight), custom_call_target="tpu_custom_call" | custom-call | flops 1073741824 | bytes 5242880 | tf_op jit(solution)/shard_map/product/pallas_call | solution.py:203
  74.3 11.8 %all-to-all-done.1.refs_0_ = bf16[32,16,512]{2,1,0:T(8,128)(2,1)S(1)} async-done(((bf16[32,16,512]{2,1,0:T(8,128)(2,1)}), bf16[32,16,512]{2,1,0:T(8,128)(2,1)S(1)}, u32[]{:S(2)}, u32[]{:S(2)}) %all-to-all-start.1) | async-done | bytes 524320 | tf_op jit(solution)/shard_map/all_to_all | solution.py:354
  86.3 21.5 %all_to_all.20.mine = bf16[16,16,640]{2,1,0:T(8,128)(2,1)S(1)} all-to-all(bf16[16,16,640]{2,1,0:T(8,128)(2,1)S(1)} %spread.1), channel_id=1, replica_groups=mesh['yh'=4,'yl'=2,'xh'=2,'core'=2,'z'=8,'xl'=2] {'yh','yl','xh'}, dimensions={0} | all-to-all | bytes 655360 | tf_op jit(solution)/shard_map/all_to_all | solution.py:357
  107.7 7.1 %all-to-all-start.3 = ((bf16[16,128,512]{2,1,0:T(8,128)(2,1)}), bf16[16,128,512]{2,1,0:T(8,128)(2,1)S(1)}, u32[]{:S(2)}, u32[]{:S(2)}) async-start(bf16[16,128,512]{2,1,0:T(8,128)(2,1)} %get-tuple-element.33), calls=%async_computation.3 | async-start | bytes 4194304 | tf_op jit(solution)/shard_map/all_to_all | solution.py:360
  114.8 2.1 %collective-permute-start.2 = (bf16[16,16,640]{2,1,0:T(8,128)(2,1)S(1)}, bf16[16,16,640]{2,1,0:T(8,128)(2,1)S(1)}, u32[]{:S(2)}, u32[]{:S(2)}) collective-permute-start(bf16[16,16,640]{2,1,0:T(8,128)(2,1)S(1)} %all_to_all.20.mine), channel_id=1, source_target_pairs={{16,0},{0,16},{17,1},{1,17},{18,2},{2,18},{19,3},{3,19},{20,4},{4,... | collective-permute-start | bytes 983048 | tf_op jit(solution)/shard_map/ppermute | solution.py:325
  117.0 1.4 collective-permute-done.2.other
  118.4 3.3 %collective-permute-start.4 = (f32[8,128]{1,0:T(8,128)S(1)}, f32[8,128]{1,0:T(8,128)S(1)}, u32[]{:S(2)}, u32[]{:S(2)}) collective-permute-start(f32[8,128]{1,0:T(8,128)S(1)} %peaks_of.1), channel_id=1, source_target_pairs={{14,0},{0,2},{2,4},{4,6},{6,8},{8,10},{10,12},{12,14},{15,1},{1,3}... | collective-permute-start | bytes 12296 | tf_op jit(solution)/shard_map/ppermute | solution.py:325
  121.6 3.2 %collective-permute-start.3 = (f32[8,128]{1,0:T(8,128)S(1)}, f32[8,128]{1,0:T(8,128)S(1)}, u32[]{:S(2)}, u32[]{:S(2)}) collective-permute-start(f32[8,128]{1,0:T(8,128)S(1)} %peaks_of.1), channel_id=1, source_target_pairs={{2,0},{4,2},{6,4},{8,6},{10,8},{12,10},{14,12},{0,14},{3,1},{5,3},... | collective-permute-start | bytes 12296 | tf_op jit(solution)/shard_map/ppermute | solution.py:325
  124.9 1.1 merge.1
  126.3 3.9 %collective-permute-start.6 = (f32[8,128]{1,0:T(8,128)S(1)}, f32[8,128]{1,0:T(8,128)S(1)}, u32[]{:S(2)}, u32[]{:S(2)}) collective-permute-start(f32[8,128]{1,0:T(8,128)S(1)} %maximum_maximum_fusion.1), channel_id=1, source_target_pairs={{10,0},{12,2},{14,4},{0,6},{2,8},{4,10},{6,12},{8,14},{11,1},{13,3... | collective-permute-start | bytes 12296 | tf_op jit(solution)/shard_map/ppermute | solution.py:325
  130.2 4.4 %collective-permute-start.5 = (f32[8,128]{1,0:T(8,128)S(1)}, f32[8,128]{1,0:T(8,128)S(1)}, u32[]{:S(2)}, u32[]{:S(2)}) collective-permute-start(f32[8,128]{1,0:T(8,128)S(1)} %maximum_maximum_fusion.1), channel_id=1, source_target_pairs={{6,0},{8,2},{10,4},{12,6},{14,8},{0,10},{2,12},{4,14},{7,1},{9,3},... | collective-permute-start | bytes 12296 | tf_op jit(solution)/shard_map/ppermute | solution.py:325
  134.6 1.8 %collective-permute-done.5 = f32[8,128]{1,0:T(8,128)S(1)} collective-permute-done((f32[8,128]{1,0:T(8,128)S(1)}, f32[8,128]{1,0:T(8,128)S(1)}, u32[]{:S(2)}, u32[]{:S(2)}) %collective-permute-start.5) | collective-permute-done | bytes 4128 | tf_op jit(solution)/shard_map/ppermute | solution.py:325
  136.4 3.0 %collective-permute-start.7 = (f32[8,128]{1,0:T(8,128)S(1)}, f32[8,128]{1,0:T(8,128)S(1)}, u32[]{:S(2)}, u32[]{:S(2)}) collective-permute-start(f32[8,128]{1,0:T(8,128)S(1)} %maximum_maximum_fusion.a), channel_id=1, source_target_pairs={{1,0},{0,1},{3,2},{2,3},{5,4},{4,5},{7,6},{6,7},{9,8},{8,9},{11,10... | collective-permute-start | bytes 12296 | tf_op jit(solution)/shard_map/ppermute | solution.py:325
  139.4 1.2 all-to-all-done.3.back
  140.5 1.6 %unpack.1 = bf16[128,8192]{1,0:T(8,128)(2,1)} custom-call(bf16[16,128,512]{2,1,0:T(8,128)(2,1)S(1)} %all-to-all-done.3.back), custom_call_target="tpu_custom_call" | custom-call | bytes 4194304 | tf_op jit(solution)/shard_map/unpack/pallas_call | solution.py:277
  (12 shorter events, 2.3 us)
Async XLA Ops:
  3.9 47.3 %all-to-all-start = ((bf16[16,192,512]{2,1,0:T(8,128)(2,1)}), bf16[16,192,512]{2,1,0:T(8,128)(2,1)S(1)}, u32[]{:S(2)}, u32[]{:S(2)}) async-start(bf16[16,192,512]{2,1,0:T(8,128)(2,1)} %get-tuple-element.21), calls=%async_computation | async-start | bytes 6291456 | tf_op jit(solution)/shard_map/all_to_all | solution.py:348
  14.3 14.3 %collective-permute-start = (bf16[512,512]{1,0:T(8,128)(2,1)}, bf16[512,512]{1,0:T(8,128)(2,1)}, u32[]{:S(2)}, u32[]{:S(2)}) collective-permute-start(bf16[512,512]{1,0:T(8,128)(2,1)} %get-tuple-element.22), channel_id=1, source_target_pairs={{0,0},{2,2},{4,4},{6,6},{8,8},{10,10},{12,12},{14,14},{24,16},{26,... | collective-permute-start | bytes 1572872 | tf_op jit(solution)/shard_map/ppermute | solution.py:340
  51.3 6.3 %collective-permute-start.1 = (bf16[16,64,512]{2,1,0:T(8,128)(2,1)S(1)}, bf16[16,64,512]{2,1,0:T(8,128)(2,1)S(1)}, u32[]{:S(2)}, u32[]{:S(2)}) collective-permute-start(bf16[16,64,512]{2,1,0:T(8,128)(2,1)S(1)} %slice.3), channel_id=1, source_target_pairs={{16,0},{0,16},{17,1},{1,17},{18,2},{2,18},{19,3},{3,19},{20,4},{4,... | collective-permute-start | bytes 3145736 | tf_op jit(solution)/shard_map/ppermute | solution.py:325
  59.2 26.8 %all-to-all-start.1 = ((bf16[32,16,512]{2,1,0:T(8,128)(2,1)}), bf16[32,16,512]{2,1,0:T(8,128)(2,1)S(1)}, u32[]{:S(2)}, u32[]{:S(2)}) async-start(bf16[32,16,512]{2,1,0:T(8,128)(2,1)} %get-tuple-element.29), calls=%async_computation.1 | async-start | bytes 1048576 | tf_op jit(solution)/shard_map/all_to_all | solution.py:354
  107.7 32.8 %all-to-all-start.3 = ((bf16[16,128,512]{2,1,0:T(8,128)(2,1)}), bf16[16,128,512]{2,1,0:T(8,128)(2,1)S(1)}, u32[]{:S(2)}, u32[]{:S(2)}) async-start(bf16[16,128,512]{2,1,0:T(8,128)(2,1)} %get-tuple-element.33), calls=%async_computation.3 | async-start | bytes 4194304 | tf_op jit(solution)/shard_map/all_to_all | solution.py:360
  114.8 3.5 %collective-permute-start.2 = (bf16[16,16,640]{2,1,0:T(8,128)(2,1)S(1)}, bf16[16,16,640]{2,1,0:T(8,128)(2,1)S(1)}, u32[]{:S(2)}, u32[]{:S(2)}) collective-permute-start(bf16[16,16,640]{2,1,0:T(8,128)(2,1)S(1)} %all_to_all.20.mine), channel_id=1, source_target_pairs={{16,0},{0,16},{17,1},{1,17},{18,2},{2,18},{19,3},{3,19},{20,4},{4,... | collective-permute-start | bytes 983048 | tf_op jit(solution)/shard_map/ppermute | solution.py:325
  118.4 7.6 %collective-permute-start.4 = (f32[8,128]{1,0:T(8,128)S(1)}, f32[8,128]{1,0:T(8,128)S(1)}, u32[]{:S(2)}, u32[]{:S(2)}) collective-permute-start(f32[8,128]{1,0:T(8,128)S(1)} %peaks_of.1), channel_id=1, source_target_pairs={{14,0},{0,2},{2,4},{4,6},{6,8},{8,10},{10,12},{12,14},{15,1},{1,3}... | collective-permute-start | bytes 12296 | tf_op jit(solution)/shard_map/ppermute | solution.py:325
  121.6 4.6 %collective-permute-start.3 = (f32[8,128]{1,0:T(8,128)S(1)}, f32[8,128]{1,0:T(8,128)S(1)}, u32[]{:S(2)}, u32[]{:S(2)}) collective-permute-start(f32[8,128]{1,0:T(8,128)S(1)} %peaks_of.1), channel_id=1, source_target_pairs={{2,0},{4,2},{6,4},{8,6},{10,8},{12,10},{14,12},{0,14},{3,1},{5,3},... | collective-permute-start | bytes 12296 | tf_op jit(solution)/shard_map/ppermute | solution.py:325
  126.3 8.3 %collective-permute-start.6 = (f32[8,128]{1,0:T(8,128)S(1)}, f32[8,128]{1,0:T(8,128)S(1)}, u32[]{:S(2)}, u32[]{:S(2)}) collective-permute-start(f32[8,128]{1,0:T(8,128)S(1)} %maximum_maximum_fusion.1), channel_id=1, source_target_pairs={{10,0},{12,2},{14,4},{0,6},{2,8},{4,10},{6,12},{8,14},{11,1},{13,3... | collective-permute-start | bytes 12296 | tf_op jit(solution)/shard_map/ppermute | solution.py:325
  130.2 6.2 %collective-permute-start.5 = (f32[8,128]{1,0:T(8,128)S(1)}, f32[8,128]{1,0:T(8,128)S(1)}, u32[]{:S(2)}, u32[]{:S(2)}) collective-permute-start(f32[8,128]{1,0:T(8,128)S(1)} %maximum_maximum_fusion.1), channel_id=1, source_target_pairs={{6,0},{8,2},{10,4},{12,6},{14,8},{0,10},{2,12},{4,14},{7,1},{9,3},... | collective-permute-start | bytes 12296 | tf_op jit(solution)/shard_map/ppermute | solution.py:325
  136.4 5.7 %collective-permute-start.7 = (f32[8,128]{1,0:T(8,128)S(1)}, f32[8,128]{1,0:T(8,128)S(1)}, u32[]{:S(2)}, u32[]{:S(2)}) collective-permute-start(f32[8,128]{1,0:T(8,128)S(1)} %maximum_maximum_fusion.a), channel_id=1, source_target_pairs={{1,0},{0,1},{3,2},{2,3},{5,4},{4,5},{7,6},{6,7},{9,8},{8,9},{11,10... | collective-permute-start | bytes 12296 | tf_op jit(solution)/shard_map/ppermute | solution.py:325

commit v7 on v6

--- a/solution.py
+++ b/solution.py
@@ -13,7 +13,7 @@
 SIZES = (4, 2, 2, 2, 8, 2)
 GROUP = ("yl", "xh", "core", "xl")
 SPREAD = ("yh", "z")
-PLANE = ("yh", "yl", "xh")
+PLANE = ("xh", "yh", "yl")
 SHIFT = (0, 4, 1, 7, 2, 6, 3, 5)
 BF16 = jnp.bfloat16
 F32 = jnp.float32
@@ -314,7 +314,7 @@
         for yh in range(4):
             for t in range(4):
                 row = pl.multiple_of(t * 128 + s * 64 + yh * 16, 16)
-                out[pl.ds(row, 16), :] = source[yh * 4 + t, :, 0:KW].astype(F32)
+                out[pl.ds(row, 16), :] = source[t % 2 * 8 + yh * 2 + t // 2, :, 0:KW].astype(F32)
 
 
 def merge(mine, other):

time: 145 us -> 144 us (level)
  blocking collectives: 21.5 us -> 19.4 us
    all_to_all x1, blocking collectives: 21.5 us -> 19.4 us  [local(): plane = lax.all_to_all(spread(piece, peaks), PLANE, 0, 0, tiled=True)]
where the time goes in v7:
time: 144 us; the launch traced here: 142 us
  starting transfers between devices  60.3 us (42%)
  waiting for transfers between devices  47.7 us (33%)
  blocking collectives  19.4 us (13%)
  Pallas kernels  13.2 us (9%)
    ppermute x7, starting transfers between devices, from_ahead(): return lax.ppermute(x, axis, [((i + step) % size, i) for i in range(size)])  23.8 us
    all_to_all x1, waiting for transfers between devices, local(): got = lax.all_to_all(packed, GROUP, 0, 0, tiled=True)  22.6 us
    all_to_all x1, blocking collectives, local(): plane = lax.all_to_all(spread(piece, peaks), PLANE, 0, 0, tiled=True)  19.4 us
    all_to_all x1, waiting for transfers between devices, local(): terms = lax.all_to_all(share, SPREAD, 0, 0, tiled=True)  11.8 us
    all_to_all x1, starting transfers between devices, local(): terms = lax.all_to_all(share, SPREAD, 0, 0, tiled=True)  11.2 us
    all_to_all x1, starting transfers between devices, local(): got = lax.all_to_all(packed, GROUP, 0, 0, tiled=True)  10.4 us
    all_to_all x1, starting transfers between devices, local(): back = lax.all_to_all(back, GROUP, 0, 0, tiled=True)  7.94 us
    ppermute x1, waiting for transfers between devices, shift_weight(): return lax.ppermute(weight, ('yl', 'xh', 'core', 'z'), pairs)  7.27 us
  transfers between devices with their start and end apart: 11, of which 8 were waited for; matrix products, arithmetic and copies ran while one was open for 0% of the time, Pallas kernels for 5%

profile of v7, /device:TPU:1, one launch (start us, length us, event | category | flops | bytes accessed | tf_op | source)
XLA Modules:
  0.0 141.6 jit_solution(1306336196311991588)
XLA Ops:
  0.6 3.2 %pack.1 = (bf16[16,192,512]{2,1,0:T(8,128)(2,1)}, bf16[512,512]{1,0:T(8,128)(2,1)}) custom-call(bf16[128,8192]{1,0:T(8,128)(2,1)} %tokens.1, bf16[128,512]{1,0:T(8,128)(2,1)} %keys.1, bf16[512,512]{1,0:T(8,128)(2,1)} %codes.1, f32[4]{0:T(128)} %scales.1), custom_call_target="tpu_custom_call" | custom-call | bytes 9437184 | tf_op jit(solution)/shard_map/pack/pallas_call | solution.py:95
  3.9 10.4 %all-to-all-start = ((bf16[16,192,512]{2,1,0:T(8,128)(2,1)}), bf16[16,192,512]{2,1,0:T(8,128)(2,1)S(1)}, u32[]{:S(2)}, u32[]{:S(2)}) async-start(bf16[16,192,512]{2,1,0:T(8,128)(2,1)} %get-tuple-element.21), calls=%async_computation | async-start | bytes 6291456 | tf_op jit(solution)/shard_map/all_to_all | solution.py:348
  14.3 7.0 %collective-permute-start = (bf16[512,512]{1,0:T(8,128)(2,1)}, bf16[512,512]{1,0:T(8,128)(2,1)}, u32[]{:S(2)}, u32[]{:S(2)}) collective-permute-start(bf16[512,512]{1,0:T(8,128)(2,1)} %get-tuple-element.22), channel_id=1, source_target_pairs={{0,0},{2,2},{4,4},{6,6},{8,8},{10,10},{12,12},{14,14},{24,16},{26,... | collective-permute-start | bytes 1572872 | tf_op jit(solution)/shard_map/ppermute | solution.py:340
  21.3 7.3 %collective-permute-done.weight = bf16[512,512]{1,0:T(8,128)(2,1)} collective-permute-done((bf16[512,512]{1,0:T(8,128)(2,1)}, bf16[512,512]{1,0:T(8,128)(2,1)}, u32[]{:S(2)}, u32[]{:S(2)}) %collective-permute-start) | collective-permute-done | bytes 524320 | tf_op jit(solution)/shard_map/ppermute | solution.py:340
  28.6 22.6 %all-to-all-done.got = bf16[16,192,512]{2,1,0:T(8,128)(2,1)S(1)} async-done(((bf16[16,192,512]{2,1,0:T(8,128)(2,1)}), bf16[16,192,512]{2,1,0:T(8,128)(2,1)S(1)}, u32[]{:S(2)}, u32[]{:S(2)}) %all-to-all-start) | async-done | bytes 3145760 | tf_op jit(solution)/shard_map/all_to_all | solution.py:348
  51.3 4.0 %collective-permute-start.1 = (bf16[16,64,512]{2,1,0:T(8,128)(2,1)S(1)}, bf16[16,64,512]{2,1,0:T(8,128)(2,1)S(1)}, u32[]{:S(2)}, u32[]{:S(2)}) collective-permute-start(bf16[16,64,512]{2,1,0:T(8,128)(2,1)S(1)} %slice.3), channel_id=1, source_target_pairs={{16,0},{0,16},{17,1},{1,17},{18,2},{2,18},{19,3},{3,19},{20,4},{4,... | collective-permute-start | bytes 3145736 | tf_op jit(solution)/shard_map/ppermute | solution.py:325
  56.3 1.3 collective-permute-done.1.other
  57.6 1.6 %other_half.1 = (bf16[32,16,512]{2,1,0:T(8,128)(2,1)}, bf16[16,64,512]{2,1,0:T(8,128)(2,1)}) custom-call(bf16[16,192,512]{2,1,0:T(8,128)(2,1)S(1)} %all-to-all-done.got, bf16[16,64,512]{2,1,0:T(8,128)(2,1)S(1)} %collective-permute-done.1.other, f32[512,512]{1,0:T(8,128)S(1)} %get-tuple-element.25.total), custom_call_target="tpu_custom_call" | custom-call | flops 536870912 | bytes 4194304 | tf_op jit(solution)/shard_map/other_half/pallas_call | solution.py:166
  59.2 11.2 %all-to-all-start.1 = ((bf16[32,16,512]{2,1,0:T(8,128)(2,1)}), bf16[32,16,512]{2,1,0:T(8,128)(2,1)S(1)}, u32[]{:S(2)}, u32[]{:S(2)}) async-start(bf16[32,16,512]{2,1,0:T(8,128)(2,1)} %get-tuple-element.29), calls=%async_computation.1 | async-start | bytes 1048576 | tf_op jit(solution)/shard_map/all_to_all | solution.py:354
  70.4 3.9 %product.1 = (bf16[16,128,512]{2,1,0:T(8,128)(2,1)}, f32[8,512]{1,0:T(8,128)S(1)}) custom-call(bf16[16,64,512]{2,1,0:T(8,128)(2,1)} %get-tuple-element.24.mine, bf16[16,64,512]{2,1,0:T(8,128)(2,1)} %get-tuple-element.26.other, bf16[512,512]{1,0:T(8,128)(2,1)} %collective-permute-done.weight), custom_call_target="tpu_custom_call" | custom-call | flops 1073741824 | bytes 5242880 | tf_op jit(solution)/shard_map/product/pallas_call | solution.py:203
  74.3 11.8 %all-to-all-done.1.refs_0_ = bf16[32,16,512]{2,1,0:T(8,128)(2,1)S(1)} async-done(((bf16[32,16,512]{2,1,0:T(8,128)(2,1)}), bf16[32,16,512]{2,1,0:T(8,128)(2,1)S(1)}, u32[]{:S(2)}, u32[]{:S(2)}) %all-to-all-start.1) | async-done | bytes 524320 | tf_op jit(solution)/shard_map/all_to_all | solution.py:354
  86.3 19.4 %all_to_all.20.mine = bf16[16,16,640]{2,1,0:T(8,128)(2,1)S(1)} all-to-all(bf16[16,16,640]{2,1,0:T(8,128)(2,1)S(1)} %spread.1), channel_id=1, replica_groups=mesh['yh'=4,'yl'=2,'xh'=2,'core'=2,'z'=8,'xl'=2] {'xh','yh','yl'}, dimensions={0} | all-to-all | bytes 655360 | tf_op jit(solution)/shard_map/all_to_all | solution.py:357
  105.7 7.9 %all-to-all-start.3 = ((bf16[16,128,512]{2,1,0:T(8,128)(2,1)}), bf16[16,128,512]{2,1,0:T(8,128)(2,1)S(1)}, u32[]{:S(2)}, u32[]{:S(2)}) async-start(bf16[16,128,512]{2,1,0:T(8,128)(2,1)} %get-tuple-element.33), calls=%async_computation.3 | async-start | bytes 4194304 | tf_op jit(solution)/shard_map/all_to_all | solution.py:360
  113.6 2.0 %collective-permute-start.2 = (bf16[16,16,640]{2,1,0:T(8,128)(2,1)S(1)}, bf16[16,16,640]{2,1,0:T(8,128)(2,1)S(1)}, u32[]{:S(2)}, u32[]{:S(2)}) collective-permute-start(bf16[16,16,640]{2,1,0:T(8,128)(2,1)S(1)} %all_to_all.20.mine), channel_id=1, source_target_pairs={{16,0},{0,16},{17,1},{1,17},{18,2},{2,18},{19,3},{3,19},{20,4},{4,... | collective-permute-start | bytes 983048 | tf_op jit(solution)/shard_map/ppermute | solution.py:325
  115.7 1.5 %collective-permute-done.2.other = bf16[16,16,640]{2,1,0:T(8,128)(2,1)S(1)} collective-permute-done((bf16[16,16,640]{2,1,0:T(8,128)(2,1)S(1)}, bf16[16,16,640]{2,1,0:T(8,128)(2,1)S(1)}, u32[]{:S(2)}, u32[]{:S(2)}) %collective-permute-start.2) | collective-permute-done | bytes 327712 | tf_op jit(solution)/shard_map/ppermute | solution.py:325
  117.2 3.0 %collective-permute-start.4 = (f32[8,128]{1,0:T(8,128)S(1)}, f32[8,128]{1,0:T(8,128)S(1)}, u32[]{:S(2)}, u32[]{:S(2)}) collective-permute-start(f32[8,128]{1,0:T(8,128)S(1)} %peaks_of.1), channel_id=1, source_target_pairs={{14,0},{0,2},{2,4},{4,6},{6,8},{8,10},{10,12},{12,14},{15,1},{1,3}... | collective-permute-start | bytes 12296 | tf_op jit(solution)/shard_map/ppermute | solution.py:325
  120.2 3.5 %collective-permute-start.3 = (f32[8,128]{1,0:T(8,128)S(1)}, f32[8,128]{1,0:T(8,128)S(1)}, u32[]{:S(2)}, u32[]{:S(2)}) collective-permute-start(f32[8,128]{1,0:T(8,128)S(1)} %peaks_of.1), channel_id=1, source_target_pairs={{2,0},{4,2},{6,4},{8,6},{10,8},{12,10},{14,12},{0,14},{3,1},{5,3},... | collective-permute-start | bytes 12296 | tf_op jit(solution)/shard_map/ppermute | solution.py:325
  123.7 1.1 merge.1
  124.8 4.1 %collective-permute-start.6 = (f32[8,128]{1,0:T(8,128)S(1)}, f32[8,128]{1,0:T(8,128)S(1)}, u32[]{:S(2)}, u32[]{:S(2)}) collective-permute-start(f32[8,128]{1,0:T(8,128)S(1)} %maximum_maximum_fusion.1), channel_id=1, source_target_pairs={{10,0},{12,2},{14,4},{0,6},{2,8},{4,10},{6,12},{8,14},{11,1},{13,3... | collective-permute-start | bytes 12296 | tf_op jit(solution)/shard_map/ppermute | solution.py:325
  128.9 4.2 %collective-permute-start.5 = (f32[8,128]{1,0:T(8,128)S(1)}, f32[8,128]{1,0:T(8,128)S(1)}, u32[]{:S(2)}, u32[]{:S(2)}) collective-permute-start(f32[8,128]{1,0:T(8,128)S(1)} %maximum_maximum_fusion.1), channel_id=1, source_target_pairs={{6,0},{8,2},{10,4},{12,6},{14,8},{0,10},{2,12},{4,14},{7,1},{9,3},... | collective-permute-start | bytes 12296 | tf_op jit(solution)/shard_map/ppermute | solution.py:325
  133.1 1.9 %collective-permute-done.5 = f32[8,128]{1,0:T(8,128)S(1)} collective-permute-done((f32[8,128]{1,0:T(8,128)S(1)}, f32[8,128]{1,0:T(8,128)S(1)}, u32[]{:S(2)}, u32[]{:S(2)}) %collective-permute-start.5) | collective-permute-done | bytes 4128 | tf_op jit(solution)/shard_map/ppermute | solution.py:325
  135.1 3.0 %collective-permute-start.7 = (f32[8,128]{1,0:T(8,128)S(1)}, f32[8,128]{1,0:T(8,128)S(1)}, u32[]{:S(2)}, u32[]{:S(2)}) collective-permute-start(f32[8,128]{1,0:T(8,128)S(1)} %maximum_maximum_fusion.a), channel_id=1, source_target_pairs={{1,0},{0,1},{3,2},{2,3},{5,4},{4,5},{7,6},{6,7},{9,8},{8,9},{11,10... | collective-permute-start | bytes 12296 | tf_op jit(solution)/shard_map/ppermute | solution.py:325
  138.0 1.3 all-to-all-done.3.back
  139.3 1.6 %unpack.1 = bf16[128,8192]{1,0:T(8,128)(2,1)} custom-call(bf16[16,128,512]{2,1,0:T(8,128)(2,1)S(1)} %all-to-all-done.3.back), custom_call_target="tpu_custom_call" | custom-call | bytes 4194304 | tf_op jit(solution)/shard_map/unpack/pallas_call | solution.py:277
  (12 shorter events, 2.1 us)
Async XLA Ops:
  3.9 47.3 %all-to-all-start = ((bf16[16,192,512]{2,1,0:T(8,128)(2,1)}), bf16[16,192,512]{2,1,0:T(8,128)(2,1)S(1)}, u32[]{:S(2)}, u32[]{:S(2)}) async-start(bf16[16,192,512]{2,1,0:T(8,128)(2,1)} %get-tuple-element.21), calls=%async_computation | async-start | bytes 6291456 | tf_op jit(solution)/shard_map/all_to_all | solution.py:348
  14.3 14.3 %collective-permute-start = (bf16[512,512]{1,0:T(8,128)(2,1)}, bf16[512,512]{1,0:T(8,128)(2,1)}, u32[]{:S(2)}, u32[]{:S(2)}) collective-permute-start(bf16[512,512]{1,0:T(8,128)(2,1)} %get-tuple-element.22), channel_id=1, source_target_pairs={{0,0},{2,2},{4,4},{6,6},{8,8},{10,10},{12,12},{14,14},{24,16},{26,... | collective-permute-start | bytes 1572872 | tf_op jit(solution)/shard_map/ppermute | solution.py:340
  51.3 6.3 %collective-permute-start.1 = (bf16[16,64,512]{2,1,0:T(8,128)(2,1)S(1)}, bf16[16,64,512]{2,1,0:T(8,128)(2,1)S(1)}, u32[]{:S(2)}, u32[]{:S(2)}) collective-permute-start(bf16[16,64,512]{2,1,0:T(8,128)(2,1)S(1)} %slice.3), channel_id=1, source_target_pairs={{16,0},{0,16},{17,1},{1,17},{18,2},{2,18},{19,3},{3,19},{20,4},{4,... | collective-permute-start | bytes 3145736 | tf_op jit(solution)/shard_map/ppermute | solution.py:325
  59.2 26.8 %all-to-all-start.1 = ((bf16[32,16,512]{2,1,0:T(8,128)(2,1)}), bf16[32,16,512]{2,1,0:T(8,128)(2,1)S(1)}, u32[]{:S(2)}, u32[]{:S(2)}) async-start(bf16[32,16,512]{2,1,0:T(8,128)(2,1)} %get-tuple-element.29), calls=%async_computation.1 | async-start | bytes 1048576 | tf_op jit(solution)/shard_map/all_to_all | solution.py:354
  105.7 33.6 %all-to-all-start.3 = ((bf16[16,128,512]{2,1,0:T(8,128)(2,1)}), bf16[16,128,512]{2,1,0:T(8,128)(2,1)S(1)}, u32[]{:S(2)}, u32[]{:S(2)}) async-start(bf16[16,128,512]{2,1,0:T(8,128)(2,1)} %get-tuple-element.33), calls=%async_computation.3 | async-start | bytes 4194304 | tf_op jit(solution)/shard_map/all_to_all | solution.py:360
  113.6 3.5 %collective-permute-start.2 = (bf16[16,16,640]{2,1,0:T(8,128)(2,1)S(1)}, bf16[16,16,640]{2,1,0:T(8,128)(2,1)S(1)}, u32[]{:S(2)}, u32[]{:S(2)}) collective-permute-start(bf16[16,16,640]{2,1,0:T(8,128)(2,1)S(1)} %all_to_all.20.mine), channel_id=1, source_target_pairs={{16,0},{0,16},{17,1},{1,17},{18,2},{2,18},{19,3},{3,19},{20,4},{4,... | collective-permute-start | bytes 983048 | tf_op jit(solution)/shard_map/ppermute | solution.py:325
  117.2 7.6 %collective-permute-start.4 = (f32[8,128]{1,0:T(8,128)S(1)}, f32[8,128]{1,0:T(8,128)S(1)}, u32[]{:S(2)}, u32[]{:S(2)}) collective-permute-start(f32[8,128]{1,0:T(8,128)S(1)} %peaks_of.1), channel_id=1, source_target_pairs={{14,0},{0,2},{2,4},{4,6},{6,8},{8,10},{10,12},{12,14},{15,1},{1,3}... | collective-permute-start | bytes 12296 | tf_op jit(solution)/shard_map/ppermute | solution.py:325
  120.2 4.6 %collective-permute-start.3 = (f32[8,128]{1,0:T(8,128)S(1)}, f32[8,128]{1,0:T(8,128)S(1)}, u32[]{:S(2)}, u32[]{:S(2)}) collective-permute-start(f32[8,128]{1,0:T(8,128)S(1)} %peaks_of.1), channel_id=1, source_target_pairs={{2,0},{4,2},{6,4},{8,6},{10,8},{12,10},{14,12},{0,14},{3,1},{5,3},... | collective-permute-start | bytes 12296 | tf_op jit(solution)/shard_map/ppermute | solution.py:325
  124.8 8.3 %collective-permute-start.6 = (f32[8,128]{1,0:T(8,128)S(1)}, f32[8,128]{1,0:T(8,128)S(1)}, u32[]{:S(2)}, u32[]{:S(2)}) collective-permute-start(f32[8,128]{1,0:T(8,128)S(1)} %maximum_maximum_fusion.1), channel_id=1, source_target_pairs={{10,0},{12,2},{14,4},{0,6},{2,8},{4,10},{6,12},{8,14},{11,1},{13,3... | collective-permute-start | bytes 12296 | tf_op jit(solution)/shard_map/ppermute | solution.py:325
  128.9 6.2 %collective-permute-start.5 = (f32[8,128]{1,0:T(8,128)S(1)}, f32[8,128]{1,0:T(8,128)S(1)}, u32[]{:S(2)}, u32[]{:S(2)}) collective-permute-start(f32[8,128]{1,0:T(8,128)S(1)} %maximum_maximum_fusion.1), channel_id=1, source_target_pairs={{6,0},{8,2},{10,4},{12,6},{14,8},{0,10},{2,12},{4,14},{7,1},{9,3},... | collective-permute-start | bytes 12296 | tf_op jit(solution)/shard_map/ppermute | solution.py:325
  135.1 5.9 %collective-permute-start.7 = (f32[8,128]{1,0:T(8,128)S(1)}, f32[8,128]{1,0:T(8,128)S(1)}, u32[]{:S(2)}, u32[]{:S(2)}) collective-permute-start(f32[8,128]{1,0:T(8,128)S(1)} %maximum_maximum_fusion.a), channel_id=1, source_target_pairs={{1,0},{0,1},{3,2},{2,3},{5,4},{4,5},{7,6},{6,7},{9,8},{8,9},{11,10... | collective-permute-start | bytes 12296 | tf_op jit(solution)/shard_map/ppermute | solution.py:325

commit v8 on v7

--- a/solution.py
+++ b/solution.py
@@ -80,7 +80,7 @@
                     for core in range(2):
                         first, second = (even, odd) if core == 0 else (odd, even)
                         at = HALF * (half ^ core)
-                        ready[t * 4 + core * 2 + e, at : at + HALF, lanes] = jnp.where(low, first, second)
+                        ready[t * 4 + half * 2 + e, at : at + HALF, lanes] = jnp.where(low, first, second)
         stores.append(pltpu.make_async_copy(ready.at[:, :, lanes], out.at[:, :, lanes], sems.at[11 + m]))
         stores[-1].start()
     for store in stores:
@@ -125,17 +125,25 @@
     return out, jnp.max(jnp.abs(out.astype(F32)).reshape(-1, 8, KW), axis=0)
 
 
-def own_kernel(got, total, mine, sem):
+def away_kernel(got, out):
+    out[...] = gradients(got[:, HALF:COUNT, :], got[:, COUNT:PACK, :]).astype(BF16)
+
+
+def away(got):
+    return call(away_kernel, "away", array((KW, KW)), [VMEM], VMEM, 2**29, 3 * 2**20)(got)
+
+
+def home_kernel(got, total, mine, sem):
     copy = pltpu.make_async_copy(got.at[:, pl.ds(COUNT, HALF), :], mine, sem)
     copy.start()
     total[...] = gradients(got[:, 0:HALF, :], got[:, COUNT:PACK, :])
     copy.wait()
 
 
-def own_half(got):
-    return call(
-        own_kernel,
-        "own_half",
+def home(got):
+    return call(
+        home_kernel,
+        "home",
         [array((KW, KW), F32), pltpu.HBM((16, HALF, KW), BF16)],
         [VMEM],
         [VMEM, ANY],
@@ -145,61 +153,58 @@
     )(got)
 
 
-def other_kernel(got, other, total, share, kept, chunks, sems):
+def join_kernel(total, other, share, chunks, sem):
     core = lax.axis_index("core")
-    keep = pltpu.make_async_copy(other, kept, sems.at[0])
-    keep.start()
-    summed = (total[...] + gradients(got[:, HALF:COUNT, :], other[...])).astype(BF16)
+    summed = (total[...] + other[...].astype(F32)).astype(BF16)
     for m in range(4):
         for s in range(2):
             z = 2 * m + jnp.where(core == 0, s, 1 - s)
             for yh in range(4):
                 row = m * 128 + s * 64 + yh * 16
                 chunks[yh * 8 + z] = summed[row : row + 16, :]
-    store = pltpu.make_async_copy(chunks, share, sems.at[1])
+    store = pltpu.make_async_copy(chunks, share, sem)
     store.start()
-    keep.wait()
     store.wait()
 
 
-def other_half(got, other, total):
-    return call(
-        other_kernel,
-        "other_half",
-        [pltpu.HBM((32, 16, KW), BF16), pltpu.HBM((16, HALF, KW), BF16)],
-        [VMEM] * 3,
-        [ANY] * 2,
-        2**29,
-        4 * 2**20,
-        scratch_shapes=[pltpu.VMEM((32, 16, KW), BF16), pltpu.SemaphoreType.DMA((2,))],
-    )(got, other, total)
-
-
-def product_kernel(mine, other, weight, back, high, keys, scaled, rest, sems):
+def join(total, other):
+    return call(
+        join_kernel,
+        "join",
+        pltpu.HBM((32, 16, KW), BF16),
+        [VMEM] * 2,
+        ANY,
+        2**18,
+        2**21,
+        scratch_shapes=[pltpu.VMEM((32, 16, KW), BF16), pltpu.SemaphoreType.DMA],
+    )(total, other)
+
+
+def product_kernel(mine, weight, across, back, high, keys, scaled, rest, sems):
     loads = [
-        pltpu.make_async_copy(weight, scaled, sems.at[0]),
-        pltpu.make_async_copy(mine, keys.at[0], sems.at[1]),
-        pltpu.make_async_copy(other, keys.at[1], sems.at[2]),
+        pltpu.make_async_copy(mine, keys, sems.at[0]),
+        pltpu.make_async_copy(weight, scaled.at[0], sems.at[1]),
+        pltpu.make_async_copy(across, scaled.at[1], sems.at[2]),
     ]
     for load in loads:
         load.start()
     loads[0].wait()
     stores = []
     sizes = []
-    for half in range(2):
-        loads[1 + half].wait()
-        out, size = products(keys[half], scaled[...])
+    for which in range(2):
+        loads[1 + which].wait()
+        out, size = products(keys[...], scaled[which])
         sizes.append(size)
-        rest[half] = out.reshape(16, HALF, KW)
-        rows = pl.ds(half * HALF, HALF)
-        stores.append(pltpu.make_async_copy(rest.at[half], back.at[:, rows, :], sems.at[3 + half]))
+        rest[which] = out.reshape(16, HALF, KW)
+        rows = pl.ds(which * HALF, HALF)
+        stores.append(pltpu.make_async_copy(rest.at[which], back.at[:, rows, :], sems.at[3 + which]))
         stores[-1].start()
     high[...] = jnp.maximum(sizes[0], sizes[1])
     for store in stores:
         store.wait()
 
 
-def product(mine, other, weight):
+def product(mine, weight, across):
     return call(
         product_kernel,
         "product",
@@ -209,12 +214,12 @@
         2**30,
         5 * 2**20,
         scratch_shapes=[
-            pltpu.VMEM((2, 16, HALF, KW), BF16),
-            pltpu.VMEM((KW, KW), BF16),
+            pltpu.VMEM((16, HALF, KW), BF16),
+            pltpu.VMEM((2, KW, KW), BF16),
             pltpu.VMEM((2, 16, HALF, KW), BF16),
             pltpu.SemaphoreType.DMA((5,)),
         ],
-    )(hbm(mine), hbm(other), hbm(weight))
+    )(hbm(mine), hbm(weight), hbm(across))
 
 
 def reduce_kernel(factor, terms, high, piece, peaks):
@@ -256,15 +261,15 @@
     z = lax.axis_index("z")
     copies = []
     for q in range(8):
-        place = lax.rem(z + SHIFT[q], 8) * 1024
-        for e in range(2):
-            lanes = pl.ds(pl.multiple_of(place + e * 512, 512), 512)
-            for half in range(2):
-                at = HALF * (half ^ (q % 2))
+        core = q % 2
+        for which in range(2):
+            place = lax.rem(z + SHIFT[q ^ which], 8) * 1024
+            for e in range(2):
+                lanes = pl.ds(pl.multiple_of(place + e * 512, 512), 512)
                 copies.append(
                     pltpu.make_async_copy(
-                        back.at[q * 2 + e, pl.ds(half * HALF, HALF), :],
-                        out.at[pl.ds(at, HALF), lanes],
+                        back.at[q * 2 + e, pl.ds(which * HALF, HALF), :],
+                        out.at[pl.ds(core * HALF, HALF), lanes],
                         sems.at[len(copies)],
                     )
                 )
@@ -346,10 +351,11 @@
     packed, weight = pack(tokens, key_grad, weight_codes, block_scales)
     weight = shift_weight(weight)
     got = lax.all_to_all(packed, GROUP, 0, 0, tiled=True)
-    got, weight = lax.optimization_barrier((got, weight))
-    total, mine = own_half(got)
-    share, other = other_half(got, swap(got[:, COUNT:]), total)
-    back, high = product(mine, other, weight)
+    got, weight, across = lax.optimization_barrier((got, weight, swap(weight)))
+    other = swap(away(got))
+    total, mine = home(got)
+    share = join(total, other)
+    back, high = product(mine, weight, across)
 
     terms = lax.all_to_all(share, SPREAD, 0, 0, tiled=True)
     piece, peaks = reduce_terms(factor, terms, high)

time: 144 us -> 143 us (level)
  waiting for transfers between devices: 47.7 us -> 45 us
  starting transfers between devices: 60.3 us -> 62.2 us
    all_to_all x1, waiting for transfers between devices: 22.6 us -> 18.8 us  [local(): got = lax.all_to_all(packed, GROUP, 0, 0, tiled=True)]
    ppermute x7 -> x8, starting transfers between devices: 23.8 us -> 25.7 us  [from_ahead(): return lax.ppermute(x, axis, [((i + step) % size, i) for i in range(size)])]
    ppermute x7 -> x8, waiting for transfers between devices: 4.75 us -> 6.01 us  [from_ahead(): return lax.ppermute(x, axis, [((i + step) % size, i) for i in range(size)])]
  transfers between devices with their start and end apart: 11 -> 12, of which waited for: 8 -> 9; matrix products, arithmetic and copies ran while one was open for 0% -> 0% of each run, Pallas kernels for 5% -> 5%
where the time goes in v8:
time: 143 us; the launch traced here: 141 us
  starting transfers between devices  62.2 us (43%)
  waiting for transfers between devices  45 us (31%)
  blocking collectives  19.4 us (14%)
  Pallas kernels  13.2 us (9%)
    ppermute x8, starting transfers between devices, from_ahead(): return lax.ppermute(x, axis, [((i + step) % size, i) for i in range(size)])  25.7 us
    all_to_all x1, blocking collectives, local(): plane = lax.all_to_all(spread(piece, peaks), PLANE, 0, 0, tiled=True)  19.4 us
    all_to_all x1, waiting for transfers between devices, local(): got = lax.all_to_all(packed, GROUP, 0, 0, tiled=True)  18.8 us
    all_to_all x1, waiting for transfers between devices, local(): terms = lax.all_to_all(share, SPREAD, 0, 0, tiled=True)  11.8 us
    all_to_all x1, starting transfers between devices, local(): terms = lax.all_to_all(share, SPREAD, 0, 0, tiled=True)  11.1 us
    all_to_all x1, starting transfers between devices, local(): got = lax.all_to_all(packed, GROUP, 0, 0, tiled=True)  10.4 us
    all_to_all x1, starting transfers between devices, local(): back = lax.all_to_all(back, GROUP, 0, 0, tiled=True)  7.92 us
    ppermute x1, waiting for transfers between devices, shift_weight(): return lax.ppermute(weight, ('yl', 'xh', 'core', 'z'), pairs)  7.17 us
  transfers between devices with their start and end apart: 12, of which 9 were waited for; matrix products, arithmetic and copies ran while one was open for 0% of the time, Pallas kernels for 5%

profile of v8, /device:TPU:1, one launch (start us, length us, event | category | flops | bytes accessed | tf_op | source)
XLA Modules:
  0.0 140.7 jit_solution(6304324023794722123)
XLA Ops:
  0.6 3.2 %pack.1 = (bf16[16,192,512]{2,1,0:T(8,128)(2,1)}, bf16[512,512]{1,0:T(8,128)(2,1)}) custom-call(bf16[128,8192]{1,0:T(8,128)(2,1)} %tokens.1, bf16[128,512]{1,0:T(8,128)(2,1)} %keys.1, bf16[512,512]{1,0:T(8,128)(2,1)} %codes.1, f32[4]{0:T(128)} %scales.1), custom_call_target="tpu_custom_call" | custom-call | bytes 9437184 | tf_op jit(solution)/shard_map/pack/pallas_call | solution.py:95
  3.9 10.4 %all-to-all-start = ((bf16[16,192,512]{2,1,0:T(8,128)(2,1)}), bf16[16,192,512]{2,1,0:T(8,128)(2,1)S(1)}, u32[]{:S(2)}, u32[]{:S(2)}) async-start(bf16[16,192,512]{2,1,0:T(8,128)(2,1)} %get-tuple-element.20), calls=%async_computation | async-start | bytes 6291456 | tf_op jit(solution)/shard_map/all_to_all | solution.py:353
  14.3 7.0 %collective-permute-start = (bf16[512,512]{1,0:T(8,128)(2,1)}, bf16[512,512]{1,0:T(8,128)(2,1)S(1)}, u32[]{:S(2)}, u32[]{:S(2)}) collective-permute-start(bf16[512,512]{1,0:T(8,128)(2,1)} %get-tuple-element.21), channel_id=1, source_target_pairs={{0,0},{2,2},{4,4},{6,6},{8,8},{10,10},{12,12},{14,14},{24,16},{26,... | collective-permute-start | bytes 1572872 | tf_op jit(solution)/shard_map/ppermute | solution.py:345
  21.4 7.2 %collective-permute-done.weight = bf16[512,512]{1,0:T(8,128)(2,1)S(1)} collective-permute-done((bf16[512,512]{1,0:T(8,128)(2,1)}, bf16[512,512]{1,0:T(8,128)(2,1)S(1)}, u32[]{:S(2)}, u32[]{:S(2)}) %collective-permute-start) | collective-permute-done | bytes 524320 | tf_op jit(solution)/shard_map/ppermute | solution.py:345
  28.5 1.9 %collective-permute-start.1 = (bf16[512,512]{1,0:T(8,128)(2,1)S(1)}, bf16[512,512]{1,0:T(8,128)(2,1)}, u32[]{:S(2)}, u32[]{:S(2)}) collective-permute-start(bf16[512,512]{1,0:T(8,128)(2,1)S(1)} %collective-permute-done.weight), channel_id=1, source_target_pairs={{16,0},{0,16},{17,1},{1,17},{18,2},{2,18},{19,3},{3,19},{20,4},{4,... | collective-permute-start | bytes 1572872 | tf_op jit(solution)/shard_map/ppermute | solution.py:330
  30.5 2.0 %collective-permute-done.1.across = bf16[512,512]{1,0:T(8,128)(2,1)} collective-permute-done((bf16[512,512]{1,0:T(8,128)(2,1)S(1)}, bf16[512,512]{1,0:T(8,128)(2,1)}, u32[]{:S(2)}, u32[]{:S(2)}) %collective-permute-start.1) | collective-permute-done | bytes 524320 | tf_op jit(solution)/shard_map/ppermute | solution.py:330
  32.5 18.8 %all-to-all-done.got = bf16[16,192,512]{2,1,0:T(8,128)(2,1)S(1)} async-done(((bf16[16,192,512]{2,1,0:T(8,128)(2,1)}), bf16[16,192,512]{2,1,0:T(8,128)(2,1)S(1)}, u32[]{:S(2)}, u32[]{:S(2)}) %all-to-all-start) | async-done | bytes 3145760 | tf_op jit(solution)/shard_map/all_to_all | solution.py:353
  52.0 4.0 %collective-permute-start.2 = (bf16[512,512]{1,0:T(8,128)(2,1)S(1)}, bf16[512,512]{1,0:T(8,128)(2,1)S(1)}, u32[]{:S(2)}, u32[]{:S(2)}) collective-permute-start(bf16[512,512]{1,0:T(8,128)(2,1)S(1)} %away.1), channel_id=1, source_target_pairs={{16,0},{0,16},{17,1},{1,17},{18,2},{2,18},{19,3},{3,19},{20,4},{4,... | collective-permute-start | bytes 1572872 | tf_op jit(solution)/shard_map/ppermute | solution.py:330
  58.4 11.1 %all-to-all-start.1 = ((bf16[32,16,512]{2,1,0:T(8,128)(2,1)}), bf16[32,16,512]{2,1,0:T(8,128)(2,1)S(1)}, u32[]{:S(2)}, u32[]{:S(2)}) async-start(bf16[32,16,512]{2,1,0:T(8,128)(2,1)} %join.1), calls=%async_computation.1 | async-start | bytes 1048576 | tf_op jit(solution)/shard_map/all_to_all | solution.py:360
  69.6 3.9 %product.1 = (bf16[16,128,512]{2,1,0:T(8,128)(2,1)}, f32[8,512]{1,0:T(8,128)S(1)}) custom-call(bf16[16,64,512]{2,1,0:T(8,128)(2,1)} %get-tuple-element.23.mine, bf16[512,512]{1,0:T(8,128)(2,1)} %copy-done, bf16[512,512]{1,0:T(8,128)(2,1)} %collective-permute-done.1.across), custom_call_target="tpu_custom_call" | custom-call | flops 1073741824 | bytes 5242880 | tf_op jit(solution)/shard_map/product/pallas_call | solution.py:208
  73.4 11.8 %all-to-all-done.1.refs_0_ = bf16[32,16,512]{2,1,0:T(8,128)(2,1)S(1)} async-done(((bf16[32,16,512]{2,1,0:T(8,128)(2,1)}), bf16[32,16,512]{2,1,0:T(8,128)(2,1)S(1)}, u32[]{:S(2)}, u32[]{:S(2)}) %all-to-all-start.1) | async-done | bytes 524320 | tf_op jit(solution)/shard_map/all_to_all | solution.py:360
  85.5 19.4 %all_to_all.20.mine = bf16[16,16,640]{2,1,0:T(8,128)(2,1)S(1)} all-to-all(bf16[16,16,640]{2,1,0:T(8,128)(2,1)S(1)} %spread.1), channel_id=1, replica_groups=mesh['yh'=4,'yl'=2,'xh'=2,'core'=2,'z'=8,'xl'=2] {'xh','yh','yl'}, dimensions={0} | all-to-all | bytes 655360 | tf_op jit(solution)/shard_map/all_to_all | solution.py:363
  104.9 7.9 %all-to-all-start.3 = ((bf16[16,128,512]{2,1,0:T(8,128)(2,1)}), bf16[16,128,512]{2,1,0:T(8,128)(2,1)S(1)}, u32[]{:S(2)}, u32[]{:S(2)}) async-start(bf16[16,128,512]{2,1,0:T(8,128)(2,1)} %get-tuple-element.31), calls=%async_computation.3 | async-start | bytes 4194304 | tf_op jit(solution)/shard_map/all_to_all | solution.py:366
  112.8 2.0 %collective-permute-start.3 = (bf16[16,16,640]{2,1,0:T(8,128)(2,1)S(1)}, bf16[16,16,640]{2,1,0:T(8,128)(2,1)S(1)}, u32[]{:S(2)}, u32[]{:S(2)}) collective-permute-start(bf16[16,16,640]{2,1,0:T(8,128)(2,1)S(1)} %all_to_all.20.mine), channel_id=1, source_target_pairs={{16,0},{0,16},{17,1},{1,17},{18,2},{2,18},{19,3},{3,19},{20,4},{4,... | collective-permute-start | bytes 983048 | tf_op jit(solution)/shard_map/ppermute | solution.py:330
  114.8 1.5 %collective-permute-done.3.other = bf16[16,16,640]{2,1,0:T(8,128)(2,1)S(1)} collective-permute-done((bf16[16,16,640]{2,1,0:T(8,128)(2,1)S(1)}, bf16[16,16,640]{2,1,0:T(8,128)(2,1)S(1)}, u32[]{:S(2)}, u32[]{:S(2)}) %collective-permute-start.3) | collective-permute-done | bytes 327712 | tf_op jit(solution)/shard_map/ppermute | solution.py:330
  116.3 3.0 %collective-permute-start.5 = (f32[8,128]{1,0:T(8,128)S(1)}, f32[8,128]{1,0:T(8,128)S(1)}, u32[]{:S(2)}, u32[]{:S(2)}) collective-permute-start(f32[8,128]{1,0:T(8,128)S(1)} %peaks_of.1), channel_id=1, source_target_pairs={{14,0},{0,2},{2,4},{4,6},{6,8},{8,10},{10,12},{12,14},{15,1},{1,3}... | collective-permute-start | bytes 12296 | tf_op jit(solution)/shard_map/ppermute | solution.py:330
  119.3 3.5 %collective-permute-start.4 = (f32[8,128]{1,0:T(8,128)S(1)}, f32[8,128]{1,0:T(8,128)S(1)}, u32[]{:S(2)}, u32[]{:S(2)}) collective-permute-start(f32[8,128]{1,0:T(8,128)S(1)} %peaks_of.1), channel_id=1, source_target_pairs={{2,0},{4,2},{6,4},{8,6},{10,8},{12,10},{14,12},{0,14},{3,1},{5,3},... | collective-permute-start | bytes 12296 | tf_op jit(solution)/shard_map/ppermute | solution.py:330
  122.9 1.1 merge.1
  124.0 4.1 %collective-permute-start.7 = (f32[8,128]{1,0:T(8,128)S(1)}, f32[8,128]{1,0:T(8,128)S(1)}, u32[]{:S(2)}, u32[]{:S(2)}) collective-permute-start(f32[8,128]{1,0:T(8,128)S(1)} %maximum_maximum_fusion.1), channel_id=1, source_target_pairs={{10,0},{12,2},{14,4},{0,6},{2,8},{4,10},{6,12},{8,14},{11,1},{13,3... | collective-permute-start | bytes 12296 | tf_op jit(solution)/shard_map/ppermute | solution.py:330
  128.1 4.2 %collective-permute-start.6 = (f32[8,128]{1,0:T(8,128)S(1)}, f32[8,128]{1,0:T(8,128)S(1)}, u32[]{:S(2)}, u32[]{:S(2)}) collective-permute-start(f32[8,128]{1,0:T(8,128)S(1)} %maximum_maximum_fusion.1), channel_id=1, source_target_pairs={{6,0},{8,2},{10,4},{12,6},{14,8},{0,10},{2,12},{4,14},{7,1},{9,3},... | collective-permute-start | bytes 12296 | tf_op jit(solution)/shard_map/ppermute | solution.py:330
  132.3 1.9 %collective-permute-done.6 = f32[8,128]{1,0:T(8,128)S(1)} collective-permute-done((f32[8,128]{1,0:T(8,128)S(1)}, f32[8,128]{1,0:T(8,128)S(1)}, u32[]{:S(2)}, u32[]{:S(2)}) %collective-permute-start.6) | collective-permute-done | bytes 4128 | tf_op jit(solution)/shard_map/ppermute | solution.py:330
  134.2 3.0 %collective-permute-start.8 = (f32[8,128]{1,0:T(8,128)S(1)}, f32[8,128]{1,0:T(8,128)S(1)}, u32[]{:S(2)}, u32[]{:S(2)}) collective-permute-start(f32[8,128]{1,0:T(8,128)S(1)} %maximum_maximum_fusion.a), channel_id=1, source_target_pairs={{1,0},{0,1},{3,2},{2,3},{5,4},{4,5},{7,6},{6,7},{9,8},{8,9},{11,10... | collective-permute-start | bytes 12296 | tf_op jit(solution)/shard_map/ppermute | solution.py:330
  137.2 1.3 all-to-all-done.3.back
  138.5 1.6 %unpack.1 = bf16[128,8192]{1,0:T(8,128)(2,1)} custom-call(bf16[16,128,512]{2,1,0:T(8,128)(2,1)S(1)} %all-to-all-done.3.back), custom_call_target="tpu_custom_call" | custom-call | bytes 4194304 | tf_op jit(solution)/shard_map/unpack/pallas_call | solution.py:282
  (16 shorter events, 4.1 us)
Async XLA Ops:
  3.9 47.3 %all-to-all-start = ((bf16[16,192,512]{2,1,0:T(8,128)(2,1)}), bf16[16,192,512]{2,1,0:T(8,128)(2,1)S(1)}, u32[]{:S(2)}, u32[]{:S(2)}) async-start(bf16[16,192,512]{2,1,0:T(8,128)(2,1)} %get-tuple-element.20), calls=%async_computation | async-start | bytes 6291456 | tf_op jit(solution)/shard_map/all_to_all | solution.py:353
  14.3 14.2 %collective-permute-start = (bf16[512,512]{1,0:T(8,128)(2,1)}, bf16[512,512]{1,0:T(8,128)(2,1)S(1)}, u32[]{:S(2)}, u32[]{:S(2)}) collective-permute-start(bf16[512,512]{1,0:T(8,128)(2,1)} %get-tuple-element.21), channel_id=1, source_target_pairs={{0,0},{2,2},{4,4},{6,6},{8,8},{10,10},{12,12},{14,14},{24,16},{26,... | collective-permute-start | bytes 1572872 | tf_op jit(solution)/shard_map/ppermute | solution.py:345
  28.5 1.9 %copy-start = (bf16[512,512]{1,0:T(8,128)(2,1)}, bf16[512,512]{1,0:T(8,128)(2,1)S(1)}, u32[]{:S(2)}) copy-start(bf16[512,512]{1,0:T(8,128)(2,1)S(1)} %collective-permute-done.weight) | copy-start | bytes 1572868
  28.5 3.9 %collective-permute-start.1 = (bf16[512,512]{1,0:T(8,128)(2,1)S(1)}, bf16[512,512]{1,0:T(8,128)(2,1)}, u32[]{:S(2)}, u32[]{:S(2)}) collective-permute-start(bf16[512,512]{1,0:T(8,128)(2,1)S(1)} %collective-permute-done.weight), channel_id=1, source_target_pairs={{16,0},{0,16},{17,1},{1,17},{18,2},{2,18},{19,3},{3,19},{20,4},{4,... | collective-permute-start | bytes 1572872 | tf_op jit(solution)/shard_map/ppermute | solution.py:330
  52.0 5.5 %collective-permute-start.2 = (bf16[512,512]{1,0:T(8,128)(2,1)S(1)}, bf16[512,512]{1,0:T(8,128)(2,1)S(1)}, u32[]{:S(2)}, u32[]{:S(2)}) collective-permute-start(bf16[512,512]{1,0:T(8,128)(2,1)S(1)} %away.1), channel_id=1, source_target_pairs={{16,0},{0,16},{17,1},{1,17},{18,2},{2,18},{19,3},{3,19},{20,4},{4,... | collective-permute-start | bytes 1572872 | tf_op jit(solution)/shard_map/ppermute | solution.py:330
  58.4 26.8 %all-to-all-start.1 = ((bf16[32,16,512]{2,1,0:T(8,128)(2,1)}), bf16[32,16,512]{2,1,0:T(8,128)(2,1)S(1)}, u32[]{:S(2)}, u32[]{:S(2)}) async-start(bf16[32,16,512]{2,1,0:T(8,128)(2,1)} %join.1), calls=%async_computation.1 | async-start | bytes 1048576 | tf_op jit(solution)/shard_map/all_to_all | solution.py:360
  104.9 33.6 %all-to-all-start.3 = ((bf16[16,128,512]{2,1,0:T(8,128)(2,1)}), bf16[16,128,512]{2,1,0:T(8,128)(2,1)S(1)}, u32[]{:S(2)}, u32[]{:S(2)}) async-start(bf16[16,128,512]{2,1,0:T(8,128)(2,1)} %get-tuple-element.31), calls=%async_computation.3 | async-start | bytes 4194304 | tf_op jit(solution)/shard_map/all_to_all | solution.py:366
  112.8 3.5 %collective-permute-start.3 = (bf16[16,16,640]{2,1,0:T(8,128)(2,1)S(1)}, bf16[16,16,640]{2,1,0:T(8,128)(2,1)S(1)}, u32[]{:S(2)}, u32[]{:S(2)}) collective-permute-start(bf16[16,16,640]{2,1,0:T(8,128)(2,1)S(1)} %all_to_all.20.mine), channel_id=1, source_target_pairs={{16,0},{0,16},{17,1},{1,17},{18,2},{2,18},{19,3},{3,19},{20,4},{4,... | collective-permute-start | bytes 983048 | tf_op jit(solution)/shard_map/ppermute | solution.py:330
  116.3 7.6 %collective-permute-start.5 = (f32[8,128]{1,0:T(8,128)S(1)}, f32[8,128]{1,0:T(8,128)S(1)}, u32[]{:S(2)}, u32[]{:S(2)}) collective-permute-start(f32[8,128]{1,0:T(8,128)S(1)} %peaks_of.1), channel_id=1, source_target_pairs={{14,0},{0,2},{2,4},{4,6},{6,8},{8,10},{10,12},{12,14},{15,1},{1,3}... | collective-permute-start | bytes 12296 | tf_op jit(solution)/shard_map/ppermute | solution.py:330
  119.3 4.6 %collective-permute-start.4 = (f32[8,128]{1,0:T(8,128)S(1)}, f32[8,128]{1,0:T(8,128)S(1)}, u32[]{:S(2)}, u32[]{:S(2)}) collective-permute-start(f32[8,128]{1,0:T(8,128)S(1)} %peaks_of.1), channel_id=1, source_target_pairs={{2,0},{4,2},{6,4},{8,6},{10,8},{12,10},{14,12},{0,14},{3,1},{5,3},... | collective-permute-start | bytes 12296 | tf_op jit(solution)/shard_map/ppermute | solution.py:330
  124.0 8.3 %collective-permute-start.7 = (f32[8,128]{1,0:T(8,128)S(1)}, f32[8,128]{1,0:T(8,128)S(1)}, u32[]{:S(2)}, u32[]{:S(2)}) collective-permute-start(f32[8,128]{1,0:T(8,128)S(1)} %maximum_maximum_fusion.1), channel_id=1, source_target_pairs={{10,0},{12,2},{14,4},{0,6},{2,8},{4,10},{6,12},{8,14},{11,1},{13,3... | collective-permute-start | bytes 12296 | tf_op jit(solution)/shard_map/ppermute | solution.py:330
  128.1 6.2 %collective-permute-start.6 = (f32[8,128]{1,0:T(8,128)S(1)}, f32[8,128]{1,0:T(8,128)S(1)}, u32[]{:S(2)}, u32[]{:S(2)}) collective-permute-start(f32[8,128]{1,0:T(8,128)S(1)} %maximum_maximum_fusion.1), channel_id=1, source_target_pairs={{6,0},{8,2},{10,4},{12,6},{14,8},{0,10},{2,12},{4,14},{7,1},{9,3},... | collective-permute-start | bytes 12296 | tf_op jit(solution)/shard_map/ppermute | solution.py:330
  134.2 5.9 %collective-permute-start.8 = (f32[8,128]{1,0:T(8,128)S(1)}, f32[8,128]{1,0:T(8,128)S(1)}, u32[]{:S(2)}, u32[]{:S(2)}) collective-permute-start(f32[8,128]{1,0:T(8,128)S(1)} %maximum_maximum_fusion.a), channel_id=1, source_target_pairs={{1,0},{0,1},{3,2},{2,3},{5,4},{4,5},{7,6},{6,7},{9,8},{8,9},{11,10... | collective-permute-start | bytes 12296 | tf_op jit(solution)/shard_map/ppermute | solution.py:330

commit v9 on v8

--- a/solution.py
+++ b/solution.py
@@ -11,7 +11,7 @@
 QBLOCK = 128
 AXES = ("yh", "yl", "xh", "core", "z", "xl")
 SIZES = (4, 2, 2, 2, 8, 2)
-GROUP = ("yl", "xh", "core", "xl")
+GROUP = ("xh", "xl", "core", "yl")
 SPREAD = ("yh", "z")
 PLANE = ("xh", "yh", "yl")
 SHIFT = (0, 4, 1, 7, 2, 6, 3, 5)
@@ -80,7 +80,7 @@
                     for core in range(2):
                         first, second = (even, odd) if core == 0 else (odd, even)
                         at = HALF * (half ^ core)
-                        ready[t * 4 + half * 2 + e, at : at + HALF, lanes] = jnp.where(low, first, second)
+                        ready[t % 2 * 8 + e * 4 + half * 2 + t // 2, at : at + HALF, lanes] = jnp.where(low, first, second)
         stores.append(pltpu.make_async_copy(ready.at[:, :, lanes], out.at[:, :, lanes], sems.at[11 + m]))
         stores[-1].start()
     for store in stores:
@@ -268,7 +268,7 @@
                 lanes = pl.ds(pl.multiple_of(place + e * 512, 512), 512)
                 copies.append(
                     pltpu.make_async_copy(
-                        back.at[q * 2 + e, pl.ds(which * HALF, HALF), :],
+                        back.at[q // 2 % 2 * 8 + e * 4 + core * 2 + q // 4, pl.ds(which * HALF, HALF), :],
                         out.at[pl.ds(core * HALF, HALF), lanes],
                         sems.at[len(copies)],
                     )

time: 143 us -> 142 us (level)
  starting transfers between devices: 62.2 us -> 59.3 us
  waiting for transfers between devices: 45 us -> 46.7 us
    ppermute x8, starting transfers between devices: 25.7 us -> 24.1 us  [from_ahead(): return lax.ppermute(x, axis, [((i + step) % size, i) for i in range(size)])]
  transfers between devices with their start and end apart: 12 -> 12, of which waited for: 9 -> 8; matrix products, arithmetic and copies ran while one was open for 0% -> 0% of each run, Pallas kernels for 5% -> 5%
where the time goes in v9:
time: 142 us; the launch traced here: 141 us
  starting transfers between devices  59.3 us (42%)
  waiting for transfers between devices  46.7 us (33%)
  blocking collectives  20.5 us (14%)
  Pallas kernels  13.2 us (9%)
    ppermute x8, starting transfers between devices, from_ahead(): return lax.ppermute(x, axis, [((i + step) % size, i) for i in range(size)])  24.1 us
    all_to_all x1, blocking collectives, local(): plane = lax.all_to_all(spread(piece, peaks), PLANE, 0, 0, tiled=True)  20.5 us
    all_to_all x1, waiting for transfers between devices, local(): got = lax.all_to_all(packed, GROUP, 0, 0, tiled=True)  19.6 us
    all_to_all x1, waiting for transfers between devices, local(): terms = lax.all_to_all(share, SPREAD, 0, 0, tiled=True)  11.9 us
    all_to_all x1, starting transfers between devices, local(): terms = lax.all_to_all(share, SPREAD, 0, 0, tiled=True)  11.2 us
    all_to_all x1, starting transfers between devices, local(): got = lax.all_to_all(packed, GROUP, 0, 0, tiled=True)  10.4 us
    ppermute x1, waiting for transfers between devices, shift_weight(): return lax.ppermute(weight, ('yl', 'xh', 'core', 'z'), pairs)  7.17 us
    ppermute x1, starting transfers between devices, shift_weight(): return lax.ppermute(weight, ('yl', 'xh', 'core', 'z'), pairs)  7.04 us
  transfers between devices with their start and end apart: 12, of which 8 were waited for; matrix products, arithmetic and copies ran while one was open for 0% of the time, Pallas kernels for 5%

profile of v9, /device:TPU:1, one launch (start us, length us, event | category | flops | bytes accessed | tf_op | source)
XLA Modules:
  0.0 140.6 jit_solution(14368843862554772589)
XLA Ops:
  0.6 3.2 %pack.1 = (bf16[16,192,512]{2,1,0:T(8,128)(2,1)}, bf16[512,512]{1,0:T(8,128)(2,1)}) custom-call(bf16[128,8192]{1,0:T(8,128)(2,1)} %tokens.1, bf16[128,512]{1,0:T(8,128)(2,1)} %keys.1, bf16[512,512]{1,0:T(8,128)(2,1)} %codes.1, f32[4]{0:T(128)} %scales.1), custom_call_target="tpu_custom_call" | custom-call | bytes 9437184 | tf_op jit(solution)/shard_map/pack/pallas_call | solution.py:95
  3.9 10.4 %all-to-all-start = ((bf16[16,192,512]{2,1,0:T(8,128)(2,1)}), bf16[16,192,512]{2,1,0:T(8,128)(2,1)S(1)}, u32[]{:S(2)}, u32[]{:S(2)}) async-start(bf16[16,192,512]{2,1,0:T(8,128)(2,1)} %get-tuple-element.20), calls=%async_computation | async-start | bytes 6291456 | tf_op jit(solution)/shard_map/all_to_all | solution.py:353
  14.3 7.0 %collective-permute-start = (bf16[512,512]{1,0:T(8,128)(2,1)}, bf16[512,512]{1,0:T(8,128)(2,1)S(1)}, u32[]{:S(2)}, u32[]{:S(2)}) collective-permute-start(bf16[512,512]{1,0:T(8,128)(2,1)} %get-tuple-element.21), channel_id=1, source_target_pairs={{0,0},{2,2},{4,4},{6,6},{8,8},{10,10},{12,12},{14,14},{24,16},{26,... | collective-permute-start | bytes 1572872 | tf_op jit(solution)/shard_map/ppermute | solution.py:345
  21.4 7.2 %collective-permute-done.weight = bf16[512,512]{1,0:T(8,128)(2,1)S(1)} collective-permute-done((bf16[512,512]{1,0:T(8,128)(2,1)}, bf16[512,512]{1,0:T(8,128)(2,1)S(1)}, u32[]{:S(2)}, u32[]{:S(2)}) %collective-permute-start) | collective-permute-done | bytes 524320 | tf_op jit(solution)/shard_map/ppermute | solution.py:345
  28.5 1.9 %collective-permute-start.1 = (bf16[512,512]{1,0:T(8,128)(2,1)S(1)}, bf16[512,512]{1,0:T(8,128)(2,1)}, u32[]{:S(2)}, u32[]{:S(2)}) collective-permute-start(bf16[512,512]{1,0:T(8,128)(2,1)S(1)} %collective-permute-done.weight), channel_id=1, source_target_pairs={{16,0},{0,16},{17,1},{1,17},{18,2},{2,18},{19,3},{3,19},{20,4},{4,... | collective-permute-start | bytes 1572872 | tf_op jit(solution)/shard_map/ppermute | solution.py:330
  30.5 2.0 %collective-permute-done.1.across = bf16[512,512]{1,0:T(8,128)(2,1)} collective-permute-done((bf16[512,512]{1,0:T(8,128)(2,1)S(1)}, bf16[512,512]{1,0:T(8,128)(2,1)}, u32[]{:S(2)}, u32[]{:S(2)}) %collective-permute-start.1) | collective-permute-done | bytes 524320 | tf_op jit(solution)/shard_map/ppermute | solution.py:330
  32.5 19.6 %all-to-all-done.got = bf16[16,192,512]{2,1,0:T(8,128)(2,1)S(1)} async-done(((bf16[16,192,512]{2,1,0:T(8,128)(2,1)}), bf16[16,192,512]{2,1,0:T(8,128)(2,1)S(1)}, u32[]{:S(2)}, u32[]{:S(2)}) %all-to-all-start) | async-done | bytes 3145760 | tf_op jit(solution)/shard_map/all_to_all | solution.py:353
  52.8 2.1 %collective-permute-start.2 = (bf16[512,512]{1,0:T(8,128)(2,1)S(1)}, bf16[512,512]{1,0:T(8,128)(2,1)S(1)}, u32[]{:S(2)}, u32[]{:S(2)}) collective-permute-start(bf16[512,512]{1,0:T(8,128)(2,1)S(1)} %away.1), channel_id=1, source_target_pairs={{16,0},{0,16},{17,1},{1,17},{18,2},{2,18},{19,3},{3,19},{20,4},{4,... | collective-permute-start | bytes 1572872 | tf_op jit(solution)/shard_map/ppermute | solution.py:330
  57.5 11.2 %all-to-all-start.1 = ((bf16[32,16,512]{2,1,0:T(8,128)(2,1)}), bf16[32,16,512]{2,1,0:T(8,128)(2,1)S(1)}, u32[]{:S(2)}, u32[]{:S(2)}) async-start(bf16[32,16,512]{2,1,0:T(8,128)(2,1)} %join.1), calls=%async_computation.1 | async-start | bytes 1048576 | tf_op jit(solution)/shard_map/all_to_all | solution.py:360
  68.7 3.9 %product.1 = (bf16[16,128,512]{2,1,0:T(8,128)(2,1)}, f32[8,512]{1,0:T(8,128)S(1)}) custom-call(bf16[16,64,512]{2,1,0:T(8,128)(2,1)} %get-tuple-element.23.mine, bf16[512,512]{1,0:T(8,128)(2,1)} %copy-done, bf16[512,512]{1,0:T(8,128)(2,1)} %collective-permute-done.1.across), custom_call_target="tpu_custom_call" | custom-call | flops 1073741824 | bytes 5242880 | tf_op jit(solution)/shard_map/product/pallas_call | solution.py:208
  72.6 11.9 %all-to-all-done.1.refs_0_ = bf16[32,16,512]{2,1,0:T(8,128)(2,1)S(1)} async-done(((bf16[32,16,512]{2,1,0:T(8,128)(2,1)}), bf16[32,16,512]{2,1,0:T(8,128)(2,1)S(1)}, u32[]{:S(2)}, u32[]{:S(2)}) %all-to-all-start.1) | async-done | bytes 524320 | tf_op jit(solution)/shard_map/all_to_all | solution.py:360
  84.7 20.5 %all_to_all.20.mine = bf16[16,16,640]{2,1,0:T(8,128)(2,1)S(1)} all-to-all(bf16[16,16,640]{2,1,0:T(8,128)(2,1)S(1)} %spread.1), channel_id=1, replica_groups=mesh['yh'=4,'yl'=2,'xh'=2,'core'=2,'z'=8,'xl'=2] {'xh','yh','yl'}, dimensions={0} | all-to-all | bytes 655360 | tf_op jit(solution)/shard_map/all_to_all | solution.py:363
  105.2 6.6 %all-to-all-start.3 = ((bf16[16,128,512]{2,1,0:T(8,128)(2,1)}), bf16[16,128,512]{2,1,0:T(8,128)(2,1)S(1)}, u32[]{:S(2)}, u32[]{:S(2)}) async-start(bf16[16,128,512]{2,1,0:T(8,128)(2,1)} %get-tuple-element.31), calls=%async_computation.3 | async-start | bytes 4194304 | tf_op jit(solution)/shard_map/all_to_all | solution.py:366
  111.9 2.0 %collective-permute-start.3 = (bf16[16,16,640]{2,1,0:T(8,128)(2,1)S(1)}, bf16[16,16,640]{2,1,0:T(8,128)(2,1)S(1)}, u32[]{:S(2)}, u32[]{:S(2)}) collective-permute-start(bf16[16,16,640]{2,1,0:T(8,128)(2,1)S(1)} %all_to_all.20.mine), channel_id=1, source_target_pairs={{16,0},{0,16},{17,1},{1,17},{18,2},{2,18},{19,3},{3,19},{20,4},{4,... | collective-permute-start | bytes 983048 | tf_op jit(solution)/shard_map/ppermute | solution.py:330
  113.9 1.5 %collective-permute-done.3.other = bf16[16,16,640]{2,1,0:T(8,128)(2,1)S(1)} collective-permute-done((bf16[16,16,640]{2,1,0:T(8,128)(2,1)S(1)}, bf16[16,16,640]{2,1,0:T(8,128)(2,1)S(1)}, u32[]{:S(2)}, u32[]{:S(2)}) %collective-permute-start.3) | collective-permute-done | bytes 327712 | tf_op jit(solution)/shard_map/ppermute | solution.py:330
  115.4 2.9 %collective-permute-start.5 = (f32[8,128]{1,0:T(8,128)S(1)}, f32[8,128]{1,0:T(8,128)S(1)}, u32[]{:S(2)}, u32[]{:S(2)}) collective-permute-start(f32[8,128]{1,0:T(8,128)S(1)} %peaks_of.1), channel_id=1, source_target_pairs={{14,0},{0,2},{2,4},{4,6},{6,8},{8,10},{10,12},{12,14},{15,1},{1,3}... | collective-permute-start | bytes 12296 | tf_op jit(solution)/shard_map/ppermute | solution.py:330
  118.3 3.6 %collective-permute-start.4 = (f32[8,128]{1,0:T(8,128)S(1)}, f32[8,128]{1,0:T(8,128)S(1)}, u32[]{:S(2)}, u32[]{:S(2)}) collective-permute-start(f32[8,128]{1,0:T(8,128)S(1)} %peaks_of.1), channel_id=1, source_target_pairs={{2,0},{4,2},{6,4},{8,6},{10,8},{12,10},{14,12},{0,14},{3,1},{5,3},... | collective-permute-start | bytes 12296 | tf_op jit(solution)/shard_map/ppermute | solution.py:330
  121.9 1.1 merge.1
  123.0 4.1 %collective-permute-start.7 = (f32[8,128]{1,0:T(8,128)S(1)}, f32[8,128]{1,0:T(8,128)S(1)}, u32[]{:S(2)}, u32[]{:S(2)}) collective-permute-start(f32[8,128]{1,0:T(8,128)S(1)} %maximum_maximum_fusion.1), channel_id=1, source_target_pairs={{10,0},{12,2},{14,4},{0,6},{2,8},{4,10},{6,12},{8,14},{11,1},{13,3... | collective-permute-start | bytes 12296 | tf_op jit(solution)/shard_map/ppermute | solution.py:330
  127.1 4.2 %collective-permute-start.6 = (f32[8,128]{1,0:T(8,128)S(1)}, f32[8,128]{1,0:T(8,128)S(1)}, u32[]{:S(2)}, u32[]{:S(2)}) collective-permute-start(f32[8,128]{1,0:T(8,128)S(1)} %maximum_maximum_fusion.1), channel_id=1, source_target_pairs={{6,0},{8,2},{10,4},{12,6},{14,8},{0,10},{2,12},{4,14},{7,1},{9,3},... | collective-permute-start | bytes 12296 | tf_op jit(solution)/shard_map/ppermute | solution.py:330
  131.3 1.9 %collective-permute-done.6 = f32[8,128]{1,0:T(8,128)S(1)} collective-permute-done((f32[8,128]{1,0:T(8,128)S(1)}, f32[8,128]{1,0:T(8,128)S(1)}, u32[]{:S(2)}, u32[]{:S(2)}) %collective-permute-start.6) | collective-permute-done | bytes 4128 | tf_op jit(solution)/shard_map/ppermute | solution.py:330
  133.2 3.3 %collective-permute-start.8 = (f32[8,128]{1,0:T(8,128)S(1)}, f32[8,128]{1,0:T(8,128)S(1)}, u32[]{:S(2)}, u32[]{:S(2)}) collective-permute-start(f32[8,128]{1,0:T(8,128)S(1)} %maximum_maximum_fusion.a), channel_id=1, source_target_pairs={{1,0},{0,1},{3,2},{2,3},{5,4},{4,5},{7,6},{6,7},{9,8},{8,9},{11,10... | collective-permute-start | bytes 12296 | tf_op jit(solution)/shard_map/ppermute | solution.py:330
  136.5 1.8 %all-to-all-done.3.back = bf16[16,128,512]{2,1,0:T(8,128)(2,1)S(1)} async-done(((bf16[16,128,512]{2,1,0:T(8,128)(2,1)}), bf16[16,128,512]{2,1,0:T(8,128)(2,1)S(1)}, u32[]{:S(2)}, u32[]{:S(2)}) %all-to-all-start.3) | async-done | bytes 2097184 | tf_op jit(solution)/shard_map/all_to_all | solution.py:366
  138.4 1.6 %unpack.1 = bf16[128,8192]{1,0:T(8,128)(2,1)} custom-call(bf16[16,128,512]{2,1,0:T(8,128)(2,1)S(1)} %all-to-all-done.3.back), custom_call_target="tpu_custom_call" | custom-call | bytes 4194304 | tf_op jit(solution)/shard_map/unpack/pallas_call | solution.py:282
  (16 shorter events, 4.3 us)
Async XLA Ops:
  3.9 48.2 %all-to-all-start = ((bf16[16,192,512]{2,1,0:T(8,128)(2,1)}), bf16[16,192,512]{2,1,0:T(8,128)(2,1)S(1)}, u32[]{:S(2)}, u32[]{:S(2)}) async-start(bf16[16,192,512]{2,1,0:T(8,128)(2,1)} %get-tuple-element.20), calls=%async_computation | async-start | bytes 6291456 | tf_op jit(solution)/shard_map/all_to_all | solution.py:353
  14.3 14.2 %collective-permute-start = (bf16[512,512]{1,0:T(8,128)(2,1)}, bf16[512,512]{1,0:T(8,128)(2,1)S(1)}, u32[]{:S(2)}, u32[]{:S(2)}) collective-permute-start(bf16[512,512]{1,0:T(8,128)(2,1)} %get-tuple-element.21), channel_id=1, source_target_pairs={{0,0},{2,2},{4,4},{6,6},{8,8},{10,10},{12,12},{14,14},{24,16},{26,... | collective-permute-start | bytes 1572872 | tf_op jit(solution)/shard_map/ppermute | solution.py:345
  28.5 1.9 %copy-start = (bf16[512,512]{1,0:T(8,128)(2,1)}, bf16[512,512]{1,0:T(8,128)(2,1)S(1)}, u32[]{:S(2)}) copy-start(bf16[512,512]{1,0:T(8,128)(2,1)S(1)} %collective-permute-done.weight) | copy-start | bytes 1572868
  28.5 3.9 %collective-permute-start.1 = (bf16[512,512]{1,0:T(8,128)(2,1)S(1)}, bf16[512,512]{1,0:T(8,128)(2,1)}, u32[]{:S(2)}, u32[]{:S(2)}) collective-permute-start(bf16[512,512]{1,0:T(8,128)(2,1)S(1)} %collective-permute-done.weight), channel_id=1, source_target_pairs={{16,0},{0,16},{17,1},{1,17},{18,2},{2,18},{19,3},{3,19},{20,4},{4,... | collective-permute-start | bytes 1572872 | tf_op jit(solution)/shard_map/ppermute | solution.py:330
  52.8 3.8 %collective-permute-start.2 = (bf16[512,512]{1,0:T(8,128)(2,1)S(1)}, bf16[512,512]{1,0:T(8,128)(2,1)S(1)}, u32[]{:S(2)}, u32[]{:S(2)}) collective-permute-start(bf16[512,512]{1,0:T(8,128)(2,1)S(1)} %away.1), channel_id=1, source_target_pairs={{16,0},{0,16},{17,1},{1,17},{18,2},{2,18},{19,3},{3,19},{20,4},{4,... | collective-permute-start | bytes 1572872 | tf_op jit(solution)/shard_map/ppermute | solution.py:330
  57.5 26.9 %all-to-all-start.1 = ((bf16[32,16,512]{2,1,0:T(8,128)(2,1)}), bf16[32,16,512]{2,1,0:T(8,128)(2,1)S(1)}, u32[]{:S(2)}, u32[]{:S(2)}) async-start(bf16[32,16,512]{2,1,0:T(8,128)(2,1)} %join.1), calls=%async_computation.1 | async-start | bytes 1048576 | tf_op jit(solution)/shard_map/all_to_all | solution.py:360
  105.2 33.1 %all-to-all-start.3 = ((bf16[16,128,512]{2,1,0:T(8,128)(2,1)}), bf16[16,128,512]{2,1,0:T(8,128)(2,1)S(1)}, u32[]{:S(2)}, u32[]{:S(2)}) async-start(bf16[16,128,512]{2,1,0:T(8,128)(2,1)} %get-tuple-element.31), calls=%async_computation.3 | async-start | bytes 4194304 | tf_op jit(solution)/shard_map/all_to_all | solution.py:366
  111.9 3.5 %collective-permute-start.3 = (bf16[16,16,640]{2,1,0:T(8,128)(2,1)S(1)}, bf16[16,16,640]{2,1,0:T(8,128)(2,1)S(1)}, u32[]{:S(2)}, u32[]{:S(2)}) collective-permute-start(bf16[16,16,640]{2,1,0:T(8,128)(2,1)S(1)} %all_to_all.20.mine), channel_id=1, source_target_pairs={{16,0},{0,16},{17,1},{1,17},{18,2},{2,18},{19,3},{3,19},{20,4},{4,... | collective-permute-start | bytes 983048 | tf_op jit(solution)/shard_map/ppermute | solution.py:330
  115.4 7.6 %collective-permute-start.5 = (f32[8,128]{1,0:T(8,128)S(1)}, f32[8,128]{1,0:T(8,128)S(1)}, u32[]{:S(2)}, u32[]{:S(2)}) collective-permute-start(f32[8,128]{1,0:T(8,128)S(1)} %peaks_of.1), channel_id=1, source_target_pairs={{14,0},{0,2},{2,4},{4,6},{6,8},{8,10},{10,12},{12,14},{15,1},{1,3}... | collective-permute-start | bytes 12296 | tf_op jit(solution)/shard_map/ppermute | solution.py:330
  118.3 4.7 %collective-permute-start.4 = (f32[8,128]{1,0:T(8,128)S(1)}, f32[8,128]{1,0:T(8,128)S(1)}, u32[]{:S(2)}, u32[]{:S(2)}) collective-permute-start(f32[8,128]{1,0:T(8,128)S(1)} %peaks_of.1), channel_id=1, source_target_pairs={{2,0},{4,2},{6,4},{8,6},{10,8},{12,10},{14,12},{0,14},{3,1},{5,3},... | collective-permute-start | bytes 12296 | tf_op jit(solution)/shard_map/ppermute | solution.py:330
  123.0 8.3 %collective-permute-start.7 = (f32[8,128]{1,0:T(8,128)S(1)}, f32[8,128]{1,0:T(8,128)S(1)}, u32[]{:S(2)}, u32[]{:S(2)}) collective-permute-start(f32[8,128]{1,0:T(8,128)S(1)} %maximum_maximum_fusion.1), channel_id=1, source_target_pairs={{10,0},{12,2},{14,4},{0,6},{2,8},{4,10},{6,12},{8,14},{11,1},{13,3... | collective-permute-start | bytes 12296 | tf_op jit(solution)/shard_map/ppermute | solution.py:330
  127.1 6.2 %collective-permute-start.6 = (f32[8,128]{1,0:T(8,128)S(1)}, f32[8,128]{1,0:T(8,128)S(1)}, u32[]{:S(2)}, u32[]{:S(2)}) collective-permute-start(f32[8,128]{1,0:T(8,128)S(1)} %maximum_maximum_fusion.1), channel_id=1, source_target_pairs={{6,0},{8,2},{10,4},{12,6},{14,8},{0,10},{2,12},{4,14},{7,1},{9,3},... | collective-permute-start | bytes 12296 | tf_op jit(solution)/shard_map/ppermute | solution.py:330
  133.2 6.7 %collective-permute-start.8 = (f32[8,128]{1,0:T(8,128)S(1)}, f32[8,128]{1,0:T(8,128)S(1)}, u32[]{:S(2)}, u32[]{:S(2)}) collective-permute-start(f32[8,128]{1,0:T(8,128)S(1)} %maximum_maximum_fusion.a), channel_id=1, source_target_pairs={{1,0},{0,1},{3,2},{2,3},{5,4},{4,5},{7,6},{6,7},{9,8},{8,9},{11,10... | collective-permute-start | bytes 12296 | tf_op jit(solution)/shard_map/ppermute | solution.py:330

commit v10 on v9

--- a/solution.py
+++ b/solution.py
@@ -12,7 +12,7 @@
 AXES = ("yh", "yl", "xh", "core", "z", "xl")
 SIZES = (4, 2, 2, 2, 8, 2)
 GROUP = ("xh", "xl", "core", "yl")
-SPREAD = ("yh", "z")
+SPREAD = ("z", "yh")
 PLANE = ("xh", "yh", "yl")
 SHIFT = (0, 4, 1, 7, 2, 6, 3, 5)
 BF16 = jnp.bfloat16
@@ -161,7 +161,7 @@
             z = 2 * m + jnp.where(core == 0, s, 1 - s)
             for yh in range(4):
                 row = m * 128 + s * 64 + yh * 16
-                chunks[yh * 8 + z] = summed[row : row + 16, :]
+                chunks[z * 4 + yh] = summed[row : row + 16, :]
     store = pltpu.make_async_copy(chunks, share, sem)
     store.start()
     store.wait()

time: 142 us -> 142 us (level)
  transfers between devices with their start and end apart: 12 -> 12, of which waited for: 8 -> 9; matrix products, arithmetic and copies ran while one was open for 0% -> 0% of each run, Pallas kernels for 5% -> 5%
where the time goes in v10:
time: 142 us; the launch traced here: 141 us
  starting transfers between devices  59 us (42%)
  waiting for transfers between devices  46.6 us (33%)
  blocking collectives  21.1 us (15%)
  Pallas kernels  13.2 us (9%)
    ppermute x8, starting transfers between devices, from_ahead(): return lax.ppermute(x, axis, [((i + step) % size, i) for i in range(size)])  23.7 us
    all_to_all x1, blocking collectives, local(): plane = lax.all_to_all(spread(piece, peaks), PLANE, 0, 0, tiled=True)  21.1 us
    all_to_all x1, waiting for transfers between devices, local(): got = lax.all_to_all(packed, GROUP, 0, 0, tiled=True)  19.6 us
    all_to_all x1, waiting for transfers between devices, local(): terms = lax.all_to_all(share, SPREAD, 0, 0, tiled=True)  11.5 us
    all_to_all x1, starting transfers between devices, local(): terms = lax.all_to_all(share, SPREAD, 0, 0, tiled=True)  11.2 us
    all_to_all x1, starting transfers between devices, local(): got = lax.all_to_all(packed, GROUP, 0, 0, tiled=True)  10.4 us
    ppermute x1, waiting for transfers between devices, shift_weight(): return lax.ppermute(weight, ('yl', 'xh', 'core', 'z'), pairs)  7.17 us
    ppermute x1, starting transfers between devices, shift_weight(): return lax.ppermute(weight, ('yl', 'xh', 'core', 'z'), pairs)  7.04 us
  transfers between devices with their start and end apart: 12, of which 9 were waited for; matrix products, arithmetic and copies ran while one was open for 0% of the time, Pallas kernels for 5%

profile of v10, /device:TPU:1, one launch (start us, length us, event | category | flops | bytes accessed | tf_op | source)
XLA Modules:
  0.0 140.8 jit_solution(12141672984318170795)
XLA Ops:
  0.6 3.2 %pack.1 = (bf16[16,192,512]{2,1,0:T(8,128)(2,1)}, bf16[512,512]{1,0:T(8,128)(2,1)}) custom-call(bf16[128,8192]{1,0:T(8,128)(2,1)} %tokens.1, bf16[128,512]{1,0:T(8,128)(2,1)} %keys.1, bf16[512,512]{1,0:T(8,128)(2,1)} %codes.1, f32[4]{0:T(128)} %scales.1), custom_call_target="tpu_custom_call" | custom-call | bytes 9437184 | tf_op jit(solution)/shard_map/pack/pallas_call | solution.py:95
  3.9 10.4 %all-to-all-start = ((bf16[16,192,512]{2,1,0:T(8,128)(2,1)}), bf16[16,192,512]{2,1,0:T(8,128)(2,1)S(1)}, u32[]{:S(2)}, u32[]{:S(2)}) async-start(bf16[16,192,512]{2,1,0:T(8,128)(2,1)} %get-tuple-element.20), calls=%async_computation | async-start | bytes 6291456 | tf_op jit(solution)/shard_map/all_to_all | solution.py:353
  14.3 7.0 %collective-permute-start = (bf16[512,512]{1,0:T(8,128)(2,1)}, bf16[512,512]{1,0:T(8,128)(2,1)S(1)}, u32[]{:S(2)}, u32[]{:S(2)}) collective-permute-start(bf16[512,512]{1,0:T(8,128)(2,1)} %get-tuple-element.21), channel_id=1, source_target_pairs={{0,0},{2,2},{4,4},{6,6},{8,8},{10,10},{12,12},{14,14},{24,16},{26,... | collective-permute-start | bytes 1572872 | tf_op jit(solution)/shard_map/ppermute | solution.py:345
  21.4 7.2 %collective-permute-done.weight = bf16[512,512]{1,0:T(8,128)(2,1)S(1)} collective-permute-done((bf16[512,512]{1,0:T(8,128)(2,1)}, bf16[512,512]{1,0:T(8,128)(2,1)S(1)}, u32[]{:S(2)}, u32[]{:S(2)}) %collective-permute-start) | collective-permute-done | bytes 524320 | tf_op jit(solution)/shard_map/ppermute | solution.py:345
  28.5 1.9 %collective-permute-start.1 = (bf16[512,512]{1,0:T(8,128)(2,1)S(1)}, bf16[512,512]{1,0:T(8,128)(2,1)}, u32[]{:S(2)}, u32[]{:S(2)}) collective-permute-start(bf16[512,512]{1,0:T(8,128)(2,1)S(1)} %collective-permute-done.weight), channel_id=1, source_target_pairs={{16,0},{0,16},{17,1},{1,17},{18,2},{2,18},{19,3},{3,19},{20,4},{4,... | collective-permute-start | bytes 1572872 | tf_op jit(solution)/shard_map/ppermute | solution.py:330
  30.5 2.0 %collective-permute-done.1.across = bf16[512,512]{1,0:T(8,128)(2,1)} collective-permute-done((bf16[512,512]{1,0:T(8,128)(2,1)S(1)}, bf16[512,512]{1,0:T(8,128)(2,1)}, u32[]{:S(2)}, u32[]{:S(2)}) %collective-permute-start.1) | collective-permute-done | bytes 524320 | tf_op jit(solution)/shard_map/ppermute | solution.py:330
  32.5 19.6 %all-to-all-done.got = bf16[16,192,512]{2,1,0:T(8,128)(2,1)S(1)} async-done(((bf16[16,192,512]{2,1,0:T(8,128)(2,1)}), bf16[16,192,512]{2,1,0:T(8,128)(2,1)S(1)}, u32[]{:S(2)}, u32[]{:S(2)}) %all-to-all-start) | async-done | bytes 3145760 | tf_op jit(solution)/shard_map/all_to_all | solution.py:353
  52.8 2.1 %collective-permute-start.2 = (bf16[512,512]{1,0:T(8,128)(2,1)S(1)}, bf16[512,512]{1,0:T(8,128)(2,1)S(1)}, u32[]{:S(2)}, u32[]{:S(2)}) collective-permute-start(bf16[512,512]{1,0:T(8,128)(2,1)S(1)} %away.1), channel_id=1, source_target_pairs={{16,0},{0,16},{17,1},{1,17},{18,2},{2,18},{19,3},{3,19},{20,4},{4,... | collective-permute-start | bytes 1572872 | tf_op jit(solution)/shard_map/ppermute | solution.py:330
  57.5 11.2 %all-to-all-start.1 = ((bf16[32,16,512]{2,1,0:T(8,128)(2,1)}), bf16[32,16,512]{2,1,0:T(8,128)(2,1)S(1)}, u32[]{:S(2)}, u32[]{:S(2)}) async-start(bf16[32,16,512]{2,1,0:T(8,128)(2,1)} %join.1), calls=%async_computation.1 | async-start | bytes 1048576 | tf_op jit(solution)/shard_map/all_to_all | solution.py:360
  68.7 3.9 %product.1 = (bf16[16,128,512]{2,1,0:T(8,128)(2,1)}, f32[8,512]{1,0:T(8,128)S(1)}) custom-call(bf16[16,64,512]{2,1,0:T(8,128)(2,1)} %get-tuple-element.23.mine, bf16[512,512]{1,0:T(8,128)(2,1)} %copy-done, bf16[512,512]{1,0:T(8,128)(2,1)} %collective-permute-done.1.across), custom_call_target="tpu_custom_call" | custom-call | flops 1073741824 | bytes 5242880 | tf_op jit(solution)/shard_map/product/pallas_call | solution.py:208
  72.6 11.5 %all-to-all-done.1.refs_0_ = bf16[32,16,512]{2,1,0:T(8,128)(2,1)S(1)} async-done(((bf16[32,16,512]{2,1,0:T(8,128)(2,1)}), bf16[32,16,512]{2,1,0:T(8,128)(2,1)S(1)}, u32[]{:S(2)}, u32[]{:S(2)}) %all-to-all-start.1) | async-done | bytes 524320 | tf_op jit(solution)/shard_map/all_to_all | solution.py:360
  84.3 21.1 %all_to_all.20.mine = bf16[16,16,640]{2,1,0:T(8,128)(2,1)S(1)} all-to-all(bf16[16,16,640]{2,1,0:T(8,128)(2,1)S(1)} %spread.1), channel_id=1, replica_groups=mesh['yh'=4,'yl'=2,'xh'=2,'core'=2,'z'=8,'xl'=2] {'xh','yh','yl'}, dimensions={0} | all-to-all | bytes 655360 | tf_op jit(solution)/shard_map/all_to_all | solution.py:363
  105.4 6.7 %all-to-all-start.3 = ((bf16[16,128,512]{2,1,0:T(8,128)(2,1)}), bf16[16,128,512]{2,1,0:T(8,128)(2,1)S(1)}, u32[]{:S(2)}, u32[]{:S(2)}) async-start(bf16[16,128,512]{2,1,0:T(8,128)(2,1)} %get-tuple-element.31), calls=%async_computation.3 | async-start | bytes 4194304 | tf_op jit(solution)/shard_map/all_to_all | solution.py:366
  112.0 2.0 %collective-permute-start.3 = (bf16[16,16,640]{2,1,0:T(8,128)(2,1)S(1)}, bf16[16,16,640]{2,1,0:T(8,128)(2,1)S(1)}, u32[]{:S(2)}, u32[]{:S(2)}) collective-permute-start(bf16[16,16,640]{2,1,0:T(8,128)(2,1)S(1)} %all_to_all.20.mine), channel_id=1, source_target_pairs={{16,0},{0,16},{17,1},{1,17},{18,2},{2,18},{19,3},{3,19},{20,4},{4,... | collective-permute-start | bytes 983048 | tf_op jit(solution)/shard_map/ppermute | solution.py:330
  114.0 1.5 %collective-permute-done.3.other = bf16[16,16,640]{2,1,0:T(8,128)(2,1)S(1)} collective-permute-done((bf16[16,16,640]{2,1,0:T(8,128)(2,1)S(1)}, bf16[16,16,640]{2,1,0:T(8,128)(2,1)S(1)}, u32[]{:S(2)}, u32[]{:S(2)}) %collective-permute-start.3) | collective-permute-done | bytes 327712 | tf_op jit(solution)/shard_map/ppermute | solution.py:330
  115.6 3.2 %collective-permute-start.5 = (f32[8,128]{1,0:T(8,128)S(1)}, f32[8,128]{1,0:T(8,128)S(1)}, u32[]{:S(2)}, u32[]{:S(2)}) collective-permute-start(f32[8,128]{1,0:T(8,128)S(1)} %peaks_of.1), channel_id=1, source_target_pairs={{14,0},{0,2},{2,4},{4,6},{6,8},{8,10},{10,12},{12,14},{15,1},{1,3}... | collective-permute-start | bytes 12296 | tf_op jit(solution)/shard_map/ppermute | solution.py:330
  118.7 3.3 %collective-permute-start.4 = (f32[8,128]{1,0:T(8,128)S(1)}, f32[8,128]{1,0:T(8,128)S(1)}, u32[]{:S(2)}, u32[]{:S(2)}) collective-permute-start(f32[8,128]{1,0:T(8,128)S(1)} %peaks_of.1), channel_id=1, source_target_pairs={{2,0},{4,2},{6,4},{8,6},{10,8},{12,10},{14,12},{0,14},{3,1},{5,3},... | collective-permute-start | bytes 12296 | tf_op jit(solution)/shard_map/ppermute | solution.py:330
  122.1 1.1 merge.1
  123.4 4.2 %collective-permute-start.7 = (f32[8,128]{1,0:T(8,128)S(1)}, f32[8,128]{1,0:T(8,128)S(1)}, u32[]{:S(2)}, u32[]{:S(2)}) collective-permute-start(f32[8,128]{1,0:T(8,128)S(1)} %maximum_maximum_fusion.1), channel_id=1, source_target_pairs={{10,0},{12,2},{14,4},{0,6},{2,8},{4,10},{6,12},{8,14},{11,1},{13,3... | collective-permute-start | bytes 12296 | tf_op jit(solution)/shard_map/ppermute | solution.py:330
  127.6 4.1 %collective-permute-start.6 = (f32[8,128]{1,0:T(8,128)S(1)}, f32[8,128]{1,0:T(8,128)S(1)}, u32[]{:S(2)}, u32[]{:S(2)}) collective-permute-start(f32[8,128]{1,0:T(8,128)S(1)} %maximum_maximum_fusion.1), channel_id=1, source_target_pairs={{6,0},{8,2},{10,4},{12,6},{14,8},{0,10},{2,12},{4,14},{7,1},{9,3},... | collective-permute-start | bytes 12296 | tf_op jit(solution)/shard_map/ppermute | solution.py:330
  131.7 2.3 %collective-permute-done.6 = f32[8,128]{1,0:T(8,128)S(1)} collective-permute-done((f32[8,128]{1,0:T(8,128)S(1)}, f32[8,128]{1,0:T(8,128)S(1)}, u32[]{:S(2)}, u32[]{:S(2)}) %collective-permute-start.6) | collective-permute-done | bytes 4128 | tf_op jit(solution)/shard_map/ppermute | solution.py:330
  134.0 3.0 %collective-permute-start.8 = (f32[8,128]{1,0:T(8,128)S(1)}, f32[8,128]{1,0:T(8,128)S(1)}, u32[]{:S(2)}, u32[]{:S(2)}) collective-permute-start(f32[8,128]{1,0:T(8,128)S(1)} %maximum_maximum_fusion.a), channel_id=1, source_target_pairs={{1,0},{0,1},{3,2},{2,3},{5,4},{4,5},{7,6},{6,7},{9,8},{8,9},{11,10... | collective-permute-start | bytes 12296 | tf_op jit(solution)/shard_map/ppermute | solution.py:330
  137.0 1.5 %all-to-all-done.3.back = bf16[16,128,512]{2,1,0:T(8,128)(2,1)S(1)} async-done(((bf16[16,128,512]{2,1,0:T(8,128)(2,1)}), bf16[16,128,512]{2,1,0:T(8,128)(2,1)S(1)}, u32[]{:S(2)}, u32[]{:S(2)}) %all-to-all-start.3) | async-done | bytes 2097184 | tf_op jit(solution)/shard_map/all_to_all | solution.py:366
  138.5 1.6 %unpack.1 = bf16[128,8192]{1,0:T(8,128)(2,1)} custom-call(bf16[16,128,512]{2,1,0:T(8,128)(2,1)S(1)} %all-to-all-done.3.back), custom_call_target="tpu_custom_call" | custom-call | bytes 4194304 | tf_op jit(solution)/shard_map/unpack/pallas_call | solution.py:282
  (16 shorter events, 4.5 us)
Async XLA Ops:
  3.9 48.2 %all-to-all-start = ((bf16[16,192,512]{2,1,0:T(8,128)(2,1)}), bf16[16,192,512]{2,1,0:T(8,128)(2,1)S(1)}, u32[]{:S(2)}, u32[]{:S(2)}) async-start(bf16[16,192,512]{2,1,0:T(8,128)(2,1)} %get-tuple-element.20), calls=%async_computation | async-start | bytes 6291456 | tf_op jit(solution)/shard_map/all_to_all | solution.py:353
  14.3 14.2 %collective-permute-start = (bf16[512,512]{1,0:T(8,128)(2,1)}, bf16[512,512]{1,0:T(8,128)(2,1)S(1)}, u32[]{:S(2)}, u32[]{:S(2)}) collective-permute-start(bf16[512,512]{1,0:T(8,128)(2,1)} %get-tuple-element.21), channel_id=1, source_target_pairs={{0,0},{2,2},{4,4},{6,6},{8,8},{10,10},{12,12},{14,14},{24,16},{26,... | collective-permute-start | bytes 1572872 | tf_op jit(solution)/shard_map/ppermute | solution.py:345
  28.5 1.9 %copy-start = (bf16[512,512]{1,0:T(8,128)(2,1)}, bf16[512,512]{1,0:T(8,128)(2,1)S(1)}, u32[]{:S(2)}) copy-start(bf16[512,512]{1,0:T(8,128)(2,1)S(1)} %collective-permute-done.weight) | copy-start | bytes 1572868
  28.5 3.9 %collective-permute-start.1 = (bf16[512,512]{1,0:T(8,128)(2,1)S(1)}, bf16[512,512]{1,0:T(8,128)(2,1)}, u32[]{:S(2)}, u32[]{:S(2)}) collective-permute-start(bf16[512,512]{1,0:T(8,128)(2,1)S(1)} %collective-permute-done.weight), channel_id=1, source_target_pairs={{16,0},{0,16},{17,1},{1,17},{18,2},{2,18},{19,3},{3,19},{20,4},{4,... | collective-permute-start | bytes 1572872 | tf_op jit(solution)/shard_map/ppermute | solution.py:330
  52.8 3.8 %collective-permute-start.2 = (bf16[512,512]{1,0:T(8,128)(2,1)S(1)}, bf16[512,512]{1,0:T(8,128)(2,1)S(1)}, u32[]{:S(2)}, u32[]{:S(2)}) collective-permute-start(bf16[512,512]{1,0:T(8,128)(2,1)S(1)} %away.1), channel_id=1, source_target_pairs={{16,0},{0,16},{17,1},{1,17},{18,2},{2,18},{19,3},{3,19},{20,4},{4,... | collective-permute-start | bytes 1572872 | tf_op jit(solution)/shard_map/ppermute | solution.py:330
  57.5 26.5 %all-to-all-start.1 = ((bf16[32,16,512]{2,1,0:T(8,128)(2,1)}), bf16[32,16,512]{2,1,0:T(8,128)(2,1)S(1)}, u32[]{:S(2)}, u32[]{:S(2)}) async-start(bf16[32,16,512]{2,1,0:T(8,128)(2,1)} %join.1), calls=%async_computation.1 | async-start | bytes 1048576 | tf_op jit(solution)/shard_map/all_to_all | solution.py:360
  105.4 33.2 %all-to-all-start.3 = ((bf16[16,128,512]{2,1,0:T(8,128)(2,1)}), bf16[16,128,512]{2,1,0:T(8,128)(2,1)S(1)}, u32[]{:S(2)}, u32[]{:S(2)}) async-start(bf16[16,128,512]{2,1,0:T(8,128)(2,1)} %get-tuple-element.31), calls=%async_computation.3 | async-start | bytes 4194304 | tf_op jit(solution)/shard_map/all_to_all | solution.py:366
  112.0 3.5 %collective-permute-start.3 = (bf16[16,16,640]{2,1,0:T(8,128)(2,1)S(1)}, bf16[16,16,640]{2,1,0:T(8,128)(2,1)S(1)}, u32[]{:S(2)}, u32[]{:S(2)}) collective-permute-start(bf16[16,16,640]{2,1,0:T(8,128)(2,1)S(1)} %all_to_all.20.mine), channel_id=1, source_target_pairs={{16,0},{0,16},{17,1},{1,17},{18,2},{2,18},{19,3},{3,19},{20,4},{4,... | collective-permute-start | bytes 983048 | tf_op jit(solution)/shard_map/ppermute | solution.py:330
  115.6 7.6 %collective-permute-start.5 = (f32[8,128]{1,0:T(8,128)S(1)}, f32[8,128]{1,0:T(8,128)S(1)}, u32[]{:S(2)}, u32[]{:S(2)}) collective-permute-start(f32[8,128]{1,0:T(8,128)S(1)} %peaks_of.1), channel_id=1, source_target_pairs={{14,0},{0,2},{2,4},{4,6},{6,8},{8,10},{10,12},{12,14},{15,1},{1,3}... | collective-permute-start | bytes 12296 | tf_op jit(solution)/shard_map/ppermute | solution.py:330
  118.7 4.6 %collective-permute-start.4 = (f32[8,128]{1,0:T(8,128)S(1)}, f32[8,128]{1,0:T(8,128)S(1)}, u32[]{:S(2)}, u32[]{:S(2)}) collective-permute-start(f32[8,128]{1,0:T(8,128)S(1)} %peaks_of.1), channel_id=1, source_target_pairs={{2,0},{4,2},{6,4},{8,6},{10,8},{12,10},{14,12},{0,14},{3,1},{5,3},... | collective-permute-start | bytes 12296 | tf_op jit(solution)/shard_map/ppermute | solution.py:330
  123.4 8.3 %collective-permute-start.7 = (f32[8,128]{1,0:T(8,128)S(1)}, f32[8,128]{1,0:T(8,128)S(1)}, u32[]{:S(2)}, u32[]{:S(2)}) collective-permute-start(f32[8,128]{1,0:T(8,128)S(1)} %maximum_maximum_fusion.1), channel_id=1, source_target_pairs={{10,0},{12,2},{14,4},{0,6},{2,8},{4,10},{6,12},{8,14},{11,1},{13,3... | collective-permute-start | bytes 12296 | tf_op jit(solution)/shard_map/ppermute | solution.py:330
  127.6 6.4 %collective-permute-start.6 = (f32[8,128]{1,0:T(8,128)S(1)}, f32[8,128]{1,0:T(8,128)S(1)}, u32[]{:S(2)}, u32[]{:S(2)}) collective-permute-start(f32[8,128]{1,0:T(8,128)S(1)} %maximum_maximum_fusion.1), channel_id=1, source_target_pairs={{6,0},{8,2},{10,4},{12,6},{14,8},{0,10},{2,12},{4,14},{7,1},{9,3},... | collective-permute-start | bytes 12296 | tf_op jit(solution)/shard_map/ppermute | solution.py:330
  134.0 6.1 %collective-permute-start.8 = (f32[8,128]{1,0:T(8,128)S(1)}, f32[8,128]{1,0:T(8,128)S(1)}, u32[]{:S(2)}, u32[]{:S(2)}) collective-permute-start(f32[8,128]{1,0:T(8,128)S(1)} %maximum_maximum_fusion.a), channel_id=1, source_target_pairs={{1,0},{0,1},{3,2},{2,3},{5,4},{4,5},{7,6},{6,7},{9,8},{8,9},{11,10... | collective-permute-start | bytes 12296 | tf_op jit(solution)/shard_map/ppermute | solution.py:330
